TPU v7x, 32 devices: a whole 2x2x4 slice. The times are simulated.
32 devices in a mesh: prow: 4 (over y, x), pcol: 8 (over z, core).
Axes of the slice: x: 2, y: 2, z: 4, core: 2. Of those that a mesh axis runs over, the one named last changes fastest.
Arguments:
- inverse_matrix: float32 [12288, 12288], P('prow', 'pcol'), may hold values from -6 to 6
- factor_blocks: float32 [4, 48, 256, 256], P(None, 'prow', 'pcol'), may hold values from -0.0546875 to 0.0546875
- factor_inverse: float32 [4, 256, 256], replicated, may hold values from -8 to 8, as said below
- diag_given: float32 [4, 256, 256], replicated, may hold values from -6 to 6
- block_lists: int32 [4, 48], replicated, may hold values from 0 to 47, as said below
- list_mask: int32 [4, 48], replicated, may hold values from 0 to 1, as said below
- slot_of_block: int32 [48], replicated, may hold values from 0 to 47, as said below
Outputs:
- panel_inverse: float32 [4, 48, 256, 256], P(None, 'prow', 'pcol')
- diag_inverse: float32 [4, 256, 256], replicated
Inputs may be any that keep to these rules, and one draw needn't show every extreme that they name: `block_lists`: each panel's list names every block of the window once; entries with mask 0 are padding. `list_mask`: 1 marks a used list entry; for every k, of the 48 pairs (p, s) with s // 12 = k, exactly 36 have slot_valid[p, s] = 1. `slot_of_block`: a permutation of the 48 slots. `factor_inverse`: lower triangular with a positive diagonal.
All inputs are finite; a program needn't handle non-finite values.
Results may differ from a plain program's by a relative error of at most 0.00007.
Values sent between devices are 32-bit elements; how exact they have to be, the bound alone decides.
No kernel may reach another device: no remote copies, remote signals or barrier semaphores. Data moves between devices by JAX's collectives and lax.ppermute only.
A program may use at most 128 MiB of HBM per device.

v0:
```python
import jax
import jax.numpy as jnp
from jax import lax
from jax.sharding import PartitionSpec as P


def spread(value, axis, source):
    kept = jnp.where(lax.axis_index(axis) == source, value, 0).astype(value.dtype)
    return lax.psum(kept, axis)


def valid_slots(block_lists, list_mask, slot_of_block):
    window_blocks = block_lists.shape[1]
    block_ids = jnp.arange(window_blocks, dtype=jnp.int32)
    chosen = (block_lists[:, :, None] == block_ids[None, None, :]).astype(jnp.int32)
    slot_ids = jnp.sum(chosen * slot_of_block[None, None, :], axis=2)
    matches = (slot_ids[:, :, None] == block_ids[None, None, :]).astype(jnp.int32) * list_mask[
        :, :, None
    ]
    return jnp.sum(matches, axis=1)


def on_device(
    inverse_matrix, factor_blocks, factor_inverse, diag_given, block_lists, list_mask, slot_of_block
):
    highest = lax.Precision.HIGHEST
    panels = factor_blocks.shape[0]
    rows_here = factor_blocks.shape[1]
    panel_width = factor_inverse.shape[1]
    cols_here = inverse_matrix.shape[1] // panel_width
    row_index = lax.axis_index("prow")
    col_index = lax.axis_index("pcol")
    slot_valid = valid_slots(block_lists, list_mask, slot_of_block).astype(jnp.float32)
    row_valid = lax.dynamic_slice_in_dim(slot_valid, row_index * rows_here, rows_here, 1)
    normalized = jnp.einsum("psij,pjk->psik", factor_blocks, factor_inverse, precision=highest)
    normalized = normalized * row_valid[:, :, None, None]
    full_rows = lax.all_gather(normalized, "pcol", axis=2, tiled=True)
    owner_row = col_index * lax.axis_size("prow") // lax.axis_size("pcol")
    offset = col_index * cols_here - owner_row * rows_here
    picked = lax.dynamic_slice_in_dim(full_rows, offset, cols_here, 1)
    column_hat = spread(picked, "prow", owner_row)
    stacked = column_hat.reshape(panels, cols_here * panel_width, panel_width)
    partial_value = jnp.einsum(
        "ij,pjk->pik",
        inverse_matrix,
        stacked,
        precision=highest,
        preferred_element_type=jnp.float32,
    )
    partial_value = partial_value.reshape(panels, rows_here, panel_width, panel_width)
    keep_count = 3 * panels * rows_here // 4
    flat_valid = row_valid.reshape(panels * rows_here)
    used_flags = (flat_valid > 0.5).astype(jnp.int32)
    positions = jnp.cumsum(used_flags) - 1
    picked_rows = jnp.nonzero(used_flags, size=keep_count, fill_value=0)[0].astype(jnp.int32)
    flat_partial = partial_value.reshape(panels * rows_here, panel_width, panel_width)
    packed = jnp.take(flat_partial, picked_rows, axis=0)
    packed_sum = lax.psum_scatter(packed, "pcol", scatter_dimension=1, tiled=True)
    back_rows = jnp.clip(positions, 0, keep_count - 1)
    unpacked = jnp.take(packed_sum, back_rows, axis=0)
    unpacked = unpacked.reshape(panels, rows_here, unpacked.shape[1], panel_width)
    panel_inverse = -(unpacked * row_valid[:, :, None, None])
    local_diag = jnp.einsum("psik,psil->pkl", normalized, panel_inverse, precision=highest)
    diag_inverse = diag_given - lax.psum(local_diag, ("prow", "pcol"))
    return (panel_inverse, diag_inverse)


def solution(mesh):
    placed = (P("prow", "pcol"), P(None, "prow", "pcol", None), P(), P(), P(), P(), P())
    return jax.shard_map(
        on_device,
        mesh=mesh,
        in_specs=placed,
        out_specs=(P(None, "prow", "pcol", None), P()),
        check_vma=False,
    )
```

profile of v0, /device:TPU:0, one launch (start us, length us, event | category | flops | bytes accessed | tf_op | source)
XLA Modules:
  0.0 628.9 jit_solution(17875137295596397534)
XLA Ops:
  7.2 0.0 copy-start
  7.2 0.0 all-gather.2.cloned.1.call-start
  7.2 1.0 select_reduce_fusion.1
  8.3 0.8 select_reduce_fusion
  9.1 0.7 convert_reduce_fusion
  9.8 0.0 copy-done
  9.8 3.9 convolution_multiply_fusion
  13.7 0.0 all-gather.2.cloned.1.call-update
  13.8 0.0 all-reduce.3.cloned.1.call-start
  13.8 119.5 %all-gather.2.cloned.1.call-done = f32[4,12,256,256]{3,2,1,0:T(8,128)} async-done(((f32[4,12,32,256]{3,2,1,0:T(8,128)}), f32[4,12,256,256]{3,2,1,0:T(8,128)}) %all-gather.2.cloned.1.call-update) | async-done | bytes 12582928 | tf_op jit(solution)/shard_map/all_gather | solution.py:37
  133.3 6.0 dynamic-slice_select_fusion
  139.4 6.6 %copy.21 = f32[4,1536,256]{1,2,0:T(8,128)} copy(f32[4,1536,256]{2,1,0:T(8,128)} %bitcast.24) | data formatting | bytes 12582912 | tf_op jit(solution)/shard_map/reshape | solution.py:42
  146.0 0.0 all-reduce.3.cloned.1.call-update
  146.0 0.0 reduce-scatter.2.cloned.1.call-start
  146.1 0.1 reshape.177
  146.2 0.1 reduce-window.12
  146.2 0.1 fusion.6
  146.4 0.9 scatter_custom_fusion
  147.2 0.1 copy.20
  147.3 0.1 select_n.115
  147.4 0.8 remainder_reduce_fusion
  148.2 0.7 compare_and_fusion
  148.8 134.0 %all-reduce.3.cloned.1.call-done = f32[4,1536,256]{1,2,0:T(8,128)} async-done(((f32[4,1536,256]{1,2,0:T(8,128)}), f32[4,1536,256]{1,2,0:T(8,128)}) %all-reduce.3.cloned.1.call-update) | async-done | bytes 6291472 | tf_op jit(solution)/shard_map/psum | solution.py:9
  282.8 69.0 %fusion.2 = f32[4,3072,256]{1,2,0:T(8,128)} fusion(f32[4,1536,256]{1,2,0:T(8,128)} %all-reduce.3.cloned.1.call-done, f32[3072,1536]{1,0:T(8,128)} %param.7), kind=kOutput, calls=%fused_computation.5 | convolution fusion | flops 57982058496 | bytes 37748736 | tf_op jit(solution)/shard_map/ij,pjk->pik/dot_general | solution.py:43
  351.8 12.6 %copy.22 = f32[4,3072,256]{2,1,0:T(8,128)} copy(f32[4,3072,256]{1,2,0:T(8,128)} %fusion.2) | data formatting | bytes 25165824 | tf_op jit(solution)/shard_map/ij,pjk->pik/transpose | solution.py:43
  364.4 11.3 %gather_fusion = f32[36,256,256]{2,1,0:T(8,128)} fusion(f32[48,256,256]{2,1,0:T(8,128)} %bitcast.23, s32[1024]{0:T(1024)S(1)} %pad_clamp_fusion.1), kind=kCustom, calls=%fused_computation | custom fusion | bytes 18874512 | tf_op jit(solution)/shard_map/jit(_take)/gather | solution.py:57
  375.7 8.8 %broadcast_select_fusion = f32[36,256,256]{2,1,0:T(8,128)} fusion(f32[36,256,256]{2,1,0:T(8,128)} %gather_fusion, pred[36]{0:T(512)(128)(4,1)S(1)} %compare_and_fusion), kind=kLoop, calls=%fused_computation.7 | loop fusion | flops 2359296 | bytes 18874404 | tf_op jit(solution)/shard_map/jit(_take)/select_n | solution.py:57
  384.5 0.0 reduce-scatter.2.cloned.1.call-update
  384.5 0.2 all-reduce.5.cloned.1.call-start
  384.7 0.1 reduce-window.9
  384.8 0.1 fusion.8
  384.9 0.1 min.14
  385.0 99.1 %reduce-scatter.2.cloned.1.call-done = f32[36,32,256]{2,1,0:T(8,128)} async-done(((f32[36,256,256]{2,1,0:T(8,128)}), f32[36,32,256]{2,1,0:T(8,128)}) %reduce-scatter.2.cloned.1.call-update) | async-done | bytes 1179664 | tf_op jit(solution)/shard_map/reduce_scatter | solution.py:58
  484.2 1.9 gather_fusion.1
  486.1 0.0 copy-start.2
  486.1 0.2 multiply_negate_fusion
  486.4 1.1 copy-done.2
  487.5 0.0 copy-start.3
  487.5 0.0 copy-start.1
  487.5 3.8 convolution_bitcast_fusion
  491.3 0.0 copy-done.3
  491.3 0.0 all-reduce.5.cloned.1.call-update
  491.3 128.4 %all-reduce.5.cloned.1.call-done = f32[4,256,256]{2,1,0:T(8,128)} async-done(((f32[4,256,256]{2,1,0:T(8,128)}), f32[4,256,256]{2,1,0:T(8,128)}) %all-reduce.5.cloned.1.call-update) | async-done | bytes 1048592 | tf_op jit(solution)/shard_map/psum | solution.py:64
  619.7 2.6 sub.20
  622.4 0.0 copy-done.1
  (7 shorter events, 0.0 us)
Async XLA Ops:
  7.2 2.6 copy-start
  7.2 126.2 %all-gather.2.cloned.1.call-start = ((), (), s32[]{:S(2)}) async-start(), calls=%async_computation.1 | async-start | bytes 14155776 | tf_op jit(solution)/shard_map/all_gather | solution.py:37
  13.8 269.1 %all-reduce.3.cloned.1.call-start = ((), (), s32[]{:S(2)}) async-start(), calls=%async_computation.2 | async-start | bytes 12582912 | tf_op jit(solution)/shard_map/psum | solution.py:9
  146.0 338.2 %reduce-scatter.2.cloned.1.call-start = ((), (), s32[]{:S(2)}) async-start(), calls=%async_computation.3 | async-start | bytes 10616832 | tf_op jit(solution)/shard_map/reduce_scatter | solution.py:58
  384.5 235.2 %all-reduce.5.cloned.1.call-start = ((), (), s32[]{:S(2)}) async-start(), calls=%async_computation.4 | async-start | bytes 2097152 | tf_op jit(solution)/shard_map/psum | solution.py:64
  486.1 1.4 copy-start.2
  487.5 3.8 copy-start.3
  487.5 134.8 %copy-start.1 = (f32[4,12,32,256]{3,2,1,0:T(8,128)S(1)}, f32[4,12,32,256]{3,2,1,0:T(8,128)}, u32[]{:S(2)}) copy-start(f32[4,12,32,256]{3,2,1,0:T(8,128)} %param.8) | copy-start | bytes 4718596
Sparse Core Ops, SparseCore 0:
  13.9 119.4 all-gather.1
  146.1 136.6 all-reduce.2
  384.6 99.5 reduce-scatter.1
  491.5 128.2 all-reduce.4
where the time goes:
time: 629 us
  waiting for transfers between devices  481 us (76%)
  matrix products  76.7 us (12%)
  local copies, waits for them, and re-layouts  33.9 us (5%)
  other arithmetic  23 us (4%)
  between operations  13.9 us (2%)
    psum x1, waiting for transfers between devices, spread(): return lax.psum(kept, axis)  134 us
    psum x1, waiting for transfers between devices, on_device(): diag_inverse = diag_given - lax.psum(local_diag, ('prow', 'pcol'))  128 us
    all_gather x1, waiting for transfers between devices, on_device(): full_rows = lax.all_gather(normalized, 'pcol', axis=2, tiled=True)  120 us
    reduce_scatter x1, waiting for transfers between devices, on_device(): lax.psum_scatter(packed, 'pcol', scatter_dimension=1, tiled=True)  99.1 us
    dot_general x1, matrix products, on_device(): jnp.einsum('ij,pjk->pik', inverse_matrix, stacked, precision=highest, pre...  69 us
    transpose x1, local copies, waits for them, and re-layouts, on_device(): jnp.einsum('ij,pjk->pik', inverse_matrix, stacked, precision=highest, pre...  12.6 us
  transfers between devices with their start and end apart: 4, of which 4 were waited for; matrix products, arithmetic and copies ran while one was open for 0% of the time, Pallas kernels for 0%

commit v1 on v0

v1 whole, which is shorter than its diff:
```python
import functools
import math
import jax
import jax.numpy as jnp
from jax import lax
from jax.experimental import pallas as pl
from jax.experimental.pallas import tpu as pltpu
from jax.sharding import PartitionSpec as P

AXES = ("prow", "pcol")
HIGHEST = lax.Precision.HIGHEST
VMEM_LIMIT = 56 * 1024 * 1024


def whole(memory_space=pltpu.VMEM):
    return pl.BlockSpec(memory_space=memory_space)


def call(kernel, outs, scratch=(), n_scalar=1, n_in=1, flops=0, moved=0):
    return pl.pallas_call(
        kernel,
        out_shape=outs,
        in_specs=[whole(pltpu.SMEM)] * n_scalar + [whole()] * n_in,
        out_specs=jax.tree.map(lambda _: whole(), outs),
        scratch_shapes=list(scratch),
        compiler_params=pltpu.CompilerParams(vmem_limit_bytes=VMEM_LIMIT),
        cost_estimate=pl.CostEstimate(flops=flops, bytes_accessed=moved, transcendentals=0),
    )


def valid_slots(block_lists, list_mask, slot_of_block):
    window_blocks = block_lists.shape[1]
    block_ids = jnp.arange(window_blocks, dtype=jnp.int32)
    chosen = (block_lists[:, :, None] == block_ids[None, None, :]).astype(jnp.int32)
    slot_ids = jnp.sum(chosen * slot_of_block[None, None, :], axis=2)
    matches = (slot_ids[:, :, None] == block_ids[None, None, :]).astype(jnp.int32)
    return jnp.sum(matches * list_mask[:, :, None], axis=1)


def normalize_kernel(groups, lines, place, valid, f_ref, inv_ref, n_ref, *rest):
    panels, slots, rb, width = f_ref.shape
    halves = slots // 2
    scratch = rest[-len(groups):]
    outs = rest[: -len(groups)]
    r = place[0]
    for g, group in enumerate(groups):
        for at, p in enumerate(group):
            block = jnp.dot(
                f_ref[p].reshape(slots * rb, width), inv_ref[p],
                precision=HIGHEST, preferred_element_type=jnp.float32,
            )
            for s in range(slots):
                used = valid[p * slots + s] > 0
                one = jnp.where(used, block[s * rb : (s + 1) * rb], 0.0)
                n_ref[p, s] = one
                row = (at * halves + s % halves) * rb
                scratch[g][s // halves, row : row + rb] = one
        n = len(group) * halves * rb // lines
        for d in range(lines):
            start = pl.multiple_of((r ^ d) * n, 8)
            outs[g * lines + d][...] = scratch[g][:, pl.ds(start, n), :]


def to_planes_kernel(lines, place, *refs):
    r, z = place[0], place[1]
    for m in range(lines):
        which = r ^ ((z + m) % lines)
        for d in range(lines):

            @pl.when(which == d)
            def _(m=m, d=d):
                refs[lines + m][...] = refs[d][...]


def by_core_kernel(lines, place, *refs):
    h = place[2]
    mine, other = refs[lines:]
    for m in range(lines):
        mine[m] = refs[m][h]
        other[m] = refs[m][1 - h]


def assemble_kernel(lines, rb, place, *refs):
    pieces = refs[: 2 * lines]
    hi_ref, lo_ref, held = refs[2 * lines :]
    r, z, h = place[0], place[1], place[2]
    n, width = pieces[0].shape[1:]
    step = math.gcd(n, rb)
    for d in range(lines):
        line = r ^ d
        for which in range(2):
            core = h if which == 0 else 1 - h
            for m in range(lines):
                plane = (z + lines - m) % lines
                for i in range(n // step):
                    flat = line * n + i * step
                    row = (flat // rb) * width + (plane * 2 + core) * rb + flat % rb
                    row = pl.multiple_of(row, 8)
                    held[pl.ds(row, step), :] = pieces[2 * d + which][m, i * step : (i + 1) * step, :]
    panels, depth, _ = hi_ref.shape

    @pl.loop(0, panels * depth // width)
    def _(i):
        row = pl.multiple_of(i * width, width)
        value = held[pl.ds(row, width), :]
        hi = value.astype(jnp.bfloat16)
        p = row // depth
        at = pl.multiple_of(row % depth, width)
        hi_ref[p, pl.ds(at, width), :] = hi
        lo_ref[p, pl.ds(at, width), :] = (value - hi.astype(jnp.float32)).astype(jnp.bfloat16)


def product_kernel(panel_ids, slots, rb, lo, hi, info, where, g_ref, *refs):
    count = len(panel_ids)
    x_hi, x_lo = refs[:count], refs[count : 2 * count]
    mine, other = refs[2 * count :]
    side, tile = pl.program_id(0), pl.program_id(1)
    tile_slots, rows, depth = g_ref.shape
    h = info[4]

    @pl.when(info[2 + side] > 0)
    def _():
        g = g_ref[...].reshape(tile_slots * rows, depth)
        g_hi = g.astype(jnp.bfloat16)
        g_lo = (g - g_hi.astype(jnp.float32)).astype(jnp.bfloat16)
        dot = functools.partial(jnp.dot, preferred_element_type=jnp.float32)
        for k, p in enumerate(panel_ids):
            value = dot(g_hi, x_hi[k][0]) + (dot(g_hi, x_lo[k][0]) + dot(g_lo, x_hi[k][0]))
            for s in range(tile_slots):
                at = where[p * slots + tile * tile_slots + s]
                top = value[s * rows : s * rows + rb]
                bottom = value[s * rows + rb : (s + 1) * rows]

                @pl.when((at >= lo) & (at < hi))
                def _(at=at, top=top, bottom=bottom):
                    mine[side, at - lo] = jnp.where(h == 0, top, bottom)
                    other[side, at - lo] = jnp.where(h == 0, bottom, top)


def product(g3, xs, panel_ids, lo, hi, rb, info, where, sides):
    slots, width, depth = g3.shape
    columns = xs[0][0].shape[2]
    rows = 2 * rb
    tile_slots = math.gcd(slots, max(1, 256 // rows))
    grid = (sides, slots // tile_slots)

    def g_map(side, tile, info, where):
        return (jnp.where(info[2 + side] > 0, tile, 0), info[side], 0)

    x_specs = [
        pl.BlockSpec((1, depth, columns), functools.partial(lambda at, a, b, i, w: (at, 0, 0), at))
        for _, _, at in xs
    ]
    out = jax.ShapeDtypeStruct((sides, hi - lo, rb, columns), jnp.float32)
    out_spec = pl.BlockSpec(out.shape, lambda a, b, i, w: (0, 0, 0, 0))
    flops = 6 * slots * rows * depth * columns * len(xs)
    return pl.pallas_call(
        functools.partial(product_kernel, panel_ids, slots, rb, lo, hi),
        out_shape=(out, out),
        grid_spec=pltpu.PrefetchScalarGridSpec(
            num_scalar_prefetch=2,
            grid=grid,
            in_specs=[pl.BlockSpec((tile_slots, rows, depth), g_map)] + x_specs + x_specs,
            out_specs=(out_spec, out_spec),
        ),
        compiler_params=pltpu.CompilerParams(vmem_limit_bytes=VMEM_LIMIT),
        cost_estimate=pl.CostEstimate(
            flops=flops, bytes_accessed=slots * rows * depth * 4, transcendentals=0
        ),
    )(info, where, g3, *[x[0] for x in xs], *[x[1] for x in xs])


def finish_kernel(parts, bounds, where, n_ref, *refs):
    ins = refs[: 4 * parts]
    panel_ref, diag_ref, total = refs[4 * parts :]
    panels, slots, rb, width = n_ref.shape
    for k in range(parts):
        own, swapped, up, down = ins[4 * k : 4 * k + 4]
        total[bounds[k] : bounds[k + 1]] = (own[0] + swapped[0]) + (up[...] + down[...])
    for p in range(panels):
        for s in range(slots):
            at = where[p * slots + s]
            value = total[jnp.maximum(at, 0)]
            panel_ref[p, s] = jnp.where(at >= 0, -value, 0.0)
        diag_ref[p] = lax.dot_general(
            n_ref[p].reshape(slots * rb, width),
            panel_ref[p].reshape(slots * rb, width),
            (((0,), (0,)), ((), ())),
            precision=HIGHEST,
            preferred_element_type=jnp.float32,
        )


def on_device(
    lines, inverse_matrix, factor_blocks, factor_inverse, diag_given, block_lists, list_mask, slot_of_block
):
    panels, slots, rb, width = factor_blocks.shape
    halves = inverse_matrix.shape[1] // width
    f32 = jnp.float32
    r = lax.axis_index("prow").astype(jnp.int32)
    col = lax.axis_index("pcol").astype(jnp.int32)
    z, h = col // 2, col % 2
    place = jnp.stack([r, z, h])

    def send(value, to):
        pairs = []
        for a in range(lines):
            for b in range(lines):
                for c in range(2):
                    target = to(a, b, c)
                    if target is not None:
                        ta, tb, tc = target
                        pairs.append(((a * lines + b) * 2 + c, (ta * lines + tb) * 2 + tc))
        return lax.ppermute(value, AXES, pairs)

    def swap(value):
        return send(value, lambda a, b, c: (a, b, 1 - c))

    def across(value, d):
        return send(value, lambda a, b, c: (a ^ d, b, c))

    def along(value, m):
        return send(value, lambda a, b, c: (a, (b + m) % lines, c))

    slot_valid = valid_slots(block_lists, list_mask, slot_of_block)
    row_valid = lax.dynamic_slice_in_dim(slot_valid, r * slots, slots, 1).reshape(panels * slots)
    order = jnp.arange(panels * slots, dtype=jnp.int32)
    before = jnp.sum(jnp.where(order[None, :] < order[:, None], row_valid[None, :], 0), axis=1)
    where = jnp.where(row_valid > 0, before, -1).astype(jnp.int32)

    keep = 3 * panels * slots // 4
    half = panels // 2
    groups = [tuple(range(half)), tuple(range(half, panels))]
    first = keep - slots * (panels - half)
    bounds = [0, first, keep]
    chunk_panels = [tuple(range(half)), tuple(range(half - 1, panels))]

    part_shapes = [(2, len(g) * halves * rb // lines, width) for g in groups]
    made = call(
        functools.partial(normalize_kernel, groups, lines),
        [jax.ShapeDtypeStruct(factor_blocks.shape, f32)]
        + [jax.ShapeDtypeStruct(s, f32) for s in part_shapes for _ in range(lines)],
        [pltpu.VMEM((2, len(g) * halves * rb, width), f32) for g in groups],
        n_scalar=2, n_in=2, flops=12 * factor_blocks.size * width, moved=12 * factor_blocks.size,
    )(place, row_valid, factor_blocks, factor_inverse)
    normalized = made[0]

    split = []
    for g, group in enumerate(groups):
        parts = made[1 + g * lines : 1 + (g + 1) * lines]
        shape = part_shapes[g]
        moved = 8 * lines * math.prod(shape)
        held = [parts[0]] + [across(parts[d], d) for d in range(1, lines)]
        outgoing = call(
            functools.partial(to_planes_kernel, lines),
            [jax.ShapeDtypeStruct(shape, f32)] * lines, n_in=lines, moved=moved,
        )(place, *held)
        held = [outgoing[0]] + [along(outgoing[m], m) for m in range(1, lines)]
        piece = jax.ShapeDtypeStruct((lines,) + shape[1:], f32)
        mine, other = call(
            functools.partial(by_core_kernel, lines), [piece, piece], n_in=lines, moved=moved
        )(place, *held)
        swapped = swap(other)
        pieces = [mine, swapped]
        if lines == 4:
            mine_1, swapped_1 = across(mine, 1), across(swapped, 1)
            mine_2, swapped_2 = across(mine, 2), across(swapped, 2)
            pieces += [mine_1, swapped_1, mine_2, swapped_2]
            pieces += [across(mine_1, 2), across(swapped_2, 1)]
        else:
            for d in range(1, lines):
                pieces += [across(mine, d), across(swapped, d)]
        block = jax.ShapeDtypeStruct((len(group), halves * width, width), jnp.bfloat16)
        x_hi, x_lo = call(
            functools.partial(assemble_kernel, lines, rb),
            [block, block],
            [pltpu.VMEM((len(group) * halves * width, width), f32)],
            n_in=2 * lines, moved=8 * len(group) * halves * width * width,
        )(place, *pieces)
        split += [(x_hi, x_lo, at) for at in range(len(group))]

    g3 = inverse_matrix.reshape(slots, width, halves * width)
    flag = lambda value: value.astype(jnp.int32)
    finals = []
    for k, ids in enumerate(chunk_panels):
        lo, hi = bounds[k], bounds[k + 1]
        xs = [split[p] for p in ids]
        make = functools.partial(product, g3, xs, ids, lo, hi, rb)
        up = down = None
        for step in range(lines - 1):
            j_up = lines - 1 - step + z
            j_down = step - (lines - 1 - z)
            info = jnp.stack([
                jnp.clip(j_up, 0, lines - 1), jnp.clip(j_down, 0, lines - 1),
                flag(z <= step), flag(z >= lines - 1 - step), h,
            ])
            mine, other = make(info, where, 2)
            swapped = swap(other)
            send_up = mine[0] + swapped[0]
            send_down = mine[1] + swapped[1]
            if step:
                send_up = send_up + up
                send_down = send_down + down
            up = send(send_up, lambda a, b, c: (a, b + 1, c) if b <= step else None)
            down = send(send_down, lambda a, b, c: (a, b - 1, c) if b >= lines - 1 - step else None)
        info = jnp.stack([z, z, jnp.int32(1), jnp.int32(1), h])
        own, other = make(info, where, 1)
        finals += [own, swap(other), up, down]

    panel_inverse, terms = call(
        functools.partial(finish_kernel, len(chunk_panels), bounds),
        [
            jax.ShapeDtypeStruct(factor_blocks.shape, f32),
            jax.ShapeDtypeStruct(factor_inverse.shape, f32),
        ],
        [pltpu.VMEM((keep, rb, width), f32)],
        n_in=1 + len(finals), flops=12 * factor_blocks.size * width, moved=20 * factor_blocks.size,
    )(where, normalized, *finals)

    pick = lambda value, at: lax.dynamic_index_in_dim(value, at, 0, False)
    two = terms.reshape(2, half * width, width)
    total = pick(two, h) + swap(pick(two, 1 - h))
    parts = total.reshape(lines, -1, width)
    total = pick(parts, r)
    for piece in [across(pick(parts, r ^ d), d) for d in range(1, lines)]:
        total = total + piece
    parts = total.reshape(lines, -1, width)
    total = pick(parts, z)
    for piece in [along(pick(parts, (z + m) % lines), m) for m in range(1, lines)]:
        total = total + piece
    pieces = [total] + [along(total, m) for m in range(1, lines)]
    gathered = jnp.zeros((lines,) + total.shape, f32)
    for m in range(lines):
        gathered = lax.dynamic_update_index_in_dim(gathered, pieces[m], (z - m) % lines, 0)
    total = gathered.reshape(-1, width)
    pieces = [total] + [across(total, d) for d in range(1, lines)]
    gathered = jnp.zeros((lines,) + total.shape, f32)
    for d in range(lines):
        gathered = lax.dynamic_update_index_in_dim(gathered, pieces[d], r ^ d, 0)
    total = gathered.reshape(half, width, width)
    swapped = swap(total)
    summed = jnp.concatenate([jnp.where(h == 0, total, swapped), jnp.where(h == 0, swapped, total)], 0)
    return (panel_inverse, diag_given - summed)


def solution(mesh):
    lines = mesh.shape["prow"]
    if mesh.shape["pcol"] != 2 * lines:
        raise ValueError("mesh shape")
    placed = (P("prow", "pcol"), P(None, "prow", "pcol", None), P(), P(), P(), P(), P())
    return jax.shard_map(
        functools.partial(on_device, lines),
        mesh=mesh,
        in_specs=placed,
        out_specs=(P(None, "prow", "pcol", None), P()),
        check_vma=False,
    )
```

time: 629 us -> 340 us (0.54)
  waiting for transfers between devices: 481 us -> 86.9 us
  Pallas kernels: 0 us -> 145 us
  starting transfers between devices: 0.34 us -> 85.4 us
  matrix products: 76.7 us -> 0 us
  local copies, waits for them, and re-layouts: 33.9 us -> 8.73 us
  between operations: 13.9 us -> 1.18 us
  other arithmetic: 23 us -> 12.8 us
    psum x2 -> x0, waiting for transfers between devices: 262 us -> none  [the longest x1 134 us: spread(): return lax.psum(kept, axis)]
    pallas_call x0 -> x16, Pallas kernels: none -> 145 us  [the longest x8 116 us: product(): pl.pallas_call(functools.partial(product_kernel, panel_ids, slots, rb, lo...]
    all_gather x1 -> x0, waiting for transfers between devices: 120 us -> none  [on_device(): full_rows = lax.all_gather(normalized, 'pcol', axis=2, tiled=True)]
    reduce_scatter x1 -> x0, waiting for transfers between devices: 99.1 us -> none  [on_device(): lax.psum_scatter(packed, 'pcol', scatter_dimension=1, tiled=True)]
    ppermute x0 -> x60, waiting for transfers between devices: none -> 86.9 us  [send(): return lax.ppermute(value, AXES, pairs)]
    ppermute x0 -> x60, starting transfers between devices: none -> 85.4 us  [send(): return lax.ppermute(value, AXES, pairs)]
    dot_general x3 -> x0, matrix products: 76.7 us -> none  [the longest x1 69 us: on_device(): jnp.einsum('ij,pjk->pik', inverse_matrix, stacked, precision=highest, pre...]
    select_n x4 -> x2, other arithmetic: 15 us -> 0.59 us  [the longest x1 0.52 us: on_device(): where = jnp.where(row_valid > 0, before, -1).astype(jnp.int32)]
  transfers between devices with their start and end apart: 4 -> 60, of which waited for: 4 -> 22; matrix products, arithmetic and copies ran while one was open for 0% -> 3% of each run, Pallas kernels for 0% -> 33%
where the time goes in v1:
time: 340 us
  Pallas kernels  145 us (43%)
  waiting for transfers between devices  86.9 us (26%)
  starting transfers between devices  85.4 us (25%)
  other arithmetic  12.8 us (4%)
  local copies, waits for them, and re-layouts  8.73 us (3%)
    pallas_call x8, Pallas kernels, product(): pl.pallas_call(functools.partial(product_kernel, panel_ids, slots, rb, lo...  116 us
    ppermute x60, waiting for transfers between devices, send(): return lax.ppermute(value, AXES, pairs)  86.9 us
    ppermute x60, starting transfers between devices, send(): return lax.ppermute(value, AXES, pairs)  85.4 us
    pallas_call x2, Pallas kernels, on_device(): call(functools.partial(assemble_kernel, lines, rb), [block, block], [pltp...  8.84 us
  transfers between devices with their start and end apart: 60, of which 22 were waited for; matrix products, arithmetic and copies ran while one was open for 3% of the time, Pallas kernels for 33%

profile of v1, /device:TPU:0, one launch (start us, length us, event | category | flops | bytes accessed | tf_op | source)
XLA Modules:
  0.0 339.6 jit_solution(1571915844346185700)
XLA Ops:
  3.7 4.8 %shard_map.86 = (f32[4,12,32,256]{3,2,1,0:T(8,128)}, f32[2,96,256]{2,1,0:T(8,128)}, f32[2,96,256]{2,1,0:T(8,128)}, f32[2,96,256]{2,1,0:T(8,128)}, f32[2,96,256]{...) custom-call(s32[3]{0:T(128)} %pad_add_fusion.place, ...), custom_call_target="tpu_custom_call" | custom-call | flops 1207959552 | bytes 4718592 | tf_op jit(solution)/shard_map/pallas_call | solution.py:239
  8.5 2.9 collective-permute-start
  11.5 1.5 collective-permute-start.1
  13.0 2.0 collective-permute-start.23
  15.0 1.5 collective-permute-start.24
  17.4 3.0 collective-permute-start.25
  20.4 3.3 collective-permute-done.1.refs_2_
  24.5 2.3 shard_map.87
  26.7 1.6 collective-permute-start.3
  28.3 2.6 collective-permute-start.4
  30.9 1.3 collective-permute-start.5
  33.0 2.3 shard_map.94
  35.9 1.9 collective-permute-start.27
  37.9 1.6 collective-permute-start.28
  39.5 6.7 %collective-permute-done.4.refs_2_ = f32[2,96,256]{2,1,0:T(8,128)S(1)} collective-permute-done((f32[2,96,256]{2,1,0:T(8,128)}, f32[2,96,256]{2,1,0:T(8,128)S(1)}, u32[]{:S(2)}, u32[]{:S(2)}) %collective-permute-start.4) | collective-permute-done | bytes 196640 | tf_op jit(solution)/shard_map/ppermute | solution.py:214
  47.0 2.2 shard_map.88
  49.1 2.1 collective-permute-start.7
  51.3 6.9 %collective-permute-done.27.refs_2_ = f32[2,96,256]{2,1,0:T(8,128)S(1)} collective-permute-done((f32[2,96,256]{2,1,0:T(8,128)}, f32[2,96,256]{2,1,0:T(8,128)S(1)}, u32[]{:S(2)}, u32[]{:S(2)}) %collective-permute-start.27) | collective-permute-done | bytes 196640 | tf_op jit(solution)/shard_map/ppermute | solution.py:214
  59.0 2.2 shard_map.95
  61.2 1.5 collective-permute-start.30
  63.2 1.3 collective-permute-start.8
  66.6 6.8 %collective-permute-done.30.refs_2_ = f32[4,96,256]{2,1,0:T(8,128)S(1)} collective-permute-done((f32[4,96,256]{2,1,0:T(8,128)}, f32[4,96,256]{2,1,0:T(8,128)S(1)}, u32[]{:S(2)}, u32[]{:S(2)}) %collective-permute-start.30) | collective-permute-done | bytes 393248 | tf_op jit(solution)/shard_map/ppermute | solution.py:214
  75.3 6.4 %collective-permute-done.8.refs_3_ = f32[4,96,256]{2,1,0:T(8,128)S(1)} collective-permute-done((f32[4,96,256]{2,1,0:T(8,128)S(1)}, f32[4,96,256]{2,1,0:T(8,128)S(1)}, u32[]{:S(2)}, u32[]{:S(2)}) %collective-permute-start.8) | collective-permute-done | bytes 393248 | tf_op jit(solution)/shard_map/ppermute | solution.py:214
  81.8 1.5 collective-permute-start.31
  83.8 7.7 %collective-permute-done.33.refs_5_ = f32[4,96,256]{2,1,0:T(8,128)S(1)} collective-permute-done((f32[4,96,256]{2,1,0:T(8,128)S(1)}, f32[4,96,256]{2,1,0:T(8,128)S(1)}, u32[]{:S(2)}, u32[]{:S(2)}) %collective-permute-start.33) | collective-permute-done | bytes 393248 | tf_op jit(solution)/shard_map/ppermute | solution.py:214
  93.4 4.5 %shard_map.89 = (bf16[2,1536,256]{2,1,0:T(8,128)(2,1)}, bf16[2,1536,256]{2,1,0:T(8,128)(2,1)}) custom-call(s32[3]{0:T(128)} %pad_add_fusion.place, f32[4,96,256]{2,1,0:T(8,128)} %get-tuple-element.54.refs_0_, f32[4,96,256]{2,1,0:T(8,128)} %copy-done.15, f32[4,96,256]{2,1,0:T(8,128)} %copy-done.12, f32[4,96,256]{2,1,0:T(8,128)} %copy-done.20, ...), custom_call_target="tpu_custom_call" | custom-call | bytes 6291456 | tf_op jit(solution)/shard_map/pallas_call | solution.py:274
  97.9 2.1 collective-permute-done.32.refs_4_
  99.9 7.8 %collective-permute-done.34.refs_6_ = f32[4,96,256]{2,1,0:T(8,128)} collective-permute-done((f32[4,96,256]{2,1,0:T(8,128)S(1)}, f32[4,96,256]{2,1,0:T(8,128)}, u32[]{:S(2)}, u32[]{:S(2)}) %collective-permute-start.34) | collective-permute-done | bytes 393248 | tf_op jit(solution)/shard_map/ppermute | solution.py:214
  107.8 4.4 %shard_map.96 = (bf16[2,1536,256]{2,1,0:T(8,128)(2,1)}, bf16[2,1536,256]{2,1,0:T(8,128)(2,1)}) custom-call(s32[3]{0:T(128)} %pad_add_fusion.place, f32[4,96,256]{2,1,0:T(8,128)} %get-tuple-element.74.refs_0_, f32[4,96,256]{2,1,0:T(8,128)} %copy-done.14, f32[4,96,256]{2,1,0:T(8,128)} %copy-done.16, f32[4,96,256]{2,1,0:T(8,128)} %collective-permute-done.31.refs_3_, ...), custom_call_target="tpu_custom_call" | custom-call | bytes 6291456 | tf_op jit(solution)/shard_map/pallas_call | solution.py:274
  112.2 16.4 %shard_map.100 = (f32[2,24,32,256]{3,2,1,0:T(8,128)}, f32[2,24,32,256]{3,2,1,0:T(8,128)}) custom-call(s32[5]{0:T(128)} %stack.131.info, s32[48]{0:T(128)} %compare_select_fusion.where, f32[12,256,1536]{2,1,0:T(8,128)} %bitcast.110, bf16[2,1536,256]{2,1,0:T(8,128)(2,1)} %get-tuple-element.56.refs_0_.refs_1_, ...), custom_call_target="tpu_custom_call" | custom-call | flops 5435817984 | bytes 4718592 | tf_op jit(solution)/shard_map/pallas_call | solution.py:157
  130.5 12.8 %shard_map.93 = (f32[2,12,32,256]{3,2,1,0:T(8,128)}, f32[2,12,32,256]{3,2,1,0:T(8,128)}) custom-call(s32[5]{0:T(128)} %stack.131.info, s32[48]{0:T(128)} %compare_select_fusion.where, f32[12,256,1536]{2,1,0:T(8,128)} %bitcast.111, bf16[2,1536,256]{2,1,0:T(8,128)(2,1)} %get-tuple-element.56.refs_0_.refs_1_, ...), custom_call_target="tpu_custom_call" | custom-call | flops 3623878656 | bytes 4718592 | tf_op jit(solution)/shard_map/pallas_call | solution.py:157
  143.9 12.8 %shard_map.92 = (f32[2,12,32,256]{3,2,1,0:T(8,128)}, f32[2,12,32,256]{3,2,1,0:T(8,128)}) custom-call(s32[5]{0:T(128)} %stack.124.info, s32[48]{0:T(128)} %compare_select_fusion.where, f32[12,256,1536]{2,1,0:T(8,128)} %bitcast.112, bf16[2,1536,256]{2,1,0:T(8,128)(2,1)} %get-tuple-element.56.refs_0_.refs_1_, ...), custom_call_target="tpu_custom_call" | custom-call | flops 3623878656 | bytes 4718592 | tf_op jit(solution)/shard_map/pallas_call | solution.py:157
  156.7 16.6 %shard_map.99 = (f32[2,24,32,256]{3,2,1,0:T(8,128)}, f32[2,24,32,256]{3,2,1,0:T(8,128)}) custom-call(s32[5]{0:T(128)} %stack.124.info, s32[48]{0:T(128)} %compare_select_fusion.where, f32[12,256,1536]{2,1,0:T(8,128)} %bitcast.113, bf16[2,1536,256]{2,1,0:T(8,128)(2,1)} %get-tuple-element.56.refs_0_.refs_1_, ...), custom_call_target="tpu_custom_call" | custom-call | flops 5435817984 | bytes 4718592 | tf_op jit(solution)/shard_map/pallas_call | solution.py:157
  174.7 1.6 collective-permute-start.40
  176.2 16.4 %shard_map.98 = (f32[2,24,32,256]{3,2,1,0:T(8,128)}, f32[2,24,32,256]{3,2,1,0:T(8,128)}) custom-call(s32[5]{0:T(128)} %stack.117.info, s32[48]{0:T(128)} %compare_select_fusion.where, f32[12,256,1536]{2,1,0:T(8,128)} %bitcast.114, bf16[2,1536,256]{2,1,0:T(8,128)(2,1)} %get-tuple-element.56.refs_0_.refs_1_, ...), custom_call_target="tpu_custom_call" | custom-call | flops 5435817984 | bytes 4718592 | tf_op jit(solution)/shard_map/pallas_call | solution.py:157
  193.7 15.7 %shard_map.97 = (f32[1,24,32,256]{3,2,1,0:T(8,128)}, f32[1,24,32,256]{3,2,1,0:T(8,128)}) custom-call(s32[5]{0:T(128)} %pad_add_fusion.1.info, s32[48]{0:T(128)} %compare_select_fusion.where, f32[12,256,1536]{2,1,0:T(8,128)} %bitcast.115, bf16[2,1536,256]{2,1,0:T(8,128)(2,1)} %get-tuple-element.56.refs_0_.refs_1_, ...), custom_call_target="tpu_custom_call" | custom-call | flops 5435817984 | bytes 4718592 | tf_op jit(solution)/shard_map/pallas_call | solution.py:157
  210.3 1.4 collective-permute-start.20
  211.7 1.3 collective-permute-start.17
  214.3 1.5 collective-permute-start.41
  215.8 12.8 %shard_map.91 = (f32[2,12,32,256]{3,2,1,0:T(8,128)}, f32[2,12,32,256]{3,2,1,0:T(8,128)}) custom-call(s32[5]{0:T(128)} %stack.117.info, s32[48]{0:T(128)} %compare_select_fusion.where, f32[12,256,1536]{2,1,0:T(8,128)} %bitcast.116, bf16[2,1536,256]{2,1,0:T(8,128)(2,1)} %get-tuple-element.56.refs_0_.refs_1_, ...), custom_call_target="tpu_custom_call" | custom-call | flops 3623878656 | bytes 4718592 | tf_op jit(solution)/shard_map/pallas_call | solution.py:157
  229.0 2.3 fusion.12
  231.3 1.5 collective-permute-start.21
  232.8 12.3 %shard_map.90 = (f32[1,12,32,256]{3,2,1,0:T(8,128)}, f32[1,12,32,256]{3,2,1,0:T(8,128)}) custom-call(s32[5]{0:T(128)} %pad_add_fusion.1.info, s32[48]{0:T(128)} %compare_select_fusion.where, f32[12,256,1536]{2,1,0:T(8,128)} %bitcast.117, bf16[2,1536,256]{2,1,0:T(8,128)(2,1)} %get-tuple-element.56.refs_0_.refs_1_, ...), custom_call_target="tpu_custom_call" | custom-call | flops 3623878656 | bytes 4718592 | tf_op jit(solution)/shard_map/pallas_call | solution.py:157
  245.7 12.1 %collective-permute-start.18 = (f32[12,32,256]{2,1,0:T(8,128)}, f32[12,32,256]{2,1,0:T(8,128)S(1)}, u32[]{:S(2)}, u32[]{:S(2)}) collective-permute-start(f32[12,32,256]{2,1,0:T(8,128)} %get-tuple-element.99), channel_id=1, source_target_pairs={{0,2},{1,3},{2,4},{3,5},{8,10},{9,11},{10,12},{11,13},{16,18},{17,... | collective-permute-start | bytes 1179656 | tf_op jit(solution)/shard_map/ppermute | solution.py:214
  258.3 4.5 %collective-permute-start.42 = (f32[24,32,256]{2,1,0:T(8,128)S(1)}, f32[24,32,256]{2,1,0:T(8,128)S(1)}, u32[]{:S(2)}, u32[]{:S(2)}) collective-permute-start(f32[24,32,256]{2,1,0:T(8,128)S(1)} %get-tuple-element.91), channel_id=1, source_target_pairs={{0,2},{1,3},{2,4},{3,5},{4,6},{5,7},{8,10},{9,11},{10,12},{11,13},... | collective-permute-start | bytes 2359304 | tf_op jit(solution)/shard_map/ppermute | solution.py:214
  264.1 3.4 collective-permute-done.18
  267.5 2.4 fusion.14
  269.9 5.3 %collective-permute-start.19 = (f32[12,32,256]{2,1,0:T(8,128)}, f32[12,32,256]{2,1,0:T(8,128)}, u32[]{:S(2)}, u32[]{:S(2)}) collective-permute-start(f32[12,32,256]{2,1,0:T(8,128)} %get-tuple-element.97), channel_id=1, source_target_pairs={{0,2},{1,3},{2,4},{3,5},{4,6},{5,7},{8,10},{9,11},{10,12},{11,13},... | collective-permute-start | bytes 1179656 | tf_op jit(solution)/shard_map/ppermute | solution.py:214
  275.2 1.5 collective-permute-start.22
  276.7 15.6 %collective-permute-done.19.refs_2_ = f32[12,32,256]{2,1,0:T(8,128)} collective-permute-done((f32[12,32,256]{2,1,0:T(8,128)}, f32[12,32,256]{2,1,0:T(8,128)}, u32[]{:S(2)}, u32[]{:S(2)}) %collective-permute-start.19) | collective-permute-done | bytes 393248 | tf_op jit(solution)/shard_map/ppermute | solution.py:214
  293.3 6.1 %shard_map.101 = (f32[4,12,32,256]{3,2,1,0:T(8,128)}, f32[4,256,256]{2,1,0:T(8,128)}) custom-call(s32[48]{0:T(128)} %compare_select_fusion.where, f32[4,12,32,256]{3,2,1,0:T(8,128)} %get-tuple-element.45.n_ref, f32[1,12,32,256]{3,2,1,0:T(8,128)} %get-tuple-element.58.refs_0_, f32[1,12,32,256]{3,2,1,0:T(8,128)} %copy-done.11, ...), custom_call_target="tpu_custom_call" | custom-call | flops 1207959552 | bytes 7864320 | tf_op jit(solution)/shard_map/pallas_call | solution.py:310
  300.6 1.9 collective-permute-done.46
  304.1 1.6 collective-permute-start.48
  305.7 1.5 collective-permute-start.47
  307.1 3.8 %collective-permute-done.49 = f32[128,256]{1,0:T(8,128)S(1)} collective-permute-done((f32[128,256]{1,0:T(8,128)S(1)}, f32[128,256]{1,0:T(8,128)S(1)}, u32[]{:S(2)}, u32[]{:S(2)}) %collective-permute-start.49) | collective-permute-done | bytes 131104 | tf_op jit(solution)/shard_map/ppermute | solution.py:214
  312.3 4.3 %collective-permute-start.51 = (f32[32,256]{1,0:T(8,128)S(1)}, f32[32,256]{1,0:T(8,128)S(1)}, u32[]{:S(2)}, u32[]{:S(2)}) collective-permute-start(f32[32,256]{1,0:T(8,128)S(1)} %get-tuple-element.109), channel_id=1, source_target_pairs={{0,4},{1,5},{2,6},{3,7},{4,0},{5,1},{6,2},{7,3},{8,12},{9,13},{10,... | collective-permute-start | bytes 98312 | tf_op jit(solution)/shard_map/ppermute | solution.py:214
  316.6 1.9 collective-permute-start.50
  319.1 3.2 collective-permute-done.50
  323.4 2.8 collective-permute-start.55
  326.2 1.9 collective-permute-done.53
  330.5 1.6 collective-permute-start.58
  332.2 1.4 collective-permute-done.56
  334.9 1.5 collective-permute-done.58
  336.5 1.9 collective-permute-done.59
  (177 shorter events, 36.1 us)
Async XLA Ops:
  8.5 8.9 %collective-permute-start = (f32[2,96,256]{2,1,0:T(8,128)}, f32[2,96,256]{2,1,0:T(8,128)S(1)}, u32[]{:S(2)}, u32[]{:S(2)}) collective-permute-start(f32[2,96,256]{2,1,0:T(8,128)} %get-tuple-element.47), channel_id=1, source_target_pairs={{0,8},{1,9},{2,10},{3,11},{4,12},{5,13},{6,14},{7,15},{8,0},{9,1},... | collective-permute-start | bytes 589832 | tf_op jit(solution)/shard_map/ppermute | solution.py:214
  11.5 12.2 %collective-permute-start.1 = (f32[2,96,256]{2,1,0:T(8,128)}, f32[2,96,256]{2,1,0:T(8,128)S(1)}, u32[]{:S(2)}, u32[]{:S(2)}) collective-permute-start(f32[2,96,256]{2,1,0:T(8,128)} %get-tuple-element.48), channel_id=1, source_target_pairs={{0,16},{1,17},{2,18},{3,19},{4,20},{5,21},{6,22},{7,23},{8,24},{9,... | collective-permute-start | bytes 589832 | tf_op jit(solution)/shard_map/ppermute | solution.py:214
  13.0 10.7 %collective-permute-start.2 = (f32[2,96,256]{2,1,0:T(8,128)}, f32[2,96,256]{2,1,0:T(8,128)S(1)}, u32[]{:S(2)}, u32[]{:S(2)}) collective-permute-start(f32[2,96,256]{2,1,0:T(8,128)} %get-tuple-element.49), channel_id=1, source_target_pairs={{0,24},{1,25},{2,26},{3,27},{4,28},{5,29},{6,30},{7,31},{8,16},{9,... | collective-permute-start | bytes 589832 | tf_op jit(solution)/shard_map/ppermute | solution.py:214
  13.0 17.9 %collective-permute-start.23 = (f32[2,96,256]{2,1,0:T(8,128)}, f32[2,96,256]{2,1,0:T(8,128)S(1)}, u32[]{:S(2)}, u32[]{:S(2)}) collective-permute-start(f32[2,96,256]{2,1,0:T(8,128)} %get-tuple-element.67), channel_id=1, source_target_pairs={{0,8},{1,9},{2,10},{3,11},{4,12},{5,13},{6,14},{7,15},{8,0},{9,1},... | collective-permute-start | bytes 589832 | tf_op jit(solution)/shard_map/ppermute | solution.py:214
  15.0 17.3 %collective-permute-start.24 = (f32[2,96,256]{2,1,0:T(8,128)}, f32[2,96,256]{2,1,0:T(8,128)S(1)}, u32[]{:S(2)}, u32[]{:S(2)}) collective-permute-start(f32[2,96,256]{2,1,0:T(8,128)} %get-tuple-element.68), channel_id=1, source_target_pairs={{0,16},{1,17},{2,18},{3,19},{4,20},{5,21},{6,22},{7,23},{8,24},{9,... | collective-permute-start | bytes 589832 | tf_op jit(solution)/shard_map/ppermute | solution.py:214
  17.4 14.8 %collective-permute-start.25 = (f32[2,96,256]{2,1,0:T(8,128)}, f32[2,96,256]{2,1,0:T(8,128)S(1)}, u32[]{:S(2)}, u32[]{:S(2)}) collective-permute-start(f32[2,96,256]{2,1,0:T(8,128)} %get-tuple-element.69), channel_id=1, source_target_pairs={{0,24},{1,25},{2,26},{3,27},{4,28},{5,29},{6,30},{7,31},{8,16},{9,... | collective-permute-start | bytes 589832 | tf_op jit(solution)/shard_map/ppermute | solution.py:214
  24.5 68.2 %copy-start.34 = (s32[48]{0:T(128)S(1)}, s32[48]{0:T(128)}, u32[]{:S(2)}) copy-start(s32[48]{0:T(128)} %reshape.43.valid) | copy-start | bytes 580
  26.7 11.1 %collective-permute-start.3 = (f32[2,96,256]{2,1,0:T(8,128)}, f32[2,96,256]{2,1,0:T(8,128)S(1)}, u32[]{:S(2)}, u32[]{:S(2)}) collective-permute-start(f32[2,96,256]{2,1,0:T(8,128)} %get-tuple-element.51), channel_id=1, source_target_pairs={{0,2},{1,3},{2,4},{3,5},{4,6},{5,7},{6,0},{7,1},{8,10},{9,11},{10,... | collective-permute-start | bytes 589832 | tf_op jit(solution)/shard_map/ppermute | solution.py:214
  28.3 17.9 %collective-permute-start.4 = (f32[2,96,256]{2,1,0:T(8,128)}, f32[2,96,256]{2,1,0:T(8,128)S(1)}, u32[]{:S(2)}, u32[]{:S(2)}) collective-permute-start(f32[2,96,256]{2,1,0:T(8,128)} %get-tuple-element.52), channel_id=1, source_target_pairs={{0,4},{1,5},{2,6},{3,7},{4,0},{5,1},{6,2},{7,3},{8,12},{9,13},{10,... | collective-permute-start | bytes 589832 | tf_op jit(solution)/shard_map/ppermute | solution.py:214
  30.9 15.3 %collective-permute-start.5 = (f32[2,96,256]{2,1,0:T(8,128)}, f32[2,96,256]{2,1,0:T(8,128)S(1)}, u32[]{:S(2)}, u32[]{:S(2)}) collective-permute-start(f32[2,96,256]{2,1,0:T(8,128)} %get-tuple-element.53), channel_id=1, source_target_pairs={{0,6},{1,7},{2,0},{3,1},{4,2},{5,3},{6,4},{7,5},{8,14},{9,15},{10,... | collective-permute-start | bytes 589832 | tf_op jit(solution)/shard_map/ppermute | solution.py:214
  35.3 16.0 %collective-permute-start.26 = (f32[2,96,256]{2,1,0:T(8,128)}, f32[2,96,256]{2,1,0:T(8,128)S(1)}, u32[]{:S(2)}, u32[]{:S(2)}) collective-permute-start(f32[2,96,256]{2,1,0:T(8,128)} %get-tuple-element.71), channel_id=1, source_target_pairs={{0,2},{1,3},{2,4},{3,5},{4,6},{5,7},{6,0},{7,1},{8,10},{9,11},{10,... | collective-permute-start | bytes 589832 | tf_op jit(solution)/shard_map/ppermute | solution.py:214
  35.9 22.3 %collective-permute-start.27 = (f32[2,96,256]{2,1,0:T(8,128)}, f32[2,96,256]{2,1,0:T(8,128)S(1)}, u32[]{:S(2)}, u32[]{:S(2)}) collective-permute-start(f32[2,96,256]{2,1,0:T(8,128)} %get-tuple-element.72), channel_id=1, source_target_pairs={{0,4},{1,5},{2,6},{3,7},{4,0},{5,1},{6,2},{7,3},{8,12},{9,13},{10,... | collective-permute-start | bytes 589832 | tf_op jit(solution)/shard_map/ppermute | solution.py:214
  37.9 20.4 %collective-permute-start.28 = (f32[2,96,256]{2,1,0:T(8,128)}, f32[2,96,256]{2,1,0:T(8,128)S(1)}, u32[]{:S(2)}, u32[]{:S(2)}) collective-permute-start(f32[2,96,256]{2,1,0:T(8,128)} %get-tuple-element.73), channel_id=1, source_target_pairs={{0,6},{1,7},{2,0},{3,1},{4,2},{5,3},{6,4},{7,5},{8,14},{9,15},{10,... | collective-permute-start | bytes 589832 | tf_op jit(solution)/shard_map/ppermute | solution.py:214
  49.1 14.1 %collective-permute-start.7 = (f32[4,96,256]{2,1,0:T(8,128)}, f32[4,96,256]{2,1,0:T(8,128)S(1)}, u32[]{:S(2)}, u32[]{:S(2)}) collective-permute-start(f32[4,96,256]{2,1,0:T(8,128)} %get-tuple-element.54.refs_0_), channel_id=1, source_target_pairs={{0,8},{1,9},{2,10},{3,11},{4,12},{5,13},{6,14},{7,15},{8,0},{9,1},... | collective-permute-start | bytes 1179656 | tf_op jit(solution)/shard_map/ppermute | solution.py:214
  51.2 13.3 %collective-permute-start.9 = (f32[4,96,256]{2,1,0:T(8,128)}, f32[4,96,256]{2,1,0:T(8,128)S(1)}, u32[]{:S(2)}, u32[]{:S(2)}) collective-permute-start(f32[4,96,256]{2,1,0:T(8,128)} %get-tuple-element.54.refs_0_), channel_id=1, source_target_pairs={{0,16},{1,17},{2,18},{3,19},{4,20},{5,21},{6,22},{7,23},{8,24},{9,... | collective-permute-start | bytes 1179656 | tf_op jit(solution)/shard_map/ppermute | solution.py:214
  51.2 11.5 %collective-permute-start.6 = (f32[4,96,256]{2,1,0:T(8,128)}, f32[4,96,256]{2,1,0:T(8,128)S(1)}, u32[]{:S(2)}, u32[]{:S(2)}) collective-permute-start(f32[4,96,256]{2,1,0:T(8,128)} %get-tuple-element.55), channel_id=1, source_target_pairs={{0,1},{1,0},{2,3},{3,2},{4,5},{5,4},{6,7},{7,6},{8,9},{9,8},{10,11... | collective-permute-start | bytes 1179656 | tf_op jit(solution)/shard_map/ppermute | solution.py:214
  61.2 4.1 %collective-permute-start.29 = (f32[4,96,256]{2,1,0:T(8,128)}, f32[4,96,256]{2,1,0:T(8,128)S(1)}, u32[]{:S(2)}, u32[]{:S(2)}) collective-permute-start(f32[4,96,256]{2,1,0:T(8,128)} %get-tuple-element.75), channel_id=1, source_target_pairs={{0,1},{1,0},{2,3},{3,2},{4,5},{5,4},{6,7},{7,6},{8,9},{9,8},{10,11... | collective-permute-start | bytes 1179656 | tf_op jit(solution)/shard_map/ppermute | solution.py:214
  61.2 12.1 %collective-permute-start.30 = (f32[4,96,256]{2,1,0:T(8,128)}, f32[4,96,256]{2,1,0:T(8,128)S(1)}, u32[]{:S(2)}, u32[]{:S(2)}) collective-permute-start(f32[4,96,256]{2,1,0:T(8,128)} %get-tuple-element.74.refs_0_), channel_id=1, source_target_pairs={{0,8},{1,9},{2,10},{3,11},{4,12},{5,13},{6,14},{7,15},{8,0},{9,1},... | collective-permute-start | bytes 1179656 | tf_op jit(solution)/shard_map/ppermute | solution.py:214
  62.7 30.6 %copy-start.15 = (f32[4,96,256]{2,1,0:T(8,128)}, f32[4,96,256]{2,1,0:T(8,128)S(1)}, u32[]{:S(2)}) copy-start(f32[4,96,256]{2,1,0:T(8,128)S(1)} %collective-permute-done.6.refs_1_) | copy-start | bytes 1179652
  62.7 11.9 %collective-permute-start.10 = (f32[4,96,256]{2,1,0:T(8,128)S(1)}, f32[4,96,256]{2,1,0:T(8,128)S(1)}, u32[]{:S(2)}, u32[]{:S(2)}) collective-permute-start(f32[4,96,256]{2,1,0:T(8,128)S(1)} %collective-permute-done.6.refs_1_), channel_id=1, source_target_pairs={{0,16},{1,17},{2,18},{3,19},{4,20},{5,21},{6,22},{7,23},{8,24},{9,... | collective-permute-start | bytes 1179656 | tf_op jit(solution)/shard_map/ppermute | solution.py:214
  63.2 30.1 %copy-start.12 = (f32[4,96,256]{2,1,0:T(8,128)}, f32[4,96,256]{2,1,0:T(8,128)S(1)}, u32[]{:S(2)}) copy-start(f32[4,96,256]{2,1,0:T(8,128)S(1)} %collective-permute-done.7.refs_2_) | copy-start | bytes 1179652
  63.2 18.5 %collective-permute-start.8 = (f32[4,96,256]{2,1,0:T(8,128)S(1)}, f32[4,96,256]{2,1,0:T(8,128)S(1)}, u32[]{:S(2)}, u32[]{:S(2)}) collective-permute-start(f32[4,96,256]{2,1,0:T(8,128)S(1)} %collective-permute-done.6.refs_1_), channel_id=1, source_target_pairs={{0,8},{1,9},{2,10},{3,11},{4,12},{5,13},{6,14},{7,15},{8,0},{9,1},... | collective-permute-start | bytes 1179656 | tf_op jit(solution)/shard_map/ppermute | solution.py:214
  64.5 18.7 %collective-permute-start.11 = (f32[4,96,256]{2,1,0:T(8,128)S(1)}, f32[4,96,256]{2,1,0:T(8,128)S(1)}, u32[]{:S(2)}, u32[]{:S(2)}) collective-permute-start(f32[4,96,256]{2,1,0:T(8,128)S(1)} %collective-permute-done.7.refs_2_), channel_id=1, source_target_pairs={{0,16},{1,17},{2,18},{3,19},{4,20},{5,21},{6,22},{7,23},{8,24},{9,... | collective-permute-start | bytes 1179656 | tf_op jit(solution)/shard_map/ppermute | solution.py:214
  65.3 32.6 %copy-start.14 = (f32[4,96,256]{2,1,0:T(8,128)}, f32[4,96,256]{2,1,0:T(8,128)S(1)}, u32[]{:S(2)}) copy-start(f32[4,96,256]{2,1,0:T(8,128)S(1)} %collective-permute-done.29.refs_1_) | copy-start | bytes 1179652
  65.3 26.2 %collective-permute-start.33 = (f32[4,96,256]{2,1,0:T(8,128)S(1)}, f32[4,96,256]{2,1,0:T(8,128)S(1)}, u32[]{:S(2)}, u32[]{:S(2)}) collective-permute-start(f32[4,96,256]{2,1,0:T(8,128)S(1)} %collective-permute-done.29.refs_1_), channel_id=1, source_target_pairs={{0,16},{1,17},{2,18},{3,19},{4,20},{5,21},{6,22},{7,23},{8,24},{9,... | collective-permute-start | bytes 1179656 | tf_op jit(solution)/shard_map/ppermute | solution.py:214
  73.3 26.6 %collective-permute-start.32 = (f32[4,96,256]{2,1,0:T(8,128)}, f32[4,96,256]{2,1,0:T(8,128)S(1)}, u32[]{:S(2)}, u32[]{:S(2)}) collective-permute-start(f32[4,96,256]{2,1,0:T(8,128)} %get-tuple-element.74.refs_0_), channel_id=1, source_target_pairs={{0,16},{1,17},{2,18},{3,19},{4,20},{5,21},{6,22},{7,23},{8,24},{9,... | collective-permute-start | bytes 1179656 | tf_op jit(solution)/shard_map/ppermute | solution.py:214
  74.7 18.7 %collective-permute-start.12 = (f32[4,96,256]{2,1,0:T(8,128)S(1)}, f32[4,96,256]{2,1,0:T(8,128)}, u32[]{:S(2)}, u32[]{:S(2)}) collective-permute-start(f32[4,96,256]{2,1,0:T(8,128)S(1)} %collective-permute-done.10.refs_5_), channel_id=1, source_target_pairs={{0,8},{1,9},{2,10},{3,11},{4,12},{5,13},{6,14},{7,15},{8,0},{9,1},... | collective-permute-start | bytes 1179656 | tf_op jit(solution)/shard_map/ppermute | solution.py:214
  81.8 18.2 %collective-permute-start.31 = (f32[4,96,256]{2,1,0:T(8,128)S(1)}, f32[4,96,256]{2,1,0:T(8,128)}, u32[]{:S(2)}, u32[]{:S(2)}) collective-permute-start(f32[4,96,256]{2,1,0:T(8,128)S(1)} %collective-permute-done.29.refs_1_), channel_id=1, source_target_pairs={{0,8},{1,9},{2,10},{3,11},{4,12},{5,13},{6,14},{7,15},{8,0},{9,1},... | collective-permute-start | bytes 1179656 | tf_op jit(solution)/shard_map/ppermute | solution.py:214
  83.3 24.5 %collective-permute-start.34 = (f32[4,96,256]{2,1,0:T(8,128)S(1)}, f32[4,96,256]{2,1,0:T(8,128)}, u32[]{:S(2)}, u32[]{:S(2)}) collective-permute-start(f32[4,96,256]{2,1,0:T(8,128)S(1)} %collective-permute-done.30.refs_2_), channel_id=1, source_target_pairs={{0,16},{1,17},{2,18},{3,19},{4,20},{5,21},{6,22},{7,23},{8,24},{9,... | collective-permute-start | bytes 1179656 | tf_op jit(solution)/shard_map/ppermute | solution.py:214
  91.5 16.3 %collective-permute-start.35 = (f32[4,96,256]{2,1,0:T(8,128)S(1)}, f32[4,96,256]{2,1,0:T(8,128)}, u32[]{:S(2)}, u32[]{:S(2)}) collective-permute-start(f32[4,96,256]{2,1,0:T(8,128)S(1)} %collective-permute-done.33.refs_5_), channel_id=1, source_target_pairs={{0,8},{1,9},{2,10},{3,11},{4,12},{5,13},{6,14},{7,15},{8,0},{9,1},... | collective-permute-start | bytes 1179656 | tf_op jit(solution)/shard_map/ppermute | solution.py:214
  128.6 45.1 %collective-permute-start.39 = (f32[2,24,32,256]{3,2,1,0:T(8,128)}, f32[2,24,32,256]{3,2,1,0:T(8,128)S(1)}, u32[]{:S(2)}, u32[]{:S(2)}) collective-permute-start(f32[2,24,32,256]{3,2,1,0:T(8,128)} %get-tuple-element.85), channel_id=1, source_target_pairs={{0,1},{1,0},{2,3},{3,2},{4,5},{5,4},{6,7},{7,6},{8,9},{9,8},{10,11... | collective-permute-start | bytes 4718600 | tf_op jit(solution)/shard_map/ppermute | solution.py:214
  143.4 49.3 %collective-permute-start.16 = (f32[2,12,32,256]{3,2,1,0:T(8,128)}, f32[2,12,32,256]{3,2,1,0:T(8,128)S(1)}, u32[]{:S(2)}, u32[]{:S(2)}) collective-permute-start(f32[2,12,32,256]{3,2,1,0:T(8,128)} %get-tuple-element.65), channel_id=1, source_target_pairs={{0,1},{1,0},{2,3},{3,2},{4,5},{5,4},{6,7},{7,6},{8,9},{9,8},{10,11... | collective-permute-start | bytes 2359304 | tf_op jit(solution)/shard_map/ppermute | solution.py:214
  156.7 57.6 %collective-permute-start.15 = (f32[2,12,32,256]{3,2,1,0:T(8,128)}, f32[2,12,32,256]{3,2,1,0:T(8,128)}, u32[]{:S(2)}, u32[]{:S(2)}) collective-permute-start(f32[2,12,32,256]{3,2,1,0:T(8,128)} %get-tuple-element.63), channel_id=1, source_target_pairs={{0,1},{1,0},{2,3},{3,2},{4,5},{5,4},{6,7},{7,6},{8,9},{9,8},{10,11... | collective-permute-start | bytes 2359304 | tf_op jit(solution)/shard_map/ppermute | solution.py:214
  173.3 37.0 %collective-permute-start.38 = (f32[2,24,32,256]{3,2,1,0:T(8,128)}, f32[2,24,32,256]{3,2,1,0:T(8,128)S(1)}, u32[]{:S(2)}, u32[]{:S(2)}) collective-permute-start(f32[2,24,32,256]{3,2,1,0:T(8,128)} %get-tuple-element.83), channel_id=1, source_target_pairs={{0,1},{1,0},{2,3},{3,2},{4,5},{5,4},{6,7},{7,6},{8,9},{9,8},{10,11... | collective-permute-start | bytes 4718600 | tf_op jit(solution)/shard_map/ppermute | solution.py:214
  174.0 37.7 %collective-permute-start.43 = (f32[24,32,256]{2,1,0:T(8,128)S(1)}, f32[24,32,256]{2,1,0:T(8,128)S(1)}, u32[]{:S(2)}, u32[]{:S(2)}) collective-permute-start(f32[24,32,256]{2,1,0:T(8,128)S(1)} %get-tuple-element.94), channel_id=1, source_target_pairs={{6,4},{7,5},{14,12},{15,13},{22,20},{23,21},{30,28},{31,29}} | collective-permute-start | bytes 2359304 | tf_op jit(solution)/shard_map/ppermute | solution.py:214
  174.7 38.3 %collective-permute-start.40 = (f32[24,32,256]{2,1,0:T(8,128)S(1)}, f32[24,32,256]{2,1,0:T(8,128)S(1)}, u32[]{:S(2)}, u32[]{:S(2)}) collective-permute-start(f32[24,32,256]{2,1,0:T(8,128)S(1)} %get-tuple-element.95), channel_id=1, source_target_pairs={{0,2},{1,3},{8,10},{9,11},{16,18},{17,19},{24,26},{25,27}} | collective-permute-start | bytes 2359304 | tf_op jit(solution)/shard_map/ppermute | solution.py:214
  193.6 51.6 %collective-permute-start.37 = (f32[2,24,32,256]{3,2,1,0:T(8,128)}, f32[2,24,32,256]{3,2,1,0:T(8,128)S(1)}, u32[]{:S(2)}, u32[]{:S(2)}) collective-permute-start(f32[2,24,32,256]{3,2,1,0:T(8,128)} %get-tuple-element.81), channel_id=1, source_target_pairs={{0,1},{1,0},{2,3},{3,2},{4,5},{5,4},{6,7},{7,6},{8,9},{9,8},{10,11... | collective-permute-start | bytes 4718600 | tf_op jit(solution)/shard_map/ppermute | solution.py:214
  210.3 18.4 %collective-permute-start.20 = (f32[12,32,256]{2,1,0:T(8,128)}, f32[12,32,256]{2,1,0:T(8,128)}, u32[]{:S(2)}, u32[]{:S(2)}) collective-permute-start(f32[12,32,256]{2,1,0:T(8,128)} %get-tuple-element.100), channel_id=1, source_target_pairs={{6,4},{7,5},{14,12},{15,13},{22,20},{23,21},{30,28},{31,29}} | collective-permute-start | bytes 1179656 | tf_op jit(solution)/shard_map/ppermute | solution.py:214
  211.7 17.3 %collective-permute-start.17 = (f32[12,32,256]{2,1,0:T(8,128)S(1)}, f32[12,32,256]{2,1,0:T(8,128)S(1)}, u32[]{:S(2)}, u32[]{:S(2)}) collective-permute-start(f32[12,32,256]{2,1,0:T(8,128)S(1)} %get-tuple-element.101), channel_id=1, source_target_pairs={{0,2},{1,3},{8,10},{9,11},{16,18},{17,19},{24,26},{25,27}} | collective-permute-start | bytes 1179656 | tf_op jit(solution)/shard_map/ppermute | solution.py:214
  213.6 31.7 %collective-permute-start.44 = (f32[24,32,256]{2,1,0:T(8,128)S(1)}, f32[24,32,256]{2,1,0:T(8,128)S(1)}, u32[]{:S(2)}, u32[]{:S(2)}) collective-permute-start(f32[24,32,256]{2,1,0:T(8,128)S(1)} %get-tuple-element.92), channel_id=1, source_target_pairs={{4,2},{5,3},{6,4},{7,5},{12,10},{13,11},{14,12},{15,13},{20,18},{2... | collective-permute-start | bytes 2359304 | tf_op jit(solution)/shard_map/ppermute | solution.py:214
  214.3 31.4 %collective-permute-start.41 = (f32[24,32,256]{2,1,0:T(8,128)S(1)}, f32[24,32,256]{2,1,0:T(8,128)S(1)}, u32[]{:S(2)}, u32[]{:S(2)}) collective-permute-start(f32[24,32,256]{2,1,0:T(8,128)S(1)} %get-tuple-element.93), channel_id=1, source_target_pairs={{0,2},{1,3},{2,4},{3,5},{8,10},{9,11},{10,12},{11,13},{16,18},{17,... | collective-permute-start | bytes 2359304 | tf_op jit(solution)/shard_map/ppermute | solution.py:214
  228.6 29.6 %collective-permute-start.14 = (f32[2,12,32,256]{3,2,1,0:T(8,128)}, f32[2,12,32,256]{3,2,1,0:T(8,128)}, u32[]{:S(2)}, u32[]{:S(2)}) collective-permute-start(f32[2,12,32,256]{3,2,1,0:T(8,128)} %get-tuple-element.61), channel_id=1, source_target_pairs={{0,1},{1,0},{2,3},{3,2},{4,5},{5,4},{6,7},{7,6},{8,9},{9,8},{10,11... | collective-permute-start | bytes 2359304 | tf_op jit(solution)/shard_map/ppermute | solution.py:214
  231.3 31.5 %collective-permute-start.21 = (f32[12,32,256]{2,1,0:T(8,128)}, f32[12,32,256]{2,1,0:T(8,128)}, u32[]{:S(2)}, u32[]{:S(2)}) collective-permute-start(f32[12,32,256]{2,1,0:T(8,128)} %get-tuple-element.98), channel_id=1, source_target_pairs={{4,2},{5,3},{6,4},{7,5},{12,10},{13,11},{14,12},{15,13},{20,18},{2... | collective-permute-start | bytes 1179656 | tf_op jit(solution)/shard_map/ppermute | solution.py:214
  245.2 30.0 %collective-permute-start.13 = (f32[1,12,32,256]{3,2,1,0:T(8,128)}, f32[1,12,32,256]{3,2,1,0:T(8,128)S(1)}, u32[]{:S(2)}, u32[]{:S(2)}) collective-permute-start(f32[1,12,32,256]{3,2,1,0:T(8,128)} %get-tuple-element.59), channel_id=1, source_target_pairs={{0,1},{1,0},{2,3},{3,2},{4,5},{5,4},{6,7},{7,6},{8,9},{9,8},{10,11... | collective-permute-start | bytes 1179656 | tf_op jit(solution)/shard_map/ppermute | solution.py:214
  245.3 31.4 %collective-permute-start.36 = (f32[1,24,32,256]{3,2,1,0:T(8,128)}, f32[1,24,32,256]{3,2,1,0:T(8,128)S(1)}, u32[]{:S(2)}, u32[]{:S(2)}) collective-permute-start(f32[1,24,32,256]{3,2,1,0:T(8,128)} %get-tuple-element.79), channel_id=1, source_target_pairs={{0,1},{1,0},{2,3},{3,2},{4,5},{5,4},{6,7},{7,6},{8,9},{9,8},{10,11... | collective-permute-start | bytes 2359304 | tf_op jit(solution)/shard_map/ppermute | solution.py:214
  245.7 21.8 %collective-permute-start.18 = (f32[12,32,256]{2,1,0:T(8,128)}, f32[12,32,256]{2,1,0:T(8,128)S(1)}, u32[]{:S(2)}, u32[]{:S(2)}) collective-permute-start(f32[12,32,256]{2,1,0:T(8,128)} %get-tuple-element.99), channel_id=1, source_target_pairs={{0,2},{1,3},{2,4},{3,5},{8,10},{9,11},{10,12},{11,13},{16,18},{17,... | collective-permute-start | bytes 1179656 | tf_op jit(solution)/shard_map/ppermute | solution.py:214
  258.3 34.1 %collective-permute-start.42 = (f32[24,32,256]{2,1,0:T(8,128)S(1)}, f32[24,32,256]{2,1,0:T(8,128)S(1)}, u32[]{:S(2)}, u32[]{:S(2)}) collective-permute-start(f32[24,32,256]{2,1,0:T(8,128)S(1)} %get-tuple-element.91), channel_id=1, source_target_pairs={{0,2},{1,3},{2,4},{3,5},{4,6},{5,7},{8,10},{9,11},{10,12},{11,13},... | collective-permute-start | bytes 2359304 | tf_op jit(solution)/shard_map/ppermute | solution.py:214
  262.8 29.5 %collective-permute-start.45 = (f32[24,32,256]{2,1,0:T(8,128)S(1)}, f32[24,32,256]{2,1,0:T(8,128)}, u32[]{:S(2)}, u32[]{:S(2)}) collective-permute-start(f32[24,32,256]{2,1,0:T(8,128)S(1)} %get-tuple-element.90), channel_id=1, source_target_pairs={{2,0},{3,1},{4,2},{5,3},{6,4},{7,5},{10,8},{11,9},{12,10},{13,11},... | collective-permute-start | bytes 2359304 | tf_op jit(solution)/shard_map/ppermute | solution.py:214
  269.9 22.4 %collective-permute-start.19 = (f32[12,32,256]{2,1,0:T(8,128)}, f32[12,32,256]{2,1,0:T(8,128)}, u32[]{:S(2)}, u32[]{:S(2)}) collective-permute-start(f32[12,32,256]{2,1,0:T(8,128)} %get-tuple-element.97), channel_id=1, source_target_pairs={{0,2},{1,3},{2,4},{3,5},{4,6},{5,7},{8,10},{9,11},{10,12},{11,13},... | collective-permute-start | bytes 1179656 | tf_op jit(solution)/shard_map/ppermute | solution.py:214
  275.2 17.2 %collective-permute-start.22 = (f32[12,32,256]{2,1,0:T(8,128)}, f32[12,32,256]{2,1,0:T(8,128)}, u32[]{:S(2)}, u32[]{:S(2)}) collective-permute-start(f32[12,32,256]{2,1,0:T(8,128)} %get-tuple-element.96), channel_id=1, source_target_pairs={{2,0},{3,1},{4,2},{5,3},{6,4},{7,5},{10,8},{11,9},{12,10},{13,11},... | collective-permute-start | bytes 1179656 | tf_op jit(solution)/shard_map/ppermute | solution.py:214
  300.5 2.0 collective-permute-start.46
  303.6 7.4 %collective-permute-start.49 = (f32[128,256]{1,0:T(8,128)S(1)}, f32[128,256]{1,0:T(8,128)S(1)}, u32[]{:S(2)}, u32[]{:S(2)}) collective-permute-start(f32[128,256]{1,0:T(8,128)S(1)} %get-tuple-element.105), channel_id=1, source_target_pairs={{0,24},{1,25},{2,26},{3,27},{4,28},{5,29},{6,30},{7,31},{8,16},{9,... | collective-permute-start | bytes 393224 | tf_op jit(solution)/shard_map/ppermute | solution.py:214
  304.1 8.1 %collective-permute-start.48 = (f32[128,256]{1,0:T(8,128)S(1)}, f32[128,256]{1,0:T(8,128)S(1)}, u32[]{:S(2)}, u32[]{:S(2)}) collective-permute-start(f32[128,256]{1,0:T(8,128)S(1)} %get-tuple-element.106), channel_id=1, source_target_pairs={{0,16},{1,17},{2,18},{3,19},{4,20},{5,21},{6,22},{7,23},{8,24},{9,... | collective-permute-start | bytes 393224 | tf_op jit(solution)/shard_map/ppermute | solution.py:214
  305.7 6.5 %collective-permute-start.47 = (f32[128,256]{1,0:T(8,128)S(1)}, f32[128,256]{1,0:T(8,128)S(1)}, u32[]{:S(2)}, u32[]{:S(2)}) collective-permute-start(f32[128,256]{1,0:T(8,128)S(1)} %get-tuple-element.104), channel_id=1, source_target_pairs={{0,8},{1,9},{2,10},{3,11},{4,12},{5,13},{6,14},{7,15},{8,0},{9,1},... | collective-permute-start | bytes 393224 | tf_op jit(solution)/shard_map/ppermute | solution.py:214
  312.2 6.3 %collective-permute-start.52 = (f32[32,256]{1,0:T(8,128)S(1)}, f32[32,256]{1,0:T(8,128)S(1)}, u32[]{:S(2)}, u32[]{:S(2)}) collective-permute-start(f32[32,256]{1,0:T(8,128)S(1)} %get-tuple-element.108), channel_id=1, source_target_pairs={{0,6},{1,7},{2,0},{3,1},{4,2},{5,3},{6,4},{7,5},{8,14},{9,15},{10,... | collective-permute-start | bytes 98312 | tf_op jit(solution)/shard_map/ppermute | solution.py:214
  312.3 6.8 %collective-permute-start.51 = (f32[32,256]{1,0:T(8,128)S(1)}, f32[32,256]{1,0:T(8,128)S(1)}, u32[]{:S(2)}, u32[]{:S(2)}) collective-permute-start(f32[32,256]{1,0:T(8,128)S(1)} %get-tuple-element.109), channel_id=1, source_target_pairs={{0,4},{1,5},{2,6},{3,7},{4,0},{5,1},{6,2},{7,3},{8,12},{9,13},{10,... | collective-permute-start | bytes 98312 | tf_op jit(solution)/shard_map/ppermute | solution.py:214
  316.6 5.7 %collective-permute-start.50 = (f32[32,256]{1,0:T(8,128)S(1)}, f32[32,256]{1,0:T(8,128)S(1)}, u32[]{:S(2)}, u32[]{:S(2)}) collective-permute-start(f32[32,256]{1,0:T(8,128)S(1)} %get-tuple-element.107), channel_id=1, source_target_pairs={{0,2},{1,3},{2,4},{3,5},{4,6},{5,7},{6,0},{7,1},{8,10},{9,11},{10,... | collective-permute-start | bytes 98312 | tf_op jit(solution)/shard_map/ppermute | solution.py:214
  322.3 5.8 %collective-permute-start.53 = (f32[32,256]{1,0:T(8,128)S(1)}, f32[32,256]{1,0:T(8,128)S(1)}, u32[]{:S(2)}, u32[]{:S(2)}) collective-permute-start(f32[32,256]{1,0:T(8,128)S(1)} %get-tuple-element.89), channel_id=1, source_target_pairs={{0,2},{1,3},{2,4},{3,5},{4,6},{5,7},{6,0},{7,1},{8,10},{9,11},{10,... | collective-permute-start | bytes 98312 | tf_op jit(solution)/shard_map/ppermute | solution.py:214
  322.5 5.6 %collective-permute-start.54 = (f32[32,256]{1,0:T(8,128)S(1)}, f32[32,256]{1,0:T(8,128)S(1)}, u32[]{:S(2)}, u32[]{:S(2)}) collective-permute-start(f32[32,256]{1,0:T(8,128)S(1)} %get-tuple-element.89), channel_id=1, source_target_pairs={{0,4},{1,5},{2,6},{3,7},{4,0},{5,1},{6,2},{7,3},{8,12},{9,13},{10,... | collective-permute-start | bytes 98312 | tf_op jit(solution)/shard_map/ppermute | solution.py:214
  323.4 5.2 %collective-permute-start.55 = (f32[32,256]{1,0:T(8,128)S(1)}, f32[32,256]{1,0:T(8,128)S(1)}, u32[]{:S(2)}, u32[]{:S(2)}) collective-permute-start(f32[32,256]{1,0:T(8,128)S(1)} %get-tuple-element.89), channel_id=1, source_target_pairs={{0,6},{1,7},{2,0},{3,1},{4,2},{5,3},{6,4},{7,5},{8,14},{9,15},{10,... | collective-permute-start | bytes 98312 | tf_op jit(solution)/shard_map/ppermute | solution.py:214
  328.7 5.0 %collective-permute-start.56 = (f32[128,256]{1,0:T(8,128)S(1)}, f32[128,256]{1,0:T(8,128)S(1)}, u32[]{:S(2)}, u32[]{:S(2)}) collective-permute-start(f32[128,256]{1,0:T(8,128)S(1)} %bitcast.124), channel_id=1, source_target_pairs={{0,8},{1,9},{2,10},{3,11},{4,12},{5,13},{6,14},{7,15},{8,0},{9,1},... | collective-permute-start | bytes 393224 | tf_op jit(solution)/shard_map/ppermute | solution.py:214
  330.0 5.0 %collective-permute-start.57 = (f32[128,256]{1,0:T(8,128)S(1)}, f32[128,256]{1,0:T(8,128)S(1)}, u32[]{:S(2)}, u32[]{:S(2)}) collective-permute-start(f32[128,256]{1,0:T(8,128)S(1)} %bitcast.125), channel_id=1, source_target_pairs={{0,16},{1,17},{2,18},{3,19},{4,20},{5,21},{6,22},{7,23},{8,24},{9,... | collective-permute-start | bytes 393224 | tf_op jit(solution)/shard_map/ppermute | solution.py:214
  330.5 5.9 %collective-permute-start.58 = (f32[128,256]{1,0:T(8,128)S(1)}, f32[128,256]{1,0:T(8,128)S(1)}, u32[]{:S(2)}, u32[]{:S(2)}) collective-permute-start(f32[128,256]{1,0:T(8,128)S(1)} %bitcast.126), channel_id=1, source_target_pairs={{0,24},{1,25},{2,26},{3,27},{4,28},{5,29},{6,30},{7,31},{8,16},{9,... | collective-permute-start | bytes 393224 | tf_op jit(solution)/shard_map/ppermute | solution.py:214
  336.4 2.0 collective-permute-start.59
  (31 other events, 279.0 us)

commit v2 on v1

v2 whole, which is shorter than its diff:
```python
import functools
import math
import jax
import jax.numpy as jnp
from jax import lax
from jax.experimental import pallas as pl
from jax.experimental.pallas import tpu as pltpu
from jax.sharding import PartitionSpec as P

AXES = ("prow", "pcol")
HIGHEST = lax.Precision.HIGHEST
VMEM_LIMIT = 56 * 1024 * 1024


def whole(memory_space=pltpu.VMEM):
    return pl.BlockSpec(memory_space=memory_space)


def call(kernel, outs, scratch=(), n_scalar=1, n_in=1, n_after=0, flops=0, moved=0):
    used = n_scalar + n_in

    def body(*refs):
        kernel(*refs[:used], *refs[used + n_after :])

    return pl.pallas_call(
        body,
        out_shape=outs,
        in_specs=[whole(pltpu.SMEM)] * n_scalar + [whole()] * n_in + [whole(pl.ANY)] * n_after,
        out_specs=jax.tree.map(lambda _: whole(), outs),
        scratch_shapes=list(scratch),
        compiler_params=pltpu.CompilerParams(vmem_limit_bytes=VMEM_LIMIT),
        cost_estimate=pl.CostEstimate(flops=flops, bytes_accessed=moved, transcendentals=0),
    )


def valid_slots(block_lists, list_mask, slot_of_block):
    window_blocks = block_lists.shape[1]
    block_ids = jnp.arange(window_blocks, dtype=jnp.int32)
    chosen = (block_lists[:, :, None] == block_ids[None, None, :]).astype(jnp.int32)
    slot_ids = jnp.sum(chosen * slot_of_block[None, None, :], axis=2)
    matches = (slot_ids[:, :, None] == block_ids[None, None, :]).astype(jnp.int32)
    return jnp.sum(matches * list_mask[:, :, None], axis=1)


def normalize_kernel(group, lines, place, valid, f_ref, partner_ref, inv_ref, n_ref, *rest):
    slots, rb, width = f_ref.shape[1:]
    halves = slots // 2
    outs, scratch = rest[:lines], rest[lines]
    r, h = place[0], place[2]
    rows = halves * rb

    def times(block, p):
        return jnp.dot(block, inv_ref[p], precision=HIGHEST, preferred_element_type=jnp.float32)

    for at, p in enumerate(group):
        block = times(f_ref[p].reshape(slots * rb, width), p)
        for s in range(slots):
            one = block[s * rb : (s + 1) * rb]
            n_ref[at, s] = jnp.where(valid[p * slots + s] > 0, one, 0.0)
        block = times(partner_ref[p].reshape(rows, width), p)
        for t in range(halves):
            one = block[t * rb : (t + 1) * rb]
            row = at * rows + t * rb
            used = valid[p * slots + h * halves + t] > 0
            scratch[1 - h, row : row + rb] = jnp.where(used, one, 0.0)
            scratch[h, row : row + rb] = n_ref[at, h * halves + t]
    n = len(group) * rows // lines
    for d in range(lines):
        start = pl.multiple_of((r ^ d) * n, 8)
        outs[d][...] = scratch[:, pl.ds(start, n), :]


def to_planes_kernel(lines, place, *refs):
    r, z = place[0], place[1]
    for m in range(lines):
        which = r ^ ((z + m) % lines)
        for d in range(lines):

            @pl.when(which == d)
            def _(m=m, d=d):
                refs[lines + m][...] = refs[d][...]


def stack_kernel(place, *refs):
    for m in range(len(refs) - 1):
        refs[-1][:, m] = refs[m][...]


def assemble_kernel(lines, rb, place, *refs):
    pieces, (hi_ref, lo_ref, held) = refs[:-3], refs[-3:]
    r, z = place[0], place[1]
    n, width = pieces[0].shape[2:]
    step = math.gcd(n, rb)
    for d in range(lines):
        line = r ^ d
        for core in range(2):
            if len(pieces) > lines and d == lines - 1:
                piece, at = pieces[d + core], 0
            else:
                piece, at = pieces[d], core
            for m in range(lines):
                plane = (z + lines - m) % lines
                for i in range(n // step):
                    flat = line * n + i * step
                    row = (flat // rb) * width + (plane * 2 + core) * rb + flat % rb
                    row = pl.multiple_of(row, 8)
                    held[pl.ds(row, step), :] = piece[at, m, i * step : (i + 1) * step, :]
    panels, depth, _ = hi_ref.shape

    @pl.loop(0, panels * depth // width)
    def _(i):
        row = pl.multiple_of(i * width, width)
        value = held[pl.ds(row, width), :]
        hi = value.astype(jnp.bfloat16)
        p = row // depth
        at = pl.multiple_of(row % depth, width)
        hi_ref[p, pl.ds(at, width), :] = hi
        lo_ref[p, pl.ds(at, width), :] = (value - hi.astype(jnp.float32)).astype(jnp.bfloat16)


def product_kernel(panel_ids, slots, rb, lo, hi, waits, info, where, g_ref, *refs):
    count = len(panel_ids)
    x_hi, x_lo = refs[:count], refs[count : 2 * count]
    mine, other, held, done = refs[2 * count + waits :]
    tile = pl.program_id(0)
    tile_slots, rows, depth = g_ref.shape
    size = hi - lo
    h = info[1]
    g = g_ref[...].reshape(tile_slots * rows, depth)
    g_hi = g.astype(jnp.bfloat16)
    g_lo = (g - g_hi.astype(jnp.float32)).astype(jnp.bfloat16)
    dot = functools.partial(jnp.dot, preferred_element_type=jnp.float32)
    for k, p in enumerate(panel_ids):
        value = dot(g_hi, x_hi[k][0]) + (dot(g_hi, x_lo[k][0]) + dot(g_lo, x_hi[k][0]))
        for s in range(tile_slots):
            at = where[p * slots + tile * tile_slots + s]
            at = jnp.where((at >= lo) & (at < hi), at - lo, size)
            for core in range(2):
                start = s * rows + core * rb
                held[(core + h) % 2, at] = value[start : start + rb]

    @pl.when(tile == pl.num_programs(0) - 1)
    def _():
        first = pltpu.make_async_copy(held.at[0, pl.ds(0, size)], mine, done.at[0])
        second = pltpu.make_async_copy(held.at[1, pl.ds(0, size)], other, done.at[1])
        first.start()
        second.start()
        first.wait()
        second.wait()


def product(g3, xs, panel_ids, lo, hi, rb, info, where, after):
    slots, width, depth = g3.shape
    columns = xs[0][0].shape[2]
    rows = 2 * rb
    tile_slots = math.gcd(slots, max(1, 256 // rows))
    x_specs = [
        pl.BlockSpec((1, depth, columns), functools.partial(lambda at, a, i, w: (at, 0, 0), at))
        for _, _, at in xs
    ]
    out = jax.ShapeDtypeStruct((hi - lo, rb, columns), jnp.float32)
    anywhere = pl.BlockSpec(memory_space=pl.ANY)
    return pl.pallas_call(
        functools.partial(product_kernel, panel_ids, slots, rb, lo, hi, len(after)),
        out_shape=(out, out),
        grid_spec=pltpu.PrefetchScalarGridSpec(
            num_scalar_prefetch=2,
            grid=(slots // tile_slots,),
            in_specs=[pl.BlockSpec((tile_slots, rows, depth), lambda tile, i, w: (tile, i[0], 0))]
            + x_specs + x_specs + [anywhere] * len(after),
            out_specs=(anywhere, anywhere),
            scratch_shapes=[
                pltpu.VMEM((2, hi - lo + 1, rb, columns), jnp.float32),
                pltpu.SemaphoreType.DMA((2,)),
            ],
        ),
        compiler_params=pltpu.CompilerParams(vmem_limit_bytes=VMEM_LIMIT),
        cost_estimate=pl.CostEstimate(
            flops=12 * slots * rows * depth * columns * len(xs),
            bytes_accessed=slots * rows * depth * 4, transcendentals=0,
        ),
    )(info, where, g3, *[x[0] for x in xs], *[x[1] for x in xs], *after)


def finish_kernel(parts, bounds, groups, where, *refs):
    n_refs, refs = refs[: len(groups)], refs[len(groups) :]
    ins = refs[: 4 * parts]
    panel_ref, diag_ref, total = refs[4 * parts :]
    panels, slots, rb, width = panel_ref.shape
    n_of = {p: n_refs[g][at] for g, group in enumerate(groups) for at, p in enumerate(group)}
    for k in range(parts):
        own, swapped, up, down = ins[4 * k : 4 * k + 4]
        total[bounds[k] : bounds[k + 1]] = (own[...] + swapped[...]) + (up[...] + down[...])
    for p in range(panels):
        for s in range(slots):
            at = where[p * slots + s]
            value = total[jnp.maximum(at, 0)]
            panel_ref[p, s] = jnp.where(at >= 0, -value, 0.0)
        diag_ref[p] = lax.dot_general(
            n_of[p].reshape(slots * rb, width),
            panel_ref[p].reshape(slots * rb, width),
            (((0,), (0,)), ((), ())),
            precision=HIGHEST,
            preferred_element_type=jnp.float32,
        )


def on_device(
    lines, inverse_matrix, factor_blocks, factor_inverse, diag_given, block_lists, list_mask, slot_of_block
):
    panels, slots, rb, width = factor_blocks.shape
    halves = inverse_matrix.shape[1] // width
    f32 = jnp.float32
    r = lax.axis_index("prow").astype(jnp.int32)
    col = lax.axis_index("pcol").astype(jnp.int32)
    z, h = col // 2, col % 2
    place = jnp.stack([r, z, h])

    def send(value, to):
        pairs = []
        for a in range(lines):
            for b in range(lines):
                for c in range(2):
                    target = to(a, b, c)
                    if target is not None:
                        ta, tb, tc = target
                        pairs.append(((a * lines + b) * 2 + c, (ta * lines + tb) * 2 + tc))
        return lax.ppermute(value, AXES, pairs)

    def swap(value):
        return send(value, lambda a, b, c: (a, b, 1 - c))

    def across(value, d):
        return send(value, lambda a, b, c: (a ^ d, b, c))

    def along(value, m):
        return send(value, lambda a, b, c: (a, (b + m) % lines, c))

    slot_valid = valid_slots(block_lists, list_mask, slot_of_block)
    row_valid = lax.dynamic_slice_in_dim(slot_valid, r * slots, slots, 1).reshape(panels * slots)
    order = jnp.arange(panels * slots, dtype=jnp.int32)
    before = jnp.sum(jnp.where(order[None, :] < order[:, None], row_valid[None, :], 0), axis=1)
    where = jnp.where(row_valid > 0, before, -1).astype(jnp.int32)

    keep = 3 * panels * slots // 4
    half = panels // 2
    groups = [tuple(range(half)), tuple(range(half, panels))]
    ends = [g[-1] + 1 for g in groups]
    bounds = [0] + [keep - slots * (panels - end) for end in ends]
    chunk_panels = [tuple(range(lo // slots, end)) for lo, end in zip(bounds, ends)]

    split, normalized, parts_of, planes, stacked, gathered = [], [], [], [], [], []

    def normalize(group, after):
        shape = (2, len(group) * halves * rb // lines, width)
        rows_made = jax.ShapeDtypeStruct((len(group), slots, rb, width), f32)
        made = call(
            functools.partial(normalize_kernel, group, lines),
            [rows_made] + [jax.ShapeDtypeStruct(shape, f32)] * lines,
            [pltpu.VMEM((2, len(group) * halves * rb, width), f32)],
            n_scalar=2, n_in=3, n_after=len(after),
            flops=6 * lines * math.prod(shape) * width, moved=8 * lines * math.prod(shape),
        )(place, row_valid, factor_blocks, partner, factor_inverse, *after)
        normalized.append(made[0])
        parts_of.append(made[1:])

    partner = swap(lax.dynamic_slice_in_dim(factor_blocks, (1 - h) * halves, halves, 1))
    spread = []
    gather_after = []
    for g, group in enumerate(groups):
        normalize(group, spread)
        parts = parts_of[g]
        moved = 8 * lines * math.prod(parts[0].shape)
        held = [parts[0]] + [across(parts[d], d) for d in range(1, lines)]
        outgoing = call(
            functools.partial(to_planes_kernel, lines),
            [jax.ShapeDtypeStruct(parts[0].shape, f32)] * lines, n_in=lines, moved=moved,
        )(place, *held)
        spread = [outgoing[0]]
        planes.append(outgoing)
    for g, group in enumerate(groups):
        outgoing = planes[g]
        shape = outgoing[0].shape
        held = [outgoing[0]] + [along(outgoing[m], m) for m in range(1, lines)]
        after = gather_after + ([planes[g + 1][0]] if g + 1 < len(groups) else [])
        [both] = call(
            stack_kernel, [jax.ShapeDtypeStruct((2, lines) + shape[1:], f32)], n_in=lines,
            n_after=len(after), moved=8 * lines * math.prod(shape),
        )(place, *held, *after)
        pieces = [both] + [across(both, d) for d in range(1, lines)]
        if lines == 4:
            pieces[3:] = [across(pieces[1][:1], 2), across(pieces[2][1:], 1)]
        gather_after = pieces[-2:]
        stacked.append(both)
        gathered.append(pieces)
    for g, group in enumerate(groups):
        pieces, after = gathered[g], stacked[g + 1 : g + 2]
        block = jax.ShapeDtypeStruct((len(group), halves * width, width), jnp.bfloat16)
        x_hi, x_lo = call(
            functools.partial(assemble_kernel, lines, rb),
            [block, block],
            [pltpu.VMEM((len(group) * halves * width, width), f32)],
            n_in=len(pieces), n_after=len(after), moved=8 * len(group) * halves * width * width,
        )(place, *pieces, *after)
        split += [(x_hi, x_lo, at) for at in range(len(group))]

    g3 = inverse_matrix.reshape(slots, width, halves * width)
    order = [
        sorted(
            (j for j in range(lines) if j != a),
            key=lambda j: (lines - 1 - j + a, 0) if j > a else (j + lines - 1 - a, 1),
        )
        + [a]
        for a in range(lines)
    ]

    def of_plane(values):
        return sum(jnp.where(z == a, jnp.int32(v), 0) for a, v in enumerate(values))

    def chosen(made, calls):
        kinds = sorted({c for c in calls if c is not None})
        value = made[kinds[-1]][0] + made[kinds[-1]][1]
        for c in kinds[:-1]:
            here = functools.reduce(jnp.logical_or, [z == a for a in range(lines) if calls[a] == c])
            value = jnp.where(here, made[c][0] + made[c][1], value)
        return value

    finals, after, arrived = [], [], []
    for k, ids in enumerate(chunk_panels):
        lo, hi = bounds[k], bounds[k + 1]
        xs = [split[p] for p in ids]
        made = []

        def compute(after):
            n = len(made)
            info = jnp.stack([of_plane([order[a][n] for a in range(lines)]), h])
            mine, other = product(g3, xs, ids, lo, hi, rb, info, where, after)
            made.append((mine, swap(other)))
            return [mine]

        compute(after)
        up = down = None
        for step in range(lines - 1):
            rises = [order[a].index(lines - 1 - step + a) if a <= step else None for a in range(lines)]
            sinks = [order[a].index(step - lines + 1 + a) if a >= lines - 1 - step else None for a in range(lines)]
            send_up, send_down = chosen(made, rises), chosen(made, sinks)
            if step:
                send_up, send_down = send_up + up, send_down + down
            up = send(send_up, lambda a, b, c: (a, b + 1, c) if b <= step else None)
            down = send(send_down, lambda a, b, c: (a, b - 1, c) if b >= lines - 1 - step else None)
            if step == 0:
                after = [send_up, send_down]
                for n in range(lines - 2):
                    after = compute(after + (arrived if n == 0 else []))
            elif step == 1:
                compute([send_up, send_down])
        after = [send_up, send_down, made[lines - 1][0]]
        arrived = [up, down]
        finals += [*made[lines - 1], up, down]

    panel_inverse, terms = call(
        functools.partial(finish_kernel, len(chunk_panels), bounds, groups),
        [
            jax.ShapeDtypeStruct(factor_blocks.shape, f32),
            jax.ShapeDtypeStruct(factor_inverse.shape, f32),
        ],
        [pltpu.VMEM((keep, rb, width), f32)],
        n_in=len(groups) + len(finals), flops=12 * factor_blocks.size * width, moved=20 * factor_blocks.size,
    )(where, *normalized, *finals)

    pick = lambda value, at: lax.dynamic_index_in_dim(value, at, 0, False)
    two = terms.reshape(2, half * width, width)
    total = pick(two, h) + swap(pick(two, 1 - h))
    parts = total.reshape(lines, -1, width)
    total = pick(parts, r)
    for piece in [across(pick(parts, r ^ d), d) for d in range(1, lines)]:
        total = total + piece
    parts = total.reshape(lines, -1, width)
    total = pick(parts, z)
    for piece in [along(pick(parts, (z + m) % lines), m) for m in range(1, lines)]:
        total = total + piece
    pieces = [total] + [along(total, m) for m in range(1, lines)]
    gathered = jnp.zeros((lines,) + total.shape, f32)
    for m in range(lines):
        gathered = lax.dynamic_update_index_in_dim(gathered, pieces[m], (z - m) % lines, 0)
    total = gathered.reshape(-1, width)
    pieces = [total] + [across(total, d) for d in range(1, lines)]
    gathered = jnp.zeros((lines,) + total.shape, f32)
    for d in range(lines):
        gathered = lax.dynamic_update_index_in_dim(gathered, pieces[d], r ^ d, 0)
    total = gathered.reshape(half, width, width)
    swapped = swap(total)
    summed = jnp.concatenate([jnp.where(h == 0, total, swapped), jnp.where(h == 0, swapped, total)], 0)
    return (panel_inverse, diag_given - summed)


def solution(mesh):
    lines = mesh.shape["prow"]
    if mesh.shape["pcol"] != 2 * lines:
        raise ValueError("mesh shape")
    placed = (P("prow", "pcol"), P(None, "prow", "pcol", None), P(), P(), P(), P(), P())
    return jax.shard_map(
        functools.partial(on_device, lines),
        mesh=mesh,
        in_specs=placed,
        out_specs=(P(None, "prow", "pcol", None), P()),
        check_vma=False,
    )
```

time: 340 us -> 307 us (0.903)
  Pallas kernels: 145 us -> 109 us
  starting transfers between devices: 85.4 us -> 78.6 us
  waiting for transfers between devices: 86.9 us -> 91.1 us
    pallas_call x8, Pallas kernels: 116 us -> 76.4 us  [product(): pl.pallas_call(functools.partial(product_kernel, panel_ids, slots, rb, lo...]
    ppermute x60 -> x55, starting transfers between devices: 85.4 us -> 78.6 us  [send(): return lax.ppermute(value, AXES, pairs)]
    ppermute x60 -> x55, waiting for transfers between devices: 86.9 us -> 91.1 us  [send(): return lax.ppermute(value, AXES, pairs)]
    pallas_call x6 -> x7, Pallas kernels: 19.8 us -> 23.6 us  [the longest x2 8.54 us: normalize(): call(functools.partial(normalize_kernel, group, lines), [rows_made] + [ja...]
    unnamed x70 -> x98, local copies, waits for them, and re-layouts: 4.82 us -> 7.18 us
  transfers between devices with their start and end apart: 60 -> 55, of which waited for: 22 -> 29; matrix products, arithmetic and copies ran while one was open for 3% -> 4% of each run, Pallas kernels for 33% -> 21%
where the time goes in v2:
time: 307 us; the launch traced here: 306 us
  Pallas kernels  109 us (36%)
  waiting for transfers between devices  91.1 us (30%)
  starting transfers between devices  78.6 us (26%)
  other arithmetic  15.1 us (5%)
  local copies, waits for them, and re-layouts  10.5 us (3%)
    ppermute x55, waiting for transfers between devices, send(): return lax.ppermute(value, AXES, pairs)  91.1 us
    ppermute x55, starting transfers between devices, send(): return lax.ppermute(value, AXES, pairs)  78.6 us
    pallas_call x8, Pallas kernels, product(): pl.pallas_call(functools.partial(product_kernel, panel_ids, slots, rb, lo...  76.4 us
    pallas_call x2, Pallas kernels, on_device(): call(functools.partial(assemble_kernel, lines, rb), [block, block], [pltp...  8.84 us
    pallas_call x2, Pallas kernels, normalize(): call(functools.partial(normalize_kernel, group, lines), [rows_made] + [ja...  8.54 us
    unnamed x98, local copies, waits for them, and re-layouts  7.18 us
  transfers between devices with their start and end apart: 55, of which 29 were waited for; matrix products, arithmetic and copies ran while one was open for 4% of the time, Pallas kernels for 21%

profile of v2, /device:TPU:0, one launch (start us, length us, event | category | flops | bytes accessed | tf_op | source)
XLA Modules:
  0.0 305.7 jit_solution(15888984164587804984)
XLA Ops:
  5.2 4.2 %shard_map.86 = (f32[2,12,32,256]{3,2,1,0:T(8,128)}, f32[2,96,256]{2,1,0:T(8,128)}, f32[2,96,256]{2,1,0:T(8,128)}, f32[2,96,256]{2,1,0:T(8,128)}, f32[2,96,256]{2,1,0:T(8,128)}) custom-call(s32[3]{0:T(128)} %pad_add_fusion.refs_0_, s32[48]{0:T(128)} %reshape.31.refs_1_, f32[4,12,32,256]{3,2,1,0:T(8,128)} %refs_2_.3, f32[4,6,32,256]{3,2,1,0:T(8,128)} %copy-done.2, ...), custom_call_target="tpu_custom_call" | custom-call | flops 301989888 | bytes 1572864 | tf_op jit(solution)/shard_map/pallas_call | solution.py:257
  9.4 2.9 collective-permute-start.1
  12.3 1.5 collective-permute-start.2
  13.8 4.4 %collective-permute-done.1.refs_2_ = f32[2,96,256]{2,1,0:T(8,128)S(1)} collective-permute-done((f32[2,96,256]{2,1,0:T(8,128)}, f32[2,96,256]{2,1,0:T(8,128)S(1)}, u32[]{:S(2)}, u32[]{:S(2)}) %collective-permute-start.1) | collective-permute-done | bytes 196640 | tf_op jit(solution)/shard_map/ppermute | solution.py:228
  18.2 5.2 %collective-permute-done.2.refs_3_ = f32[2,96,256]{2,1,0:T(8,128)S(1)} collective-permute-done((f32[2,96,256]{2,1,0:T(8,128)}, f32[2,96,256]{2,1,0:T(8,128)S(1)}, u32[]{:S(2)}, u32[]{:S(2)}) %collective-permute-start.2) | collective-permute-done | bytes 196640 | tf_op jit(solution)/shard_map/ppermute | solution.py:228
  24.1 2.3 shard_map.87
  26.4 4.3 %shard_map.88 = (f32[2,12,32,256]{3,2,1,0:T(8,128)}, f32[2,96,256]{2,1,0:T(8,128)}, f32[2,96,256]{2,1,0:T(8,128)}, f32[2,96,256]{2,1,0:T(8,128)}, f32[2,96,256]{2,1,0:T(8,128)}) custom-call(s32[3]{0:T(128)} %pad_add_fusion.refs_0_, s32[48]{0:T(128)} %reshape.31.refs_1_, f32[4,12,32,256]{3,2,1,0:T(8,128)} %refs_2_.3, f32[4,6,32,256]{3,2,1,0:T(8,128)} %copy-done.2, ...), custom_call_target="tpu_custom_call" | custom-call | flops 301989888 | bytes 1572864 | tf_op jit(solution)/shard_map/pallas_call | solution.py:257
  31.9 1.6 collective-permute-start.4
  34.4 1.4 collective-permute-start.9
  35.8 2.6 collective-permute-start.5
  38.4 3.8 %collective-permute-start.6 = (f32[2,96,256]{2,1,0:T(8,128)S(1)}, f32[2,96,256]{2,1,0:T(8,128)S(1)}, u32[]{:S(2)}, u32[]{:S(2)}) collective-permute-start(f32[2,96,256]{2,1,0:T(8,128)S(1)} %copy-done.46), channel_id=1, source_target_pairs={{0,6},{1,7},{2,0},{3,1},{4,2},{5,3},{6,4},{7,5},{8,14},{9,15},{10,... | collective-permute-start | bytes 589832 | tf_op jit(solution)/shard_map/ppermute | solution.py:228
  44.2 2.3 shard_map.89
  46.5 1.7 collective-permute-done.5.refs_3_
  48.9 2.2 shard_map.90.refs_1_
  51.9 1.3 collective-permute-start.11
  53.2 17.5 %collective-permute-done.10.refs_2_ = f32[2,4,96,256]{3,2,1,0:T(8,128)S(1)} collective-permute-done((f32[2,4,96,256]{3,2,1,0:T(8,128)}, f32[2,4,96,256]{3,2,1,0:T(8,128)S(1)}, u32[]{:S(2)}, u32[]{:S(2)}) %collective-permute-start.10) | collective-permute-done | bytes 786464 | tf_op jit(solution)/shard_map/ppermute | solution.py:228
  71.5 1.5 collective-permute-start.13
  73.7 4.8 %collective-permute-start.14 = (f32[2,96,256]{2,1,0:T(8,128)S(1)}, f32[2,96,256]{2,1,0:T(8,128)S(1)}, u32[]{:S(2)}, u32[]{:S(2)}) collective-permute-start(f32[2,96,256]{2,1,0:T(8,128)S(1)} %copy-done.45), channel_id=1, source_target_pairs={{0,2},{1,3},{2,4},{3,5},{4,6},{5,7},{6,0},{7,1},{8,10},{9,11},{10,... | collective-permute-start | bytes 589832 | tf_op jit(solution)/shard_map/ppermute | solution.py:228
  78.5 2.4 collective-permute-start.16
  81.5 2.4 collective-permute-done.14.refs_2_
  83.8 6.2 %collective-permute-done.15.refs_3_ = f32[2,96,256]{2,1,0:T(8,128)S(1)} collective-permute-done((f32[2,96,256]{2,1,0:T(8,128)S(1)}, f32[2,96,256]{2,1,0:T(8,128)S(1)}, u32[]{:S(2)}, u32[]{:S(2)}) %collective-permute-start.15) | collective-permute-done | bytes 196640 | tf_op jit(solution)/shard_map/ppermute | solution.py:228
  91.7 2.2 shard_map.91.refs_6_.refs_1_
  94.0 4.4 %shard_map.92 = (bf16[2,1536,256]{2,1,0:T(8,128)(2,1)}, bf16[2,1536,256]{2,1,0:T(8,128)(2,1)}) custom-call(s32[3]{0:T(128)} %pad_add_fusion.refs_0_, f32[2,4,96,256]{3,2,1,0:T(8,128)} %shard_map.90.refs_1_, f32[2,4,96,256]{3,2,1,0:T(8,128)} %copy-done.3, f32[2,4,96,256]{3,2,1,0:T(8,128)} %copy-done.4, f32[1,4,96,256]{3,2,1,0:T(8,128)} %copy-done.7, ...), custom_call_target="tpu_custom_call" | custom-call | bytes 6291456 | tf_op jit(solution)/shard_map/pallas_call | solution.py:299
  98.4 8.3 %shard_map.93 = (f32[12,32,256]{2,1,0:T(8,128)}, f32[12,32,256]{2,1,0:T(8,128)}) custom-call(s32[2]{0:T(128)} %get-tuple-element.100.info, s32[48]{0:T(128)} %compare_select_fusion.where.refs_0_, f32[12,256,1536]{2,1,0:T(8,128)} %bitcast.74, bf16[2,1536,256]{2,1,0:T(8,128)(2,1)} %get-tuple-element.60.refs_0_.refs_1_, ...), custom_call_target="tpu_custom_call" | custom-call | flops 7247757312 | bytes 4718592 | tf_op jit(solution)/shard_map/pallas_call | solution.py:163
  108.0 1.3 collective-permute-start.27
  110.0 1.8 add.217.refs_4_.refs_5_
  112.5 6.6 %collective-permute-start.19 = (f32[12,32,256]{2,1,0:T(8,128)}, f32[12,32,256]{2,1,0:T(8,128)S(1)}, u32[]{:S(2)}, u32[]{:S(2)}) collective-permute-start(f32[12,32,256]{2,1,0:T(8,128)} %add.217.refs_4_.refs_5_), channel_id=1, source_target_pairs={{0,2},{1,3},{8,10},{9,11},{16,18},{17,19},{24,26},{25,27}} | collective-permute-start | bytes 1179656 | tf_op jit(solution)/shard_map/ppermute | solution.py:228
  119.0 8.2 %shard_map.94 = (f32[12,32,256]{2,1,0:T(8,128)}, f32[12,32,256]{2,1,0:T(8,128)}) custom-call(s32[2]{0:T(128)} %pad_add_fusion.3.info, s32[48]{0:T(128)} %compare_select_fusion.where.refs_0_, f32[12,256,1536]{2,1,0:T(8,128)} %bitcast.75, bf16[2,1536,256]{2,1,0:T(8,128)(2,1)} %get-tuple-element.60.refs_0_.refs_1_, ...), custom_call_target="tpu_custom_call" | custom-call | flops 7247757312 | bytes 4718592 | tf_op jit(solution)/shard_map/pallas_call | solution.py:163
  127.3 8.3 %shard_map.96 = (f32[12,32,256]{2,1,0:T(8,128)}, f32[12,32,256]{2,1,0:T(8,128)}) custom-call(s32[2]{0:T(128)} %get-tuple-element.101.info, s32[48]{0:T(128)} %compare_select_fusion.where.refs_0_, f32[12,256,1536]{2,1,0:T(8,128)} %bitcast.76, bf16[2,1536,256]{2,1,0:T(8,128)(2,1)} %get-tuple-element.60.refs_0_.refs_1_, ...), custom_call_target="tpu_custom_call" | custom-call | flops 7247757312 | bytes 4718592 | tf_op jit(solution)/shard_map/pallas_call | solution.py:163
  138.1 2.1 collective-permute-start.23
  140.3 1.4 collective-permute-start.29
  142.5 8.2 %shard_map.95 = (f32[12,32,256]{2,1,0:T(8,128)}, f32[12,32,256]{2,1,0:T(8,128)}) custom-call(s32[2]{0:T(128)} %pad_add_fusion.1.info, s32[48]{0:T(128)} %compare_select_fusion.where.refs_0_, f32[12,256,1536]{2,1,0:T(8,128)} %bitcast.77, bf16[2,1536,256]{2,1,0:T(8,128)(2,1)} %get-tuple-element.60.refs_0_.refs_1_, ...), custom_call_target="tpu_custom_call" | custom-call | flops 7247757312 | bytes 4718592 | tf_op jit(solution)/shard_map/pallas_call | solution.py:163
  153.0 4.4 %shard_map.97 = (bf16[2,1536,256]{2,1,0:T(8,128)(2,1)}, bf16[2,1536,256]{2,1,0:T(8,128)(2,1)}) custom-call(s32[3]{0:T(128)} %pad_add_fusion.refs_0_, f32[2,4,96,256]{3,2,1,0:T(8,128)} %shard_map.91.refs_6_.refs_1_, f32[2,4,96,256]{3,2,1,0:T(8,128)} %copy-done.5, f32[2,4,96,256]{3,2,1,0:T(8,128)} %copy-done.6, f32[1,4,96,256]{3,2,1,0:T(8,128)} %copy-done.25, ...), custom_call_target="tpu_custom_call" | custom-call | bytes 6291456 | tf_op jit(solution)/shard_map/pallas_call | solution.py:299
  158.6 10.9 %shard_map.98 = (f32[24,32,256]{2,1,0:T(8,128)}, f32[24,32,256]{2,1,0:T(8,128)}) custom-call(s32[2]{0:T(128)} %get-tuple-element.100.info, s32[48]{0:T(128)} %compare_select_fusion.where.refs_0_, f32[12,256,1536]{2,1,0:T(8,128)} %bitcast.78, bf16[2,1536,256]{2,1,0:T(8,128)(2,1)} %get-tuple-element.60.refs_0_.refs_1_, ...), custom_call_target="tpu_custom_call" | custom-call | flops 10871635968 | bytes 4718592 | tf_op jit(solution)/shard_map/pallas_call | solution.py:163
  169.6 4.3 %collective-permute-start.24 = (f32[12,32,256]{2,1,0:T(8,128)S(1)}, f32[12,32,256]{2,1,0:T(8,128)S(1)}, u32[]{:S(2)}, u32[]{:S(2)}) collective-permute-start(f32[12,32,256]{2,1,0:T(8,128)S(1)} %copy-done.24), channel_id=1, source_target_pairs={{0,2},{1,3},{2,4},{3,5},{4,6},{5,7},{8,10},{9,11},{10,12},{11,13},... | collective-permute-start | bytes 1179656 | tf_op jit(solution)/shard_map/ppermute | solution.py:228
  175.2 2.1 add.229.refs_6_.refs_7_
  178.1 4.6 %collective-permute-start.33 = (f32[24,32,256]{2,1,0:T(8,128)}, f32[24,32,256]{2,1,0:T(8,128)S(1)}, u32[]{:S(2)}, u32[]{:S(2)}) collective-permute-start(f32[24,32,256]{2,1,0:T(8,128)} %add.229.refs_6_.refs_7_), channel_id=1, source_target_pairs={{0,2},{1,3},{8,10},{9,11},{16,18},{17,19},{24,26},{25,27}} | collective-permute-start | bytes 2359304 | tf_op jit(solution)/shard_map/ppermute | solution.py:228
  182.9 4.1 %collective-permute-done.26.refs_9_.refs_6_ = f32[12,32,256]{2,1,0:T(8,128)S(1)} collective-permute-done((f32[12,32,256]{2,1,0:T(8,128)S(1)}, f32[12,32,256]{2,1,0:T(8,128)S(1)}, u32[]{:S(2)}, u32[]{:S(2)}) %collective-permute-start.26) | collective-permute-done | bytes 393248 | tf_op jit(solution)/shard_map/ppermute | solution.py:228
  187.8 10.8 %shard_map.99 = (f32[24,32,256]{2,1,0:T(8,128)}, f32[24,32,256]{2,1,0:T(8,128)}) custom-call(s32[2]{0:T(128)} %pad_add_fusion.3.info, s32[48]{0:T(128)} %compare_select_fusion.where.refs_0_, f32[12,256,1536]{2,1,0:T(8,128)} %bitcast.79, bf16[2,1536,256]{2,1,0:T(8,128)(2,1)} %get-tuple-element.60.refs_0_.refs_1_, ...), custom_call_target="tpu_custom_call" | custom-call | flops 10871635968 | bytes 4718592 | tf_op jit(solution)/shard_map/pallas_call | solution.py:163
  198.7 10.9 %shard_map.101 = (f32[24,32,256]{2,1,0:T(8,128)}, f32[24,32,256]{2,1,0:T(8,128)}) custom-call(s32[2]{0:T(128)} %get-tuple-element.101.info, s32[48]{0:T(128)} %compare_select_fusion.where.refs_0_, f32[12,256,1536]{2,1,0:T(8,128)} %bitcast.80, bf16[2,1536,256]{2,1,0:T(8,128)(2,1)} %get-tuple-element.60.refs_0_.refs_1_, ...), custom_call_target="tpu_custom_call" | custom-call | flops 10871635968 | bytes 4718592 | tf_op jit(solution)/shard_map/pallas_call | solution.py:163
  210.2 1.6 select_add_fusion.1
  212.5 2.9 collective-permute-start.37
  215.5 10.8 %shard_map.100 = (f32[24,32,256]{2,1,0:T(8,128)}, f32[24,32,256]{2,1,0:T(8,128)}) custom-call(s32[2]{0:T(128)} %pad_add_fusion.1.info, s32[48]{0:T(128)} %compare_select_fusion.where.refs_0_, f32[12,256,1536]{2,1,0:T(8,128)} %bitcast.81, bf16[2,1536,256]{2,1,0:T(8,128)(2,1)} %get-tuple-element.60.refs_0_.refs_1_, ...), custom_call_target="tpu_custom_call" | custom-call | flops 10871635968 | bytes 4718592 | tf_op jit(solution)/shard_map/pallas_call | solution.py:163
  226.4 6.0 %collective-permute-done.37 = f32[24,32,256]{2,1,0:T(8,128)S(1)} collective-permute-done((f32[24,32,256]{2,1,0:T(8,128)S(1)}, f32[24,32,256]{2,1,0:T(8,128)S(1)}, u32[]{:S(2)}, u32[]{:S(2)}) %collective-permute-start.37) | collective-permute-done | bytes 786464 | tf_op jit(solution)/shard_map/ppermute | solution.py:228
  232.4 1.4 add_add_fusion
  233.8 4.4 %collective-permute-start.38 = (f32[24,32,256]{2,1,0:T(8,128)}, f32[24,32,256]{2,1,0:T(8,128)S(1)}, u32[]{:S(2)}, u32[]{:S(2)}) collective-permute-start(f32[24,32,256]{2,1,0:T(8,128)} %get-tuple-element.87), channel_id=1, source_target_pairs={{0,2},{1,3},{2,4},{3,5},{4,6},{5,7},{8,10},{9,11},{10,12},{11,13},... | collective-permute-start | bytes 2359304 | tf_op jit(solution)/shard_map/ppermute | solution.py:228
  238.2 1.5 collective-permute-start.40
  239.8 1.9 collective-permute-done.21.refs_4_
  241.7 12.9 %collective-permute-done.38.refs_9_ = f32[24,32,256]{2,1,0:T(8,128)S(1)} collective-permute-done((f32[24,32,256]{2,1,0:T(8,128)}, f32[24,32,256]{2,1,0:T(8,128)S(1)}, u32[]{:S(2)}, u32[]{:S(2)}) %collective-permute-start.38) | collective-permute-done | bytes 786464 | tf_op jit(solution)/shard_map/ppermute | solution.py:228
  254.6 4.1 %collective-permute-done.40.refs_10_ = f32[24,32,256]{2,1,0:T(8,128)S(1)} collective-permute-done((f32[24,32,256]{2,1,0:T(8,128)S(1)}, f32[24,32,256]{2,1,0:T(8,128)S(1)}, u32[]{:S(2)}, u32[]{:S(2)}) %collective-permute-start.40) | collective-permute-done | bytes 786464 | tf_op jit(solution)/shard_map/ppermute | solution.py:228
  259.6 6.1 %shard_map.102 = (f32[4,12,32,256]{3,2,1,0:T(8,128)}, f32[4,256,256]{2,1,0:T(8,128)}) custom-call(s32[48]{0:T(128)} %compare_select_fusion.where.refs_0_, f32[2,12,32,256]{3,2,1,0:T(8,128)} %get-tuple-element.42.refs_1_, f32[2,12,32,256]{3,2,1,0:T(8,128)} %get-tuple-element.48.refs_2_, f32[12,32,256]{2,1,0:T(8,128)} %get-tuple-element.66.refs_8_.refs_3_, ...), custom_call_target="tpu_custom_call" | custom-call | flops 1207959552 | bytes 7864320 | tf_op jit(solution)/shard_map/pallas_call | solution.py:361
  266.9 1.9 collective-permute-done.41
  269.9 1.4 collective-permute-start.44
  273.5 3.8 %collective-permute-done.44 = f32[128,256]{1,0:T(8,128)S(1)} collective-permute-done((f32[128,256]{1,0:T(8,128)S(1)}, f32[128,256]{1,0:T(8,128)S(1)}, u32[]{:S(2)}, u32[]{:S(2)}) %collective-permute-start.44) | collective-permute-done | bytes 131104 | tf_op jit(solution)/shard_map/ppermute | solution.py:228
  277.3 2.0 collective-permute-done.43
  279.8 2.8 collective-permute-start.46
  283.3 1.9 collective-permute-done.46
  285.1 3.1 %collective-permute-done.45 = f32[32,256]{1,0:T(8,128)S(1)} collective-permute-done((f32[32,256]{1,0:T(8,128)S(1)}, f32[32,256]{1,0:T(8,128)S(1)}, u32[]{:S(2)}, u32[]{:S(2)}) %collective-permute-start.45) | collective-permute-done | bytes 32800 | tf_op jit(solution)/shard_map/ppermute | solution.py:228
  288.6 3.6 %collective-permute-start.50 = (f32[32,256]{1,0:T(8,128)S(1)}, f32[32,256]{1,0:T(8,128)S(1)}, u32[]{:S(2)}, u32[]{:S(2)}) collective-permute-start(f32[32,256]{1,0:T(8,128)S(1)} %get-tuple-element.83), channel_id=1, source_target_pairs={{0,6},{1,7},{2,0},{3,1},{4,2},{5,3},{6,4},{7,5},{8,14},{9,15},{10,... | collective-permute-start | bytes 98312 | tf_op jit(solution)/shard_map/ppermute | solution.py:228
  292.2 1.9 collective-permute-done.48
  296.6 1.5 collective-permute-start.53
  298.2 1.4 collective-permute-done.51
  300.5 2.0 collective-permute-done.53
  302.6 1.9 collective-permute-done.54
  (199 shorter events, 40.0 us)
Async XLA Ops:
  1.9 2.4 collective-permute-start
  9.4 8.8 %collective-permute-start.1 = (f32[2,96,256]{2,1,0:T(8,128)}, f32[2,96,256]{2,1,0:T(8,128)S(1)}, u32[]{:S(2)}, u32[]{:S(2)}) collective-permute-start(f32[2,96,256]{2,1,0:T(8,128)} %get-tuple-element.44), channel_id=1, source_target_pairs={{0,8},{1,9},{2,10},{3,11},{4,12},{5,13},{6,14},{7,15},{8,0},{9,1},... | collective-permute-start | bytes 589832 | tf_op jit(solution)/shard_map/ppermute | solution.py:228
  12.3 11.1 %collective-permute-start.2 = (f32[2,96,256]{2,1,0:T(8,128)}, f32[2,96,256]{2,1,0:T(8,128)S(1)}, u32[]{:S(2)}, u32[]{:S(2)}) collective-permute-start(f32[2,96,256]{2,1,0:T(8,128)} %get-tuple-element.45), channel_id=1, source_target_pairs={{0,16},{1,17},{2,18},{3,19},{4,20},{5,21},{6,22},{7,23},{8,24},{9,... | collective-permute-start | bytes 589832 | tf_op jit(solution)/shard_map/ppermute | solution.py:228
  13.8 9.6 %collective-permute-start.3 = (f32[2,96,256]{2,1,0:T(8,128)}, f32[2,96,256]{2,1,0:T(8,128)S(1)}, u32[]{:S(2)}, u32[]{:S(2)}) collective-permute-start(f32[2,96,256]{2,1,0:T(8,128)} %get-tuple-element.46), channel_id=1, source_target_pairs={{0,24},{1,25},{2,26},{3,27},{4,28},{5,29},{6,30},{7,31},{8,16},{9,... | collective-permute-start | bytes 589832 | tf_op jit(solution)/shard_map/ppermute | solution.py:228
  30.7 7.7 %collective-permute-start.7 = (f32[2,96,256]{2,1,0:T(8,128)}, f32[2,96,256]{2,1,0:T(8,128)S(1)}, u32[]{:S(2)}, u32[]{:S(2)}) collective-permute-start(f32[2,96,256]{2,1,0:T(8,128)} %get-tuple-element.53), channel_id=1, source_target_pairs={{0,8},{1,9},{2,10},{3,11},{4,12},{5,13},{6,14},{7,15},{8,0},{9,1},... | collective-permute-start | bytes 589832 | tf_op jit(solution)/shard_map/ppermute | solution.py:228
  31.9 14.6 %collective-permute-start.4 = (f32[2,96,256]{2,1,0:T(8,128)S(1)}, f32[2,96,256]{2,1,0:T(8,128)S(1)}, u32[]{:S(2)}, u32[]{:S(2)}) collective-permute-start(f32[2,96,256]{2,1,0:T(8,128)S(1)} %copy-done.48), channel_id=1, source_target_pairs={{0,2},{1,3},{2,4},{3,5},{4,6},{5,7},{6,0},{7,1},{8,10},{9,11},{10,... | collective-permute-start | bytes 589832 | tf_op jit(solution)/shard_map/ppermute | solution.py:228
  33.5 10.0 %collective-permute-start.8 = (f32[2,96,256]{2,1,0:T(8,128)}, f32[2,96,256]{2,1,0:T(8,128)S(1)}, u32[]{:S(2)}, u32[]{:S(2)}) collective-permute-start(f32[2,96,256]{2,1,0:T(8,128)} %get-tuple-element.54), channel_id=1, source_target_pairs={{0,16},{1,17},{2,18},{3,19},{4,20},{5,21},{6,22},{7,23},{8,24},{9,... | collective-permute-start | bytes 589832 | tf_op jit(solution)/shard_map/ppermute | solution.py:228
  34.4 9.1 %collective-permute-start.9 = (f32[2,96,256]{2,1,0:T(8,128)}, f32[2,96,256]{2,1,0:T(8,128)S(1)}, u32[]{:S(2)}, u32[]{:S(2)}) collective-permute-start(f32[2,96,256]{2,1,0:T(8,128)} %get-tuple-element.55), channel_id=1, source_target_pairs={{0,24},{1,25},{2,26},{3,27},{4,28},{5,29},{6,30},{7,31},{8,16},{9,... | collective-permute-start | bytes 589832 | tf_op jit(solution)/shard_map/ppermute | solution.py:228
  35.8 12.4 %collective-permute-start.5 = (f32[2,96,256]{2,1,0:T(8,128)S(1)}, f32[2,96,256]{2,1,0:T(8,128)S(1)}, u32[]{:S(2)}, u32[]{:S(2)}) collective-permute-start(f32[2,96,256]{2,1,0:T(8,128)S(1)} %copy-done.47), channel_id=1, source_target_pairs={{0,4},{1,5},{2,6},{3,7},{4,0},{5,1},{6,2},{7,3},{8,12},{9,13},{10,... | collective-permute-start | bytes 589832 | tf_op jit(solution)/shard_map/ppermute | solution.py:228
  38.4 9.8 %collective-permute-start.6 = (f32[2,96,256]{2,1,0:T(8,128)S(1)}, f32[2,96,256]{2,1,0:T(8,128)S(1)}, u32[]{:S(2)}, u32[]{:S(2)}) collective-permute-start(f32[2,96,256]{2,1,0:T(8,128)S(1)} %copy-done.46), channel_id=1, source_target_pairs={{0,6},{1,7},{2,0},{3,1},{4,2},{5,3},{6,4},{7,5},{8,14},{9,15},{10,... | collective-permute-start | bytes 589832 | tf_op jit(solution)/shard_map/ppermute | solution.py:228
  48.9 24.7 %copy-start.39 = (s32[48]{0:T(128)S(1)}, s32[48]{0:T(128)}, u32[]{:S(2)}) copy-start(s32[48]{0:T(128)} %reshape.31.refs_1_) | copy-start | bytes 580
  48.9 24.8 %copy-start.45 = (f32[2,96,256]{2,1,0:T(8,128)S(1)}, f32[2,96,256]{2,1,0:T(8,128)}, u32[]{:S(2)}) copy-start(f32[2,96,256]{2,1,0:T(8,128)} %get-tuple-element.57) | copy-start | bytes 589828
  48.9 29.6 %copy-start.44 = (f32[2,96,256]{2,1,0:T(8,128)S(1)}, f32[2,96,256]{2,1,0:T(8,128)}, u32[]{:S(2)}) copy-start(f32[2,96,256]{2,1,0:T(8,128)} %get-tuple-element.58) | copy-start | bytes 589828
  48.9 29.6 %copy-start.43 = (f32[2,96,256]{2,1,0:T(8,128)S(1)}, f32[2,96,256]{2,1,0:T(8,128)}, u32[]{:S(2)}) copy-start(f32[2,96,256]{2,1,0:T(8,128)} %get-tuple-element.59) | copy-start | bytes 589828
  51.1 19.6 %collective-permute-start.10 = (f32[2,4,96,256]{3,2,1,0:T(8,128)}, f32[2,4,96,256]{3,2,1,0:T(8,128)S(1)}, u32[]{:S(2)}, u32[]{:S(2)}) collective-permute-start(f32[2,4,96,256]{3,2,1,0:T(8,128)} %shard_map.90.refs_1_), channel_id=1, source_target_pairs={{0,8},{1,9},{2,10},{3,11},{4,12},{5,13},{6,14},{7,15},{8,0},{9,1},... | collective-permute-start | bytes 2359304 | tf_op jit(solution)/shard_map/ppermute | solution.py:228
  51.9 19.6 %collective-permute-start.11 = (f32[2,4,96,256]{3,2,1,0:T(8,128)}, f32[2,4,96,256]{3,2,1,0:T(8,128)S(1)}, u32[]{:S(2)}, u32[]{:S(2)}) collective-permute-start(f32[2,4,96,256]{3,2,1,0:T(8,128)} %shard_map.90.refs_1_), channel_id=1, source_target_pairs={{0,16},{1,17},{2,18},{3,19},{4,20},{5,21},{6,22},{7,23},{8,24},{9,... | collective-permute-start | bytes 2359304 | tf_op jit(solution)/shard_map/ppermute | solution.py:228
  70.7 23.3 %copy-start.3 = (f32[2,4,96,256]{3,2,1,0:T(8,128)}, f32[2,4,96,256]{3,2,1,0:T(8,128)S(1)}, u32[]{:S(2)}) copy-start(f32[2,4,96,256]{3,2,1,0:T(8,128)S(1)} %collective-permute-done.10.refs_2_) | copy-start | bytes 2359300
  70.7 19.4 %collective-permute-start.12 = (f32[1,4,96,256]{3,2,1,0:T(8,128)S(1)}, f32[1,4,96,256]{3,2,1,0:T(8,128)S(1)}, u32[]{:S(2)}, u32[]{:S(2)}) collective-permute-start(f32[1,4,96,256]{3,2,1,0:T(8,128)S(1)} %slice.16), channel_id=1, source_target_pairs={{0,16},{1,17},{2,18},{3,19},{4,20},{5,21},{6,22},{7,23},{8,24},{9,... | collective-permute-start | bytes 1179656 | tf_op jit(solution)/shard_map/ppermute | solution.py:228
  71.5 22.5 %copy-start.4 = (f32[2,4,96,256]{3,2,1,0:T(8,128)}, f32[2,4,96,256]{3,2,1,0:T(8,128)S(1)}, u32[]{:S(2)}) copy-start(f32[2,4,96,256]{3,2,1,0:T(8,128)S(1)} %collective-permute-done.11.refs_3_) | copy-start | bytes 2359300
  71.5 18.6 %collective-permute-start.13 = (f32[1,4,96,256]{3,2,1,0:T(8,128)S(1)}, f32[1,4,96,256]{3,2,1,0:T(8,128)S(1)}, u32[]{:S(2)}, u32[]{:S(2)}) collective-permute-start(f32[1,4,96,256]{3,2,1,0:T(8,128)S(1)} %slice.17), channel_id=1, source_target_pairs={{0,8},{1,9},{2,10},{3,11},{4,12},{5,13},{6,14},{7,15},{8,0},{9,1},... | collective-permute-start | bytes 1179656 | tf_op jit(solution)/shard_map/ppermute | solution.py:228
  73.7 10.1 %collective-permute-start.14 = (f32[2,96,256]{2,1,0:T(8,128)S(1)}, f32[2,96,256]{2,1,0:T(8,128)S(1)}, u32[]{:S(2)}, u32[]{:S(2)}) collective-permute-start(f32[2,96,256]{2,1,0:T(8,128)S(1)} %copy-done.45), channel_id=1, source_target_pairs={{0,2},{1,3},{2,4},{3,5},{4,6},{5,7},{6,0},{7,1},{8,10},{9,11},{10,... | collective-permute-start | bytes 589832 | tf_op jit(solution)/shard_map/ppermute | solution.py:228
  78.5 11.6 %collective-permute-start.15 = (f32[2,96,256]{2,1,0:T(8,128)S(1)}, f32[2,96,256]{2,1,0:T(8,128)S(1)}, u32[]{:S(2)}, u32[]{:S(2)}) collective-permute-start(f32[2,96,256]{2,1,0:T(8,128)S(1)} %copy-done.44), channel_id=1, source_target_pairs={{0,4},{1,5},{2,6},{3,7},{4,0},{5,1},{6,2},{7,3},{8,12},{9,13},{10,... | collective-permute-start | bytes 589832 | tf_op jit(solution)/shard_map/ppermute | solution.py:228
  78.5 11.6 %collective-permute-start.16 = (f32[2,96,256]{2,1,0:T(8,128)S(1)}, f32[2,96,256]{2,1,0:T(8,128)S(1)}, u32[]{:S(2)}, u32[]{:S(2)}) collective-permute-start(f32[2,96,256]{2,1,0:T(8,128)S(1)} %copy-done.43), channel_id=1, source_target_pairs={{0,6},{1,7},{2,0},{3,1},{4,2},{5,3},{6,4},{7,5},{8,14},{9,15},{10,... | collective-permute-start | bytes 589832 | tf_op jit(solution)/shard_map/ppermute | solution.py:228
  106.7 3.3 %collective-permute-start.17 = (f32[12,32,256]{2,1,0:T(8,128)}, f32[12,32,256]{2,1,0:T(8,128)S(1)}, u32[]{:S(2)}, u32[]{:S(2)}) collective-permute-start(f32[12,32,256]{2,1,0:T(8,128)} %get-tuple-element.63), channel_id=1, source_target_pairs={{0,1},{1,0},{2,3},{3,2},{4,5},{5,4},{6,7},{7,6},{8,9},{9,8},{10,11... | collective-permute-start | bytes 1179656 | tf_op jit(solution)/shard_map/ppermute | solution.py:228
  108.0 32.2 %collective-permute-start.27 = (f32[2,4,96,256]{3,2,1,0:T(8,128)S(1)}, f32[2,4,96,256]{3,2,1,0:T(8,128)S(1)}, u32[]{:S(2)}, u32[]{:S(2)}) collective-permute-start(f32[2,4,96,256]{3,2,1,0:T(8,128)S(1)} %copy-done), channel_id=1, source_target_pairs={{0,8},{1,9},{2,10},{3,11},{4,12},{5,13},{6,14},{7,15},{8,0},{9,1},... | collective-permute-start | bytes 2359304 | tf_op jit(solution)/shard_map/ppermute | solution.py:228
  109.3 32.4 %collective-permute-start.28 = (f32[2,4,96,256]{3,2,1,0:T(8,128)S(1)}, f32[2,4,96,256]{3,2,1,0:T(8,128)S(1)}, u32[]{:S(2)}, u32[]{:S(2)}) collective-permute-start(f32[2,4,96,256]{3,2,1,0:T(8,128)S(1)} %copy-done), channel_id=1, source_target_pairs={{0,16},{1,17},{2,18},{3,19},{4,20},{5,21},{6,22},{7,23},{8,24},{9,... | collective-permute-start | bytes 2359304 | tf_op jit(solution)/shard_map/ppermute | solution.py:228
  111.8 23.9 %collective-permute-start.20 = (f32[12,32,256]{2,1,0:T(8,128)}, f32[12,32,256]{2,1,0:T(8,128)S(1)}, u32[]{:S(2)}, u32[]{:S(2)}) collective-permute-start(f32[12,32,256]{2,1,0:T(8,128)} %add.217.refs_4_.refs_5_), channel_id=1, source_target_pairs={{6,4},{7,5},{14,12},{15,13},{22,20},{23,21},{30,28},{31,29}} | collective-permute-start | bytes 1179656 | tf_op jit(solution)/shard_map/ppermute | solution.py:228
  112.5 23.8 %collective-permute-start.19 = (f32[12,32,256]{2,1,0:T(8,128)}, f32[12,32,256]{2,1,0:T(8,128)S(1)}, u32[]{:S(2)}, u32[]{:S(2)}) collective-permute-start(f32[12,32,256]{2,1,0:T(8,128)} %add.217.refs_4_.refs_5_), channel_id=1, source_target_pairs={{0,2},{1,3},{8,10},{9,11},{16,18},{17,19},{24,26},{25,27}} | collective-permute-start | bytes 1179656 | tf_op jit(solution)/shard_map/ppermute | solution.py:228
  127.2 9.0 %collective-permute-start.18 = (f32[12,32,256]{2,1,0:T(8,128)}, f32[12,32,256]{2,1,0:T(8,128)S(1)}, u32[]{:S(2)}, u32[]{:S(2)}) collective-permute-start(f32[12,32,256]{2,1,0:T(8,128)} %get-tuple-element.65), channel_id=1, source_target_pairs={{0,1},{1,0},{2,3},{3,2},{4,5},{5,4},{6,7},{7,6},{8,9},{9,8},{10,11... | collective-permute-start | bytes 1179656 | tf_op jit(solution)/shard_map/ppermute | solution.py:228
  135.7 21.8 %collective-permute-start.22 = (f32[12,32,256]{2,1,0:T(8,128)}, f32[12,32,256]{2,1,0:T(8,128)S(1)}, u32[]{:S(2)}, u32[]{:S(2)}) collective-permute-start(f32[12,32,256]{2,1,0:T(8,128)} %get-tuple-element.69), channel_id=1, source_target_pairs={{0,1},{1,0},{2,3},{3,2},{4,5},{5,4},{6,7},{7,6},{8,9},{9,8},{10,11... | collective-permute-start | bytes 1179656 | tf_op jit(solution)/shard_map/ppermute | solution.py:228
  137.4 20.0 %collective-permute-start.25 = (f32[12,32,256]{2,1,0:T(8,128)S(1)}, f32[12,32,256]{2,1,0:T(8,128)S(1)}, u32[]{:S(2)}, u32[]{:S(2)}) collective-permute-start(f32[12,32,256]{2,1,0:T(8,128)S(1)} %get-tuple-element.88.refs_5_), channel_id=1, source_target_pairs={{4,2},{5,3},{6,4},{7,5},{12,10},{13,11},{14,12},{15,13},{20,18},{2... | collective-permute-start | bytes 1179656 | tf_op jit(solution)/shard_map/ppermute | solution.py:228
  138.1 19.3 %collective-permute-start.23 = (f32[12,32,256]{2,1,0:T(8,128)S(1)}, f32[12,32,256]{2,1,0:T(8,128)S(1)}, u32[]{:S(2)}, u32[]{:S(2)}) collective-permute-start(f32[12,32,256]{2,1,0:T(8,128)S(1)} %get-tuple-element.89.refs_4_), channel_id=1, source_target_pairs={{0,2},{1,3},{2,4},{3,5},{8,10},{9,11},{10,12},{11,13},{16,18},{17,... | collective-permute-start | bytes 1179656 | tf_op jit(solution)/shard_map/ppermute | solution.py:228
  140.3 10.8 %collective-permute-start.29 = (f32[1,4,96,256]{3,2,1,0:T(8,128)S(1)}, f32[1,4,96,256]{3,2,1,0:T(8,128)S(1)}, u32[]{:S(2)}, u32[]{:S(2)}) collective-permute-start(f32[1,4,96,256]{3,2,1,0:T(8,128)S(1)} %slice.18), channel_id=1, source_target_pairs={{0,16},{1,17},{2,18},{3,19},{4,20},{5,21},{6,22},{7,23},{8,24},{9,... | collective-permute-start | bytes 1179656 | tf_op jit(solution)/shard_map/ppermute | solution.py:228
  141.7 10.6 %collective-permute-start.30 = (f32[1,4,96,256]{3,2,1,0:T(8,128)S(1)}, f32[1,4,96,256]{3,2,1,0:T(8,128)S(1)}, u32[]{:S(2)}, u32[]{:S(2)}) collective-permute-start(f32[1,4,96,256]{3,2,1,0:T(8,128)S(1)} %slice.19), channel_id=1, source_target_pairs={{0,8},{1,9},{2,10},{3,11},{4,12},{5,13},{6,14},{7,15},{8,0},{9,1},... | collective-permute-start | bytes 1179656 | tf_op jit(solution)/shard_map/ppermute | solution.py:228
  169.6 5.7 %collective-permute-start.31 = (f32[24,32,256]{2,1,0:T(8,128)}, f32[24,32,256]{2,1,0:T(8,128)S(1)}, u32[]{:S(2)}, u32[]{:S(2)}) collective-permute-start(f32[24,32,256]{2,1,0:T(8,128)} %get-tuple-element.73), channel_id=1, source_target_pairs={{0,1},{1,0},{2,3},{3,2},{4,5},{5,4},{6,7},{7,6},{8,9},{9,8},{10,11... | collective-permute-start | bytes 2359304 | tf_op jit(solution)/shard_map/ppermute | solution.py:228
  169.6 13.3 %collective-permute-start.24 = (f32[12,32,256]{2,1,0:T(8,128)S(1)}, f32[12,32,256]{2,1,0:T(8,128)S(1)}, u32[]{:S(2)}, u32[]{:S(2)}) collective-permute-start(f32[12,32,256]{2,1,0:T(8,128)S(1)} %copy-done.24), channel_id=1, source_target_pairs={{0,2},{1,3},{2,4},{3,5},{4,6},{5,7},{8,10},{9,11},{10,12},{11,13},... | collective-permute-start | bytes 1179656 | tf_op jit(solution)/shard_map/ppermute | solution.py:228
  173.9 13.1 %collective-permute-start.26 = (f32[12,32,256]{2,1,0:T(8,128)S(1)}, f32[12,32,256]{2,1,0:T(8,128)S(1)}, u32[]{:S(2)}, u32[]{:S(2)}) collective-permute-start(f32[12,32,256]{2,1,0:T(8,128)S(1)} %copy-done.23), channel_id=1, source_target_pairs={{2,0},{3,1},{4,2},{5,3},{6,4},{7,5},{10,8},{11,9},{12,10},{13,11},... | collective-permute-start | bytes 1179656 | tf_op jit(solution)/shard_map/ppermute | solution.py:228
  177.4 32.8 %collective-permute-start.34 = (f32[24,32,256]{2,1,0:T(8,128)}, f32[24,32,256]{2,1,0:T(8,128)S(1)}, u32[]{:S(2)}, u32[]{:S(2)}) collective-permute-start(f32[24,32,256]{2,1,0:T(8,128)} %add.229.refs_6_.refs_7_), channel_id=1, source_target_pairs={{6,4},{7,5},{14,12},{15,13},{22,20},{23,21},{30,28},{31,29}} | collective-permute-start | bytes 2359304 | tf_op jit(solution)/shard_map/ppermute | solution.py:228
  178.1 32.1 %collective-permute-start.33 = (f32[24,32,256]{2,1,0:T(8,128)}, f32[24,32,256]{2,1,0:T(8,128)S(1)}, u32[]{:S(2)}, u32[]{:S(2)}) collective-permute-start(f32[24,32,256]{2,1,0:T(8,128)} %add.229.refs_6_.refs_7_), channel_id=1, source_target_pairs={{0,2},{1,3},{8,10},{9,11},{16,18},{17,19},{24,26},{25,27}} | collective-permute-start | bytes 2359304 | tf_op jit(solution)/shard_map/ppermute | solution.py:228
  198.6 11.6 %collective-permute-start.32 = (f32[24,32,256]{2,1,0:T(8,128)}, f32[24,32,256]{2,1,0:T(8,128)S(1)}, u32[]{:S(2)}, u32[]{:S(2)}) collective-permute-start(f32[24,32,256]{2,1,0:T(8,128)} %get-tuple-element.75), channel_id=1, source_target_pairs={{0,1},{1,0},{2,3},{3,2},{4,5},{5,4},{6,7},{7,6},{8,9},{9,8},{10,11... | collective-permute-start | bytes 2359304 | tf_op jit(solution)/shard_map/ppermute | solution.py:228
  209.6 16.8 %collective-permute-start.36 = (f32[24,32,256]{2,1,0:T(8,128)}, f32[24,32,256]{2,1,0:T(8,128)S(1)}, u32[]{:S(2)}, u32[]{:S(2)}) collective-permute-start(f32[24,32,256]{2,1,0:T(8,128)} %get-tuple-element.79), channel_id=1, source_target_pairs={{0,1},{1,0},{2,3},{3,2},{4,5},{5,4},{6,7},{7,6},{8,9},{9,8},{10,11... | collective-permute-start | bytes 2359304 | tf_op jit(solution)/shard_map/ppermute | solution.py:228
  211.8 14.6 %collective-permute-start.39 = (f32[24,32,256]{2,1,0:T(8,128)S(1)}, f32[24,32,256]{2,1,0:T(8,128)S(1)}, u32[]{:S(2)}, u32[]{:S(2)}) collective-permute-start(f32[24,32,256]{2,1,0:T(8,128)S(1)} %get-tuple-element.84.refs_7_), channel_id=1, source_target_pairs={{4,2},{5,3},{6,4},{7,5},{12,10},{13,11},{14,12},{15,13},{20,18},{2... | collective-permute-start | bytes 2359304 | tf_op jit(solution)/shard_map/ppermute | solution.py:228
  212.5 19.9 %copy-start.12 = (f32[24,32,256]{2,1,0:T(8,128)S(1)}, f32[24,32,256]{2,1,0:T(8,128)}, u32[]{:S(2)}) copy-start(f32[24,32,256]{2,1,0:T(8,128)} %get-tuple-element.78) | copy-start | bytes 2359300
  212.5 19.9 %collective-permute-start.37 = (f32[24,32,256]{2,1,0:T(8,128)S(1)}, f32[24,32,256]{2,1,0:T(8,128)S(1)}, u32[]{:S(2)}, u32[]{:S(2)}) collective-permute-start(f32[24,32,256]{2,1,0:T(8,128)S(1)} %get-tuple-element.85.refs_6_), channel_id=1, source_target_pairs={{0,2},{1,3},{2,4},{3,5},{8,10},{9,11},{10,12},{11,13},{16,18},{17,... | collective-permute-start | bytes 2359304 | tf_op jit(solution)/shard_map/ppermute | solution.py:228
  226.3 15.4 %collective-permute-start.35 = (f32[24,32,256]{2,1,0:T(8,128)}, f32[24,32,256]{2,1,0:T(8,128)S(1)}, u32[]{:S(2)}, u32[]{:S(2)}) collective-permute-start(f32[24,32,256]{2,1,0:T(8,128)} %get-tuple-element.77), channel_id=1, source_target_pairs={{0,1},{1,0},{2,3},{3,2},{4,5},{5,4},{6,7},{7,6},{8,9},{9,8},{10,11... | collective-permute-start | bytes 2359304 | tf_op jit(solution)/shard_map/ppermute | solution.py:228
  233.8 20.8 %collective-permute-start.38 = (f32[24,32,256]{2,1,0:T(8,128)}, f32[24,32,256]{2,1,0:T(8,128)S(1)}, u32[]{:S(2)}, u32[]{:S(2)}) collective-permute-start(f32[24,32,256]{2,1,0:T(8,128)} %get-tuple-element.87), channel_id=1, source_target_pairs={{0,2},{1,3},{2,4},{3,5},{4,6},{5,7},{8,10},{9,11},{10,12},{11,13},... | collective-permute-start | bytes 2359304 | tf_op jit(solution)/shard_map/ppermute | solution.py:228
  238.2 20.5 %collective-permute-start.40 = (f32[24,32,256]{2,1,0:T(8,128)S(1)}, f32[24,32,256]{2,1,0:T(8,128)S(1)}, u32[]{:S(2)}, u32[]{:S(2)}) collective-permute-start(f32[24,32,256]{2,1,0:T(8,128)S(1)} %get-tuple-element.86), channel_id=1, source_target_pairs={{2,0},{3,1},{4,2},{5,3},{6,4},{7,5},{10,8},{11,9},{12,10},{13,11},... | collective-permute-start | bytes 2359304 | tf_op jit(solution)/shard_map/ppermute | solution.py:228
  239.7 2.0 collective-permute-start.21
  241.7 17.0 %copy-start.21 = (f32[12,32,256]{2,1,0:T(8,128)}, f32[12,32,256]{2,1,0:T(8,128)S(1)}, u32[]{:S(2)}) copy-start(f32[12,32,256]{2,1,0:T(8,128)S(1)} %collective-permute-done.21.refs_4_) | copy-start | bytes 1179652
  241.7 17.0 %copy-start.11 = (f32[24,32,256]{2,1,0:T(8,128)}, f32[24,32,256]{2,1,0:T(8,128)S(1)}, u32[]{:S(2)}) copy-start(f32[24,32,256]{2,1,0:T(8,128)S(1)} %collective-permute-done.35.refs_8_) | copy-start | bytes 2359300
  266.8 2.0 collective-permute-start.41
  269.9 7.3 %collective-permute-start.44 = (f32[128,256]{1,0:T(8,128)S(1)}, f32[128,256]{1,0:T(8,128)S(1)}, u32[]{:S(2)}, u32[]{:S(2)}) collective-permute-start(f32[128,256]{1,0:T(8,128)S(1)} %get-tuple-element.95), channel_id=1, source_target_pairs={{0,24},{1,25},{2,26},{3,27},{4,28},{5,29},{6,30},{7,31},{8,16},{9,... | collective-permute-start | bytes 393224 | tf_op jit(solution)/shard_map/ppermute | solution.py:228
  271.4 7.9 %collective-permute-start.43 = (f32[128,256]{1,0:T(8,128)S(1)}, f32[128,256]{1,0:T(8,128)S(1)}, u32[]{:S(2)}, u32[]{:S(2)}) collective-permute-start(f32[128,256]{1,0:T(8,128)S(1)} %get-tuple-element.96), channel_id=1, source_target_pairs={{0,16},{1,17},{2,18},{3,19},{4,20},{5,21},{6,22},{7,23},{8,24},{9,... | collective-permute-start | bytes 393224 | tf_op jit(solution)/shard_map/ppermute | solution.py:228
  272.3 6.9 %collective-permute-start.42 = (f32[128,256]{1,0:T(8,128)S(1)}, f32[128,256]{1,0:T(8,128)S(1)}, u32[]{:S(2)}, u32[]{:S(2)}) collective-permute-start(f32[128,256]{1,0:T(8,128)S(1)} %get-tuple-element.94), channel_id=1, source_target_pairs={{0,8},{1,9},{2,10},{3,11},{4,12},{5,13},{6,14},{7,15},{8,0},{9,1},... | collective-permute-start | bytes 393224 | tf_op jit(solution)/shard_map/ppermute | solution.py:228
  279.3 4.0 %collective-permute-start.47 = (f32[32,256]{1,0:T(8,128)S(1)}, f32[32,256]{1,0:T(8,128)S(1)}, u32[]{:S(2)}, u32[]{:S(2)}) collective-permute-start(f32[32,256]{1,0:T(8,128)S(1)} %get-tuple-element.98), channel_id=1, source_target_pairs={{0,6},{1,7},{2,0},{3,1},{4,2},{5,3},{6,4},{7,5},{8,14},{9,15},{10,... | collective-permute-start | bytes 98312 | tf_op jit(solution)/shard_map/ppermute | solution.py:228
  279.8 5.3 %collective-permute-start.46 = (f32[32,256]{1,0:T(8,128)S(1)}, f32[32,256]{1,0:T(8,128)S(1)}, u32[]{:S(2)}, u32[]{:S(2)}) collective-permute-start(f32[32,256]{1,0:T(8,128)S(1)} %get-tuple-element.99), channel_id=1, source_target_pairs={{0,4},{1,5},{2,6},{3,7},{4,0},{5,1},{6,2},{7,3},{8,12},{9,13},{10,... | collective-permute-start | bytes 98312 | tf_op jit(solution)/shard_map/ppermute | solution.py:228
  282.6 5.7 %collective-permute-start.45 = (f32[32,256]{1,0:T(8,128)S(1)}, f32[32,256]{1,0:T(8,128)S(1)}, u32[]{:S(2)}, u32[]{:S(2)}) collective-permute-start(f32[32,256]{1,0:T(8,128)S(1)} %get-tuple-element.97), channel_id=1, source_target_pairs={{0,2},{1,3},{2,4},{3,5},{4,6},{5,7},{6,0},{7,1},{8,10},{9,11},{10,... | collective-permute-start | bytes 98312 | tf_op jit(solution)/shard_map/ppermute | solution.py:228
  288.3 5.8 %collective-permute-start.48 = (f32[32,256]{1,0:T(8,128)S(1)}, f32[32,256]{1,0:T(8,128)S(1)}, u32[]{:S(2)}, u32[]{:S(2)}) collective-permute-start(f32[32,256]{1,0:T(8,128)S(1)} %get-tuple-element.83), channel_id=1, source_target_pairs={{0,2},{1,3},{2,4},{3,5},{4,6},{5,7},{6,0},{7,1},{8,10},{9,11},{10,... | collective-permute-start | bytes 98312 | tf_op jit(solution)/shard_map/ppermute | solution.py:228
  288.4 5.6 %collective-permute-start.49 = (f32[32,256]{1,0:T(8,128)S(1)}, f32[32,256]{1,0:T(8,128)S(1)}, u32[]{:S(2)}, u32[]{:S(2)}) collective-permute-start(f32[32,256]{1,0:T(8,128)S(1)} %get-tuple-element.83), channel_id=1, source_target_pairs={{0,4},{1,5},{2,6},{3,7},{4,0},{5,1},{6,2},{7,3},{8,12},{9,13},{10,... | collective-permute-start | bytes 98312 | tf_op jit(solution)/shard_map/ppermute | solution.py:228
  288.6 6.0 %collective-permute-start.50 = (f32[32,256]{1,0:T(8,128)S(1)}, f32[32,256]{1,0:T(8,128)S(1)}, u32[]{:S(2)}, u32[]{:S(2)}) collective-permute-start(f32[32,256]{1,0:T(8,128)S(1)} %get-tuple-element.83), channel_id=1, source_target_pairs={{0,6},{1,7},{2,0},{3,1},{4,2},{5,3},{6,4},{7,5},{8,14},{9,15},{10,... | collective-permute-start | bytes 98312 | tf_op jit(solution)/shard_map/ppermute | solution.py:228
  294.6 5.0 %collective-permute-start.51 = (f32[128,256]{1,0:T(8,128)S(1)}, f32[128,256]{1,0:T(8,128)S(1)}, u32[]{:S(2)}, u32[]{:S(2)}) collective-permute-start(f32[128,256]{1,0:T(8,128)S(1)} %bitcast.68), channel_id=1, source_target_pairs={{0,8},{1,9},{2,10},{3,11},{4,12},{5,13},{6,14},{7,15},{8,0},{9,1},... | collective-permute-start | bytes 393224 | tf_op jit(solution)/shard_map/ppermute | solution.py:228
  295.5 5.0 %collective-permute-start.52 = (f32[128,256]{1,0:T(8,128)S(1)}, f32[128,256]{1,0:T(8,128)S(1)}, u32[]{:S(2)}, u32[]{:S(2)}) collective-permute-start(f32[128,256]{1,0:T(8,128)S(1)} %bitcast.69), channel_id=1, source_target_pairs={{0,16},{1,17},{2,18},{3,19},{4,20},{5,21},{6,22},{7,23},{8,24},{9,... | collective-permute-start | bytes 393224 | tf_op jit(solution)/shard_map/ppermute | solution.py:228
  296.6 5.9 %collective-permute-start.53 = (f32[128,256]{1,0:T(8,128)S(1)}, f32[128,256]{1,0:T(8,128)S(1)}, u32[]{:S(2)}, u32[]{:S(2)}) collective-permute-start(f32[128,256]{1,0:T(8,128)S(1)} %bitcast.70), channel_id=1, source_target_pairs={{0,24},{1,25},{2,26},{3,27},{4,28},{5,29},{6,30},{7,31},{8,16},{9,... | collective-permute-start | bytes 393224 | tf_op jit(solution)/shard_map/ppermute | solution.py:228
  302.5 2.0 collective-permute-start.54
  (40 other events, 177.2 us)

commit v3 on v2

--- a/solution.py
+++ b/solution.py
@@ -84,6 +84,11 @@
 def stack_kernel(place, *refs):
     for m in range(len(refs) - 1):
         refs[-1][:, m] = refs[m][...]
+
+
+def halves_kernel(first_ref, second_ref, first_half, second_half):
+    first_half[...] = first_ref[:1]
+    second_half[...] = second_ref[1:]
 
 
 def assemble_kernel(lines, rb, place, *refs):
@@ -118,38 +123,34 @@
         lo_ref[p, pl.ds(at, width), :] = (value - hi.astype(jnp.float32)).astype(jnp.bfloat16)
 
 
-def product_kernel(panel_ids, slots, rb, lo, hi, waits, info, where, g_ref, *refs):
-    count = len(panel_ids)
-    x_hi, x_lo = refs[:count], refs[count : 2 * count]
-    mine, other, held, done = refs[2 * count + waits :]
+def product_kernel(panels, slots, bounds, waits, info, where, g_ref, *refs):
+    x_hi, x_lo = refs[:panels], refs[panels : 2 * panels]
+    outs, held, done = refs[2 * panels + waits : -2], refs[-2], refs[-1]
     tile = pl.program_id(0)
     tile_slots, rows, depth = g_ref.shape
-    size = hi - lo
-    h = info[1]
     g = g_ref[...].reshape(tile_slots * rows, depth)
     g_hi = g.astype(jnp.bfloat16)
     g_lo = (g - g_hi.astype(jnp.float32)).astype(jnp.bfloat16)
     dot = functools.partial(jnp.dot, preferred_element_type=jnp.float32)
-    for k, p in enumerate(panel_ids):
-        value = dot(g_hi, x_hi[k][0]) + (dot(g_hi, x_lo[k][0]) + dot(g_lo, x_hi[k][0]))
+    for p in range(panels):
+        value = dot(g_hi, x_hi[p][0]) + (dot(g_hi, x_lo[p][0]) + dot(g_lo, x_hi[p][0]))
         for s in range(tile_slots):
             at = where[p * slots + tile * tile_slots + s]
-            at = jnp.where((at >= lo) & (at < hi), at - lo, size)
-            for core in range(2):
-                start = s * rows + core * rb
-                held[(core + h) % 2, at] = value[start : start + rb]
+            held[jnp.where(at >= 0, at, bounds[-1])] = value[s * rows : (s + 1) * rows]
 
     @pl.when(tile == pl.num_programs(0) - 1)
     def _():
-        first = pltpu.make_async_copy(held.at[0, pl.ds(0, size)], mine, done.at[0])
-        second = pltpu.make_async_copy(held.at[1, pl.ds(0, size)], other, done.at[1])
-        first.start()
-        second.start()
-        first.wait()
-        second.wait()
-
-
-def product(g3, xs, panel_ids, lo, hi, rb, info, where, after):
+        copies = [
+            pltpu.make_async_copy(held.at[pl.ds(bounds[k], bounds[k + 1] - bounds[k])], out, done.at[k])
+            for k, out in enumerate(outs)
+        ]
+        for copy in copies:
+            copy.start()
+        for copy in copies:
+            copy.wait()
+
+
+def product(g3, xs, bounds, rb, info, where, after):
     slots, width, depth = g3.shape
     columns = xs[0][0].shape[2]
     rows = 2 * rb
@@ -158,20 +159,22 @@
         pl.BlockSpec((1, depth, columns), functools.partial(lambda at, a, i, w: (at, 0, 0), at))
         for _, _, at in xs
     ]
-    out = jax.ShapeDtypeStruct((hi - lo, rb, columns), jnp.float32)
     anywhere = pl.BlockSpec(memory_space=pl.ANY)
+    pieces = len(bounds) - 1
     return pl.pallas_call(
-        functools.partial(product_kernel, panel_ids, slots, rb, lo, hi, len(after)),
-        out_shape=(out, out),
+        functools.partial(product_kernel, len(xs), slots, bounds, len(after)),
+        out_shape=[
+            jax.ShapeDtypeStruct((bounds[k + 1] - bounds[k], rows, columns), jnp.float32) for k in range(pieces)
+        ],
         grid_spec=pltpu.PrefetchScalarGridSpec(
             num_scalar_prefetch=2,
             grid=(slots // tile_slots,),
             in_specs=[pl.BlockSpec((tile_slots, rows, depth), lambda tile, i, w: (tile, i[0], 0))]
             + x_specs + x_specs + [anywhere] * len(after),
-            out_specs=(anywhere, anywhere),
+            out_specs=[anywhere] * pieces,
             scratch_shapes=[
-                pltpu.VMEM((2, hi - lo + 1, rb, columns), jnp.float32),
-                pltpu.SemaphoreType.DMA((2,)),
+                pltpu.VMEM((bounds[-1] + 1, rows, columns), jnp.float32),
+                pltpu.SemaphoreType.DMA((pieces,)),
             ],
         ),
         compiler_params=pltpu.CompilerParams(vmem_limit_bytes=VMEM_LIMIT),
@@ -182,15 +185,29 @@
     )(info, where, g3, *[x[0] for x in xs], *[x[1] for x in xs], *after)
 
 
-def finish_kernel(parts, bounds, groups, where, *refs):
+def merge_kernel(bounds, lines, place, *refs):
+    mine, other = refs[-2:]
+    rb = mine.shape[1]
+    from_others = place[1] != jnp.where(place[2] == 0, 0, lines - 1)
+    for core in range(2):
+        rows = slice(core * rb, (core + 1) * rb)
+
+        def fill(out, rows=rows):
+            for k in range(len(bounds) - 1):
+                arrived = jnp.where(from_others, refs[2 * k + 1][:, rows, :], 0.0)
+                value = refs[2 * k][:, rows, :] + arrived
+                out[bounds[k] : bounds[k + 1]] = value
+
+        pl.when(place[2] == core)(functools.partial(fill, mine))
+        pl.when(place[2] != core)(functools.partial(fill, other))
+
+
+def finish_kernel(groups, where, *refs):
     n_refs, refs = refs[: len(groups)], refs[len(groups) :]
-    ins = refs[: 4 * parts]
-    panel_ref, diag_ref, total = refs[4 * parts :]
+    mine, swapped, panel_ref, diag_ref, total = refs
+    total[...] = mine[...] + swapped[...]
     panels, slots, rb, width = panel_ref.shape
     n_of = {p: n_refs[g][at] for g, group in enumerate(groups) for at, p in enumerate(group)}
-    for k in range(parts):
-        own, swapped, up, down = ins[4 * k : 4 * k + 4]
-        total[bounds[k] : bounds[k + 1]] = (own[...] + swapped[...]) + (up[...] + down[...])
     for p in range(panels):
         for s in range(slots):
             at = where[p * slots + s]
@@ -245,11 +262,9 @@
     keep = 3 * panels * slots // 4
     half = panels // 2
     groups = [tuple(range(half)), tuple(range(half, panels))]
-    ends = [g[-1] + 1 for g in groups]
-    bounds = [0] + [keep - slots * (panels - end) for end in ends]
-    chunk_panels = [tuple(range(lo // slots, end)) for lo, end in zip(bounds, ends)]
-
-    split, normalized, parts_of, planes, stacked, gathered = [], [], [], [], [], []
+    bounds = [0, keep // 2, keep]
+
+    split, normalized, parts_of, planes, stacked, gathered, halved = [], [], [], [], [], [], []
 
     def normalize(group, after):
         shape = (2, len(group) * halves * rb // lines, width)
@@ -266,7 +281,6 @@
 
     partner = swap(lax.dynamic_slice_in_dim(factor_blocks, (1 - h) * halves, halves, 1))
     spread = []
-    gather_after = []
     for g, group in enumerate(groups):
         normalize(group, spread)
         parts = parts_of[g]
@@ -278,23 +292,32 @@
         )(place, *held)
         spread = [outgoing[0]]
         planes.append(outgoing)
+    along_planes = [
+        [outgoing[0]] + [along(outgoing[m], m) for m in range(1, lines)] for outgoing in planes
+    ]
     for g, group in enumerate(groups):
-        outgoing = planes[g]
-        shape = outgoing[0].shape
-        held = [outgoing[0]] + [along(outgoing[m], m) for m in range(1, lines)]
-        after = gather_after + ([planes[g + 1][0]] if g + 1 < len(groups) else [])
+        held = along_planes[g]
+        shape = held[0].shape
+        after = halved[-1:] + ([planes[g + 1][0]] if g + 1 < len(groups) else [])
         [both] = call(
             stack_kernel, [jax.ShapeDtypeStruct((2, lines) + shape[1:], f32)], n_in=lines,
             n_after=len(after), moved=8 * lines * math.prod(shape),
         )(place, *held, *after)
         pieces = [both] + [across(both, d) for d in range(1, lines)]
         if lines == 4:
-            pieces[3:] = [across(pieces[1][:1], 2), across(pieces[2][1:], 1)]
-        gather_after = pieces[-2:]
+            half_shape = jax.ShapeDtypeStruct((1,) + both.shape[1:], f32)
+            before = along_planes[g + 1][1:] if g + 1 < len(groups) else []
+            split_pair = call(
+                halves_kernel, [half_shape, half_shape], n_scalar=0, n_in=2,
+                n_after=len(before), moved=8 * both.size // 2,
+            )(pieces[1], pieces[2], *before)
+            pieces[3:] = [across(split_pair[0], 2), across(split_pair[1], 1)]
+            halved.append(split_pair[0])
         stacked.append(both)
         gathered.append(pieces)
-    for g, group in enumerate(groups):
-        pieces, after = gathered[g], stacked[g + 1 : g + 2]
+
+    def assemble(g, after):
+        group, pieces = groups[g], gathered[g]
         block = jax.ShapeDtypeStruct((len(group), halves * width, width), jnp.bfloat16)
         x_hi, x_lo = call(
             functools.partial(assemble_kernel, lines, rb),
@@ -302,7 +325,7 @@
             [pltpu.VMEM((len(group) * halves * width, width), f32)],
             n_in=len(pieces), n_after=len(after), moved=8 * len(group) * halves * width * width,
         )(place, *pieces, *after)
-        split += [(x_hi, x_lo, at) for at in range(len(group))]
+        split.extend((x_hi, x_lo, at) for at in range(len(group)))
 
     g3 = inverse_matrix.reshape(slots, width, halves * width)
     order = [
@@ -318,55 +341,70 @@
         return sum(jnp.where(z == a, jnp.int32(v), 0) for a, v in enumerate(values))
 
     def chosen(made, calls):
-        kinds = sorted({c for c in calls if c is not None})
+        kinds = sorted({c for c in calls.values() if c is not None})
         value = made[kinds[-1]][0] + made[kinds[-1]][1]
         for c in kinds[:-1]:
-            here = functools.reduce(jnp.logical_or, [z == a for a in range(lines) if calls[a] == c])
+            here = [(z == a) & (h == core) for (a, core), named in calls.items() if named == c]
+            here = functools.reduce(jnp.logical_or, here)
             value = jnp.where(here, made[c][0] + made[c][1], value)
         return value
 
-    finals, after, arrived = [], [], []
-    for k, ids in enumerate(chunk_panels):
-        lo, hi = bounds[k], bounds[k + 1]
-        xs = [split[p] for p in ids]
-        made = []
-
-        def compute(after):
-            n = len(made)
-            info = jnp.stack([of_plane([order[a][n] for a in range(lines)]), h])
-            mine, other = product(g3, xs, ids, lo, hi, rb, info, where, after)
-            made.append((mine, swap(other)))
-            return [mine]
-
-        compute(after)
-        up = down = None
-        for step in range(lines - 1):
-            rises = [order[a].index(lines - 1 - step + a) if a <= step else None for a in range(lines)]
-            sinks = [order[a].index(step - lines + 1 + a) if a >= lines - 1 - step else None for a in range(lines)]
-            send_up, send_down = chosen(made, rises), chosen(made, sinks)
-            if step:
-                send_up, send_down = send_up + up, send_down + down
-            up = send(send_up, lambda a, b, c: (a, b + 1, c) if b <= step else None)
-            down = send(send_down, lambda a, b, c: (a, b - 1, c) if b >= lines - 1 - step else None)
-            if step == 0:
-                after = [send_up, send_down]
-                for n in range(lines - 2):
-                    after = compute(after + (arrived if n == 0 else []))
-            elif step == 1:
-                compute([send_up, send_down])
-        after = [send_up, send_down, made[lines - 1][0]]
-        arrived = [up, down]
-        finals += [*made[lines - 1], up, down]
-
+    def add_arrived(value, arrived, step):
+        behind = jnp.where(h == 0, z, lines - 1 - z)
+        return jnp.where((behind > 0) & (behind <= step + 1), value + arrived, value)
+
+    assemble(0, halved[1:2])
+    assemble(1, [])
+    made = [[], []]
+    moving = [[], []]
+
+    def compute(after):
+        n = len(made[0])
+        info = jnp.stack([of_plane([order[a][n] for a in range(lines)])])
+        for k, terms in enumerate(product(g3, split, bounds, rb, info, where, after)):
+            made[k].append((terms, swap(terms) if n < lines - 1 else None))
+
+    def move(k, step):
+        calls = {}
+        for a in range(lines):
+            calls[a, 0] = order[a].index(lines - 1 - step + a) if a <= step else None
+            calls[a, 1] = order[a].index(step - lines + 1 + a) if a >= lines - 1 - step else None
+        value = chosen(made[k], calls)
+        if step:
+            value = add_arrived(value, moving[k][-1], step - 1)
+        moving[k].append(
+            send(value, lambda a, b, c: (a, b + 1 - 2 * c, c) if 0 <= b + 1 - 2 * c < lines else (a, b, 1 - c))
+        )
+        return [value]
+
+    compute([])
+    for step in range(lines - 1):
+        after = move(0, step)
+        if step == 0:
+            compute(after)
+            move(1, 0)
+            continue
+        if step < lines - 2:
+            compute(after)
+        after = move(1, step)
+        if step == lines - 3:
+            compute(after)
+    made_0, made_1 = made
+    moving_0, moving_1 = moving
+
+    half_rows = jax.ShapeDtypeStruct((keep, rb, width), f32)
+    mine, other = call(
+        functools.partial(merge_kernel, bounds, lines), [half_rows, half_rows], n_in=4, moved=24 * keep * rb * width
+    )(place, made_0[-1][0], moving_0[-1], made_1[-1][0], moving_1[-1])
     panel_inverse, terms = call(
-        functools.partial(finish_kernel, len(chunk_panels), bounds, groups),
+        functools.partial(finish_kernel, groups),
         [
             jax.ShapeDtypeStruct(factor_blocks.shape, f32),
             jax.ShapeDtypeStruct(factor_inverse.shape, f32),
         ],
         [pltpu.VMEM((keep, rb, width), f32)],
-        n_in=len(groups) + len(finals), flops=12 * factor_blocks.size * width, moved=20 * factor_blocks.size,
-    )(where, *normalized, *finals)
+        n_in=len(groups) + 2, flops=12 * factor_blocks.size * width, moved=20 * factor_blocks.size,
+    )(where, *normalized, mine, swap(other))
 
     pick = lambda value, at: lax.dynamic_index_in_dim(value, at, 0, False)
     two = terms.reshape(2, half * width, width)

time: 307 us -> 279 us (0.909)
  starting transfers between devices: 78.6 us -> 61.1 us
  Pallas kernels: 109 us -> 94.1 us
  local copies, waits for them, and re-layouts: 10.5 us -> 14.1 us
    ppermute x55 -> x48, starting transfers between devices: 78.6 us -> 61.1 us  [send(): return lax.ppermute(value, AXES, pairs)]
    pallas_call x11 -> x10, Pallas kernels: 91.4 us -> 76.7 us  [the longest x4 53.6 us: product(): pl.pallas_call(functools.partial(product_kernel, len(xs), slots, bounds,...]
    select_n x0 -> x4, other arithmetic: none -> 9.42 us  [add_arrived(): jnp.where((behind > 0) & (behind <= step + 1), value + arrived, value)]
    add x4 -> x1, other arithmetic: 5.25 us -> 1.42 us  [chosen(): value = made[kinds[-1]][0] + made[kinds[-1]][1]]
    unnamed x98 -> x86, local copies, waits for them, and re-layouts: 7.18 us -> 10.9 us
    ppermute x55 -> x48, waiting for transfers between devices: 91.1 us -> 92.6 us  [send(): return lax.ppermute(value, AXES, pairs)]
  transfers between devices with their start and end apart: 55 -> 48, of which waited for: 29 -> 31; matrix products, arithmetic and copies ran while one was open for 4% -> 5% of each run, Pallas kernels for 21% -> 18%
where the time goes in v3:
time: 279 us; the launch traced here: 278 us
  Pallas kernels  94.1 us (34%)
  waiting for transfers between devices  92.6 us (33%)
  starting transfers between devices  61.1 us (22%)
  other arithmetic  15.3 us (5%)
  local copies, waits for them, and re-layouts  14.1 us (5%)
    ppermute x48, waiting for transfers between devices, send(): return lax.ppermute(value, AXES, pairs)  92.6 us
    ppermute x48, starting transfers between devices, send(): return lax.ppermute(value, AXES, pairs)  61.1 us
    pallas_call x4, Pallas kernels, product(): pl.pallas_call(functools.partial(product_kernel, len(xs), slots, bounds,...  53.6 us
    unnamed x86, local copies, waits for them, and re-layouts  10.9 us
    select_n x4, other arithmetic, add_arrived(): jnp.where((behind > 0) & (behind <= step + 1), value + arrived, value)  9.42 us
    pallas_call x2, Pallas kernels, assemble(): call(functools.partial(assemble_kernel, lines, rb), [block, block], [pltp...  9.04 us
    pallas_call x2, Pallas kernels, normalize(): call(functools.partial(normalize_kernel, group, lines), [rows_made] + [ja...  8.56 us
  transfers between devices with their start and end apart: 48, of which 31 were waited for; matrix products, arithmetic and copies ran while one was open for 5% of the time, Pallas kernels for 18%

profile of v3, /device:TPU:0, one launch (start us, length us, event | category | flops | bytes accessed | tf_op | source)
XLA Modules:
  0.0 278.5 jit_solution(4336825969405891946)
XLA Ops:
  0.7 1.2 constant_dynamic-slice_fusion
  5.2 4.2 %shard_map.86 = (f32[2,12,32,256]{3,2,1,0:T(8,128)}, f32[2,96,256]{2,1,0:T(8,128)}, f32[2,96,256]{2,1,0:T(8,128)}, f32[2,96,256]{2,1,0:T(8,128)}, f32[2,96,256]{2,1,0:T(8,128)}) custom-call(s32[3]{0:T(128)} %pad_add_fusion.refs_0_, s32[48]{0:T(128)} %reshape.31.refs_1_, f32[4,12,32,256]{3,2,1,0:T(8,128)} %refs_2_.3, f32[4,6,32,256]{3,2,1,0:T(8,128)} %copy-done.7, ...), custom_call_target="tpu_custom_call" | custom-call | flops 301989888 | bytes 1572864 | tf_op jit(solution)/shard_map/pallas_call | solution.py:272
  9.4 2.9 %collective-permute-start.1 = (f32[2,96,256]{2,1,0:T(8,128)}, f32[2,96,256]{2,1,0:T(8,128)S(1)}, u32[]{:S(2)}, u32[]{:S(2)}) collective-permute-start(f32[2,96,256]{2,1,0:T(8,128)} %get-tuple-element.42), channel_id=1, source_target_pairs={{0,8},{1,9},{2,10},{3,11},{4,12},{5,13},{6,14},{7,15},{8,0},{9,1},... | collective-permute-start | bytes 589832 | tf_op jit(solution)/shard_map/ppermute | solution.py:245
  12.3 1.5 collective-permute-start.2
  13.8 4.4 %collective-permute-done.1.refs_2_ = f32[2,96,256]{2,1,0:T(8,128)S(1)} collective-permute-done((f32[2,96,256]{2,1,0:T(8,128)}, f32[2,96,256]{2,1,0:T(8,128)S(1)}, u32[]{:S(2)}, u32[]{:S(2)}) %collective-permute-start.1) | collective-permute-done | bytes 196640 | tf_op jit(solution)/shard_map/ppermute | solution.py:245
  18.2 5.2 %collective-permute-done.2.refs_3_ = f32[2,96,256]{2,1,0:T(8,128)S(1)} collective-permute-done((f32[2,96,256]{2,1,0:T(8,128)}, f32[2,96,256]{2,1,0:T(8,128)S(1)}, u32[]{:S(2)}, u32[]{:S(2)}) %collective-permute-start.2) | collective-permute-done | bytes 196640 | tf_op jit(solution)/shard_map/ppermute | solution.py:245
  24.1 2.3 shard_map.87
  26.4 4.3 %shard_map.88 = (f32[2,12,32,256]{3,2,1,0:T(8,128)}, f32[2,96,256]{2,1,0:T(8,128)}, f32[2,96,256]{2,1,0:T(8,128)}, f32[2,96,256]{2,1,0:T(8,128)}, f32[2,96,256]{2,1,0:T(8,128)}) custom-call(s32[3]{0:T(128)} %pad_add_fusion.refs_0_, s32[48]{0:T(128)} %reshape.31.refs_1_, f32[4,12,32,256]{3,2,1,0:T(8,128)} %refs_2_.3, f32[4,6,32,256]{3,2,1,0:T(8,128)} %copy-done.7, ...), custom_call_target="tpu_custom_call" | custom-call | flops 301989888 | bytes 1572864 | tf_op jit(solution)/shard_map/pallas_call | solution.py:272
  30.7 1.2 collective-permute-start.7
  31.9 1.6 collective-permute-start.4
  34.4 1.4 collective-permute-start.9
  35.8 2.6 collective-permute-start.5
  38.4 3.8 %collective-permute-start.6 = (f32[2,96,256]{2,1,0:T(8,128)S(1)}, f32[2,96,256]{2,1,0:T(8,128)S(1)}, u32[]{:S(2)}, u32[]{:S(2)}) collective-permute-start(f32[2,96,256]{2,1,0:T(8,128)S(1)} %copy-done.37), channel_id=1, source_target_pairs={{0,6},{1,7},{2,0},{3,1},{4,2},{5,3},{6,4},{7,5},{8,14},{9,15},{10,... | collective-permute-start | bytes 589832 | tf_op jit(solution)/shard_map/ppermute | solution.py:245
  42.2 1.2 collective-permute-done.8.refs_3_
  44.2 2.3 shard_map.89
  46.5 1.7 collective-permute-done.5.refs_3_
  48.9 2.2 shard_map.90.refs_1_
  51.8 1.3 collective-permute-start.11
  53.2 4.6 %collective-permute-start.12 = (f32[2,96,256]{2,1,0:T(8,128)S(1)}, f32[2,96,256]{2,1,0:T(8,128)S(1)}, u32[]{:S(2)}, u32[]{:S(2)}) collective-permute-start(f32[2,96,256]{2,1,0:T(8,128)S(1)} %copy-done.42), channel_id=1, source_target_pairs={{0,2},{1,3},{2,4},{3,5},{4,6},{5,7},{6,0},{7,1},{8,10},{9,11},{10,... | collective-permute-start | bytes 589832 | tf_op jit(solution)/shard_map/ppermute | solution.py:245
  57.7 1.8 collective-permute-start.13
  60.2 4.7 %collective-permute-done.12.refs_2_ = f32[2,96,256]{2,1,0:T(8,128)S(1)} collective-permute-done((f32[2,96,256]{2,1,0:T(8,128)S(1)}, f32[2,96,256]{2,1,0:T(8,128)S(1)}, u32[]{:S(2)}, u32[]{:S(2)}) %collective-permute-start.12) | collective-permute-done | bytes 196640 | tf_op jit(solution)/shard_map/ppermute | solution.py:245
  64.8 6.0 %collective-permute-done.13.refs_3_ = f32[2,96,256]{2,1,0:T(8,128)S(1)} collective-permute-done((f32[2,96,256]{2,1,0:T(8,128)S(1)}, f32[2,96,256]{2,1,0:T(8,128)S(1)}, u32[]{:S(2)}, u32[]{:S(2)}) %collective-permute-start.13) | collective-permute-done | bytes 196640 | tf_op jit(solution)/shard_map/ppermute | solution.py:245
  72.7 2.3 shard_map.91
  75.0 2.2 shard_map.92.refs_1_
  81.3 16.6 %collective-permute-done.17.refs_0_.refs_2_ = f32[2,4,96,256]{3,2,1,0:T(8,128)S(1)} collective-permute-done((f32[2,4,96,256]{3,2,1,0:T(8,128)}, f32[2,4,96,256]{3,2,1,0:T(8,128)S(1)}, u32[]{:S(2)}, u32[]{:S(2)}) %collective-permute-start.17) | collective-permute-done | bytes 786464 | tf_op jit(solution)/shard_map/ppermute | solution.py:245
  99.7 2.3 shard_map.93
  104.7 2.5 collective-permute-done.15.refs_4_
  108.7 4.6 %shard_map.94 = (bf16[2,1536,256]{2,1,0:T(8,128)(2,1)}, bf16[2,1536,256]{2,1,0:T(8,128)(2,1)}) custom-call(s32[3]{0:T(128)} %pad_add_fusion.refs_0_, f32[2,4,96,256]{3,2,1,0:T(8,128)} %shard_map.90.refs_1_, f32[2,4,96,256]{3,2,1,0:T(8,128)} %copy-done.3, f32[2,4,96,256]{3,2,1,0:T(8,128)} %copy-done.4, f32[1,4,96,256]{3,2,1,0:T(8,128)} %copy-done.18, ...), custom_call_target="tpu_custom_call" | custom-call | bytes 6291456 | tf_op jit(solution)/shard_map/pallas_call | solution.py:322
  115.8 4.4 %shard_map.95 = (bf16[2,1536,256]{2,1,0:T(8,128)(2,1)}, bf16[2,1536,256]{2,1,0:T(8,128)(2,1)}) custom-call(s32[3]{0:T(128)} %pad_add_fusion.refs_0_, f32[2,4,96,256]{3,2,1,0:T(8,128)} %shard_map.92.refs_1_, f32[2,4,96,256]{3,2,1,0:T(8,128)} %copy-done.5, f32[2,4,96,256]{3,2,1,0:T(8,128)} %copy-done.6, f32[1,4,96,256]{3,2,1,0:T(8,128)} %copy-done.19, ...), custom_call_target="tpu_custom_call" | custom-call | bytes 6291456 | tf_op jit(solution)/shard_map/pallas_call | solution.py:322
  120.2 13.3 %shard_map.96 = (f32[18,64,256]{2,1,0:T(8,128)}, f32[18,64,256]{2,1,0:T(8,128)}) custom-call(s32[1]{0:T(128)} %bitcast.5.info, s32[48]{0:T(128)} %compare_select_fusion.where.refs_0_, f32[12,256,1536]{2,1,0:T(8,128)} %bitcast.74, bf16[2,1536,256]{2,1,0:T(8,128)(2,1)} %get-tuple-element.61.refs_0_.refs_1_, ...), custom_call_target="tpu_custom_call" | custom-call | flops 14495514624 | bytes 4718592 | tf_op jit(solution)/shard_map/pallas_call | solution.py:164
  134.1 3.2 %collective-permute-done.22 = f32[18,64,256]{2,1,0:T(8,128)S(1)} collective-permute-done((f32[18,64,256]{2,1,0:T(8,128)}, f32[18,64,256]{2,1,0:T(8,128)S(1)}, u32[]{:S(2)}, u32[]{:S(2)}) %collective-permute-start.22) | collective-permute-done | bytes 1179680 | tf_op jit(solution)/shard_map/ppermute | solution.py:245
  137.3 1.4 add.189.refs_8_
  138.8 4.7 %collective-permute-start.26 = (f32[18,64,256]{2,1,0:T(8,128)S(1)}, f32[18,64,256]{2,1,0:T(8,128)}, u32[]{:S(2)}, u32[]{:S(2)}) collective-permute-start(f32[18,64,256]{2,1,0:T(8,128)S(1)} %add.189.refs_8_), channel_id=1, source_target_pairs={{0,2},{1,0},{2,4},{3,1},{4,6},{5,3},{6,7},{7,5},{8,10},{9,8},{10,1... | collective-permute-start | bytes 3538952 | tf_op jit(solution)/shard_map/ppermute | solution.py:245
  143.5 13.5 %shard_map.97 = (f32[18,64,256]{2,1,0:T(8,128)}, f32[18,64,256]{2,1,0:T(8,128)}) custom-call(s32[1]{0:T(128)} %bitcast.6.info, s32[48]{0:T(128)} %compare_select_fusion.where.refs_0_, f32[12,256,1536]{2,1,0:T(8,128)} %bitcast.75, bf16[2,1536,256]{2,1,0:T(8,128)(2,1)} %get-tuple-element.61.refs_0_.refs_1_, ...), custom_call_target="tpu_custom_call" | custom-call | flops 14495514624 | bytes 4718592 | tf_op jit(solution)/shard_map/pallas_call | solution.py:164
  157.2 1.6 add.185
  160.3 3.2 %add_select_fusion.2 = (f32[18,64,256]{2,1,0:T(8,128)}, f32[18,64,256]{2,1,0:T(8,128)S(1)}) fusion(f32[18,64,256]{2,1,0:T(8,128)} %collective-permute-done.26, f32[18,64,256]{2,1,0:T(8,128)S(1)} %copy-done.1, pred[]{:T(512)S(6)} %or.8, pred[]{:T(512)S(6)} %and.64, f32[18,64,256]{2,1,0:T(8,128)S(1)} %copy-done.11, f32[18,64,256]{2,1,0:T(8,128)} %collective-permute-done.25), kind=kLoop, calls=%fused_computation.2 | loop fusion | flops 1179648 | bytes 7077890 | tf_op jit(solution)/shard_map/jit(_where)/select_n | solution.py:354
  164.5 13.4 %shard_map.99 = (f32[18,64,256]{2,1,0:T(8,128)}, f32[18,64,256]{2,1,0:T(8,128)}) custom-call(s32[1]{0:T(128)} %bitcast.7.info, s32[48]{0:T(128)} %compare_select_fusion.where.refs_0_, f32[12,256,1536]{2,1,0:T(8,128)} %bitcast.76, bf16[2,1536,256]{2,1,0:T(8,128)(2,1)} %get-tuple-element.61.refs_0_.refs_1_, ...), custom_call_target="tpu_custom_call" | custom-call | flops 14495514624 | bytes 4718592 | tf_op jit(solution)/shard_map/pallas_call | solution.py:164
  177.9 1.4 add_select_fusion.3.refs_8_
  180.2 6.1 %collective-permute-done.28 = f32[18,64,256]{2,1,0:T(8,128)} collective-permute-done((f32[18,64,256]{2,1,0:T(8,128)}, f32[18,64,256]{2,1,0:T(8,128)}, u32[]{:S(2)}, u32[]{:S(2)}) %collective-permute-start.28) | collective-permute-done | bytes 1179680 | tf_op jit(solution)/shard_map/ppermute | solution.py:245
  186.3 2.3 add_select_fusion.1
  188.7 2.5 collective-permute-start.29
  191.2 7.8 %collective-permute-done.31 = f32[18,64,256]{2,1,0:T(8,128)} collective-permute-done((f32[18,64,256]{2,1,0:T(8,128)}, f32[18,64,256]{2,1,0:T(8,128)}, u32[]{:S(2)}, u32[]{:S(2)}) %collective-permute-start.31) | collective-permute-done | bytes 1179680 | tf_op jit(solution)/shard_map/ppermute | solution.py:245
  198.9 2.5 add_select_fusion
  201.5 2.5 collective-permute-start.32
  203.9 13.4 %shard_map.98 = (f32[18,64,256]{2,1,0:T(8,128)}, f32[18,64,256]{2,1,0:T(8,128)}) custom-call(s32[1]{0:T(128)} %bitcast.3.info, s32[48]{0:T(128)} %compare_select_fusion.where.refs_0_, f32[12,256,1536]{2,1,0:T(8,128)} %bitcast.77, bf16[2,1536,256]{2,1,0:T(8,128)(2,1)} %get-tuple-element.61.refs_0_.refs_1_, ...), custom_call_target="tpu_custom_call" | custom-call | flops 14495514624 | bytes 4718592 | tf_op jit(solution)/shard_map/pallas_call | solution.py:164
  217.4 6.8 %collective-permute-done.32.refs_4_ = f32[18,64,256]{2,1,0:T(8,128)S(1)} collective-permute-done((f32[18,64,256]{2,1,0:T(8,128)S(1)}, f32[18,64,256]{2,1,0:T(8,128)S(1)}, u32[]{:S(2)}, u32[]{:S(2)}) %collective-permute-start.32) | collective-permute-done | bytes 1179680 | tf_op jit(solution)/shard_map/ppermute | solution.py:245
  225.1 4.3 %shard_map.100 = (f32[36,32,256]{2,1,0:T(8,128)}, f32[36,32,256]{2,1,0:T(8,128)}) custom-call(s32[3]{0:T(128)} %pad_add_fusion.refs_0_, f32[18,64,256]{2,1,0:T(8,128)} %get-tuple-element.69.refs_1_, f32[18,64,256]{2,1,0:T(8,128)} %copy-done.9, f32[18,64,256]{2,1,0:T(8,128)} %get-tuple-element.72.refs_3_, f32[18,64,256]{2,1,0:T(8,128)} %copy-done.10), custom_call_target="tpu_custom_call" | custom-call | bytes 7077888 | tf_op jit(solution)/shard_map/pallas_call | solution.py:396
  230.1 2.7 collective-permute-done.33.refs_4_
  233.8 5.2 %shard_map.101 = (f32[4,12,32,256]{3,2,1,0:T(8,128)}, f32[4,256,256]{2,1,0:T(8,128)}) custom-call(s32[48]{0:T(128)} %compare_select_fusion.where.refs_0_, f32[2,12,32,256]{3,2,1,0:T(8,128)} %get-tuple-element.40.refs_1_, f32[2,12,32,256]{3,2,1,0:T(8,128)} %get-tuple-element.46.refs_2_, f32[36,32,256]{2,1,0:T(8,128)} %get-tuple-element.74.refs_3_, ...), custom_call_target="tpu_custom_call" | custom-call | flops 1207959552 | bytes 7864320 | tf_op jit(solution)/shard_map/pallas_call | solution.py:399
  239.0 1.2 dynamic-slice_bitcast_fusion
  240.6 1.5 collective-permute-done.34
  242.3 1.5 collective-permute-start.37
  243.8 1.2 collective-permute-start.36
  245.9 3.8 %collective-permute-done.37 = f32[128,256]{1,0:T(8,128)S(1)} collective-permute-done((f32[128,256]{1,0:T(8,128)S(1)}, f32[128,256]{1,0:T(8,128)S(1)}, u32[]{:S(2)}, u32[]{:S(2)}) %collective-permute-start.37) | collective-permute-done | bytes 131104 | tf_op jit(solution)/shard_map/ppermute | solution.py:245
  249.6 2.2 collective-permute-done.36
  251.9 2.5 collective-permute-start.40
  256.1 3.1 %collective-permute-done.39 = f32[32,256]{1,0:T(8,128)S(1)} collective-permute-done((f32[32,256]{1,0:T(8,128)S(1)}, f32[32,256]{1,0:T(8,128)S(1)}, u32[]{:S(2)}, u32[]{:S(2)}) %collective-permute-start.39) | collective-permute-done | bytes 32800 | tf_op jit(solution)/shard_map/ppermute | solution.py:245
  259.2 1.8 collective-permute-done.38
  261.8 3.2 %collective-permute-start.43 = (f32[32,256]{1,0:T(8,128)S(1)}, f32[32,256]{1,0:T(8,128)S(1)}, u32[]{:S(2)}, u32[]{:S(2)}) collective-permute-start(f32[32,256]{1,0:T(8,128)S(1)} %get-tuple-element.79), channel_id=1, source_target_pairs={{0,6},{1,7},{2,0},{3,1},{4,2},{5,3},{6,4},{7,5},{8,14},{9,15},{10,... | collective-permute-start | bytes 98312 | tf_op jit(solution)/shard_map/ppermute | solution.py:245
  265.0 1.9 collective-permute-done.41
  269.4 1.5 collective-permute-start.46
  271.0 1.4 collective-permute-done.44
  273.5 1.7 collective-permute-done.46
  275.4 1.9 collective-permute-done.47
  (165 shorter events, 37.9 us)
Async XLA Ops:
  1.9 2.4 collective-permute-start
  9.4 8.8 %collective-permute-start.1 = (f32[2,96,256]{2,1,0:T(8,128)}, f32[2,96,256]{2,1,0:T(8,128)S(1)}, u32[]{:S(2)}, u32[]{:S(2)}) collective-permute-start(f32[2,96,256]{2,1,0:T(8,128)} %get-tuple-element.42), channel_id=1, source_target_pairs={{0,8},{1,9},{2,10},{3,11},{4,12},{5,13},{6,14},{7,15},{8,0},{9,1},... | collective-permute-start | bytes 589832 | tf_op jit(solution)/shard_map/ppermute | solution.py:245
  12.3 11.1 %collective-permute-start.2 = (f32[2,96,256]{2,1,0:T(8,128)}, f32[2,96,256]{2,1,0:T(8,128)S(1)}, u32[]{:S(2)}, u32[]{:S(2)}) collective-permute-start(f32[2,96,256]{2,1,0:T(8,128)} %get-tuple-element.43), channel_id=1, source_target_pairs={{0,16},{1,17},{2,18},{3,19},{4,20},{5,21},{6,22},{7,23},{8,24},{9,... | collective-permute-start | bytes 589832 | tf_op jit(solution)/shard_map/ppermute | solution.py:245
  13.8 9.6 %collective-permute-start.3 = (f32[2,96,256]{2,1,0:T(8,128)}, f32[2,96,256]{2,1,0:T(8,128)S(1)}, u32[]{:S(2)}, u32[]{:S(2)}) collective-permute-start(f32[2,96,256]{2,1,0:T(8,128)} %get-tuple-element.44), channel_id=1, source_target_pairs={{0,24},{1,25},{2,26},{3,27},{4,28},{5,29},{6,30},{7,31},{8,16},{9,... | collective-permute-start | bytes 589832 | tf_op jit(solution)/shard_map/ppermute | solution.py:245
  18.2 5.2 %copy-start.25 = (f32[2,96,256]{2,1,0:T(8,128)}, f32[2,96,256]{2,1,0:T(8,128)S(1)}, u32[]{:S(2)}) copy-start(f32[2,96,256]{2,1,0:T(8,128)S(1)} %collective-permute-done.1.refs_2_) | copy-start | bytes 589828
  26.4 5.5 %copy-start.39 = (f32[2,96,256]{2,1,0:T(8,128)S(1)}, f32[2,96,256]{2,1,0:T(8,128)}, u32[]{:S(2)}) copy-start(f32[2,96,256]{2,1,0:T(8,128)} %get-tuple-element.47) | copy-start | bytes 589828
  26.4 9.4 %copy-start.38 = (f32[2,96,256]{2,1,0:T(8,128)S(1)}, f32[2,96,256]{2,1,0:T(8,128)}, u32[]{:S(2)}) copy-start(f32[2,96,256]{2,1,0:T(8,128)} %get-tuple-element.48) | copy-start | bytes 589828
  26.4 12.0 %copy-start.37 = (f32[2,96,256]{2,1,0:T(8,128)S(1)}, f32[2,96,256]{2,1,0:T(8,128)}, u32[]{:S(2)}) copy-start(f32[2,96,256]{2,1,0:T(8,128)} %get-tuple-element.49) | copy-start | bytes 589828
  30.7 7.7 %collective-permute-start.7 = (f32[2,96,256]{2,1,0:T(8,128)}, f32[2,96,256]{2,1,0:T(8,128)S(1)}, u32[]{:S(2)}, u32[]{:S(2)}) collective-permute-start(f32[2,96,256]{2,1,0:T(8,128)} %get-tuple-element.51), channel_id=1, source_target_pairs={{0,8},{1,9},{2,10},{3,11},{4,12},{5,13},{6,14},{7,15},{8,0},{9,1},... | collective-permute-start | bytes 589832 | tf_op jit(solution)/shard_map/ppermute | solution.py:245
  31.9 14.6 %collective-permute-start.4 = (f32[2,96,256]{2,1,0:T(8,128)S(1)}, f32[2,96,256]{2,1,0:T(8,128)S(1)}, u32[]{:S(2)}, u32[]{:S(2)}) collective-permute-start(f32[2,96,256]{2,1,0:T(8,128)S(1)} %copy-done.39), channel_id=1, source_target_pairs={{0,2},{1,3},{2,4},{3,5},{4,6},{5,7},{6,0},{7,1},{8,10},{9,11},{10,... | collective-permute-start | bytes 589832 | tf_op jit(solution)/shard_map/ppermute | solution.py:245
  33.5 10.0 %collective-permute-start.8 = (f32[2,96,256]{2,1,0:T(8,128)}, f32[2,96,256]{2,1,0:T(8,128)S(1)}, u32[]{:S(2)}, u32[]{:S(2)}) collective-permute-start(f32[2,96,256]{2,1,0:T(8,128)} %get-tuple-element.52), channel_id=1, source_target_pairs={{0,16},{1,17},{2,18},{3,19},{4,20},{5,21},{6,22},{7,23},{8,24},{9,... | collective-permute-start | bytes 589832 | tf_op jit(solution)/shard_map/ppermute | solution.py:245
  34.4 9.1 %collective-permute-start.9 = (f32[2,96,256]{2,1,0:T(8,128)}, f32[2,96,256]{2,1,0:T(8,128)S(1)}, u32[]{:S(2)}, u32[]{:S(2)}) collective-permute-start(f32[2,96,256]{2,1,0:T(8,128)} %get-tuple-element.53), channel_id=1, source_target_pairs={{0,24},{1,25},{2,26},{3,27},{4,28},{5,29},{6,30},{7,31},{8,16},{9,... | collective-permute-start | bytes 589832 | tf_op jit(solution)/shard_map/ppermute | solution.py:245
  35.8 12.3 %collective-permute-start.5 = (f32[2,96,256]{2,1,0:T(8,128)S(1)}, f32[2,96,256]{2,1,0:T(8,128)S(1)}, u32[]{:S(2)}, u32[]{:S(2)}) collective-permute-start(f32[2,96,256]{2,1,0:T(8,128)S(1)} %copy-done.38), channel_id=1, source_target_pairs={{0,4},{1,5},{2,6},{3,7},{4,0},{5,1},{6,2},{7,3},{8,12},{9,13},{10,... | collective-permute-start | bytes 589832 | tf_op jit(solution)/shard_map/ppermute | solution.py:245
  38.4 5.1 %copy-start.22 = (f32[2,96,256]{2,1,0:T(8,128)}, f32[2,96,256]{2,1,0:T(8,128)S(1)}, u32[]{:S(2)}) copy-start(f32[2,96,256]{2,1,0:T(8,128)S(1)} %collective-permute-done.7.refs_2_) | copy-start | bytes 589828
  38.4 9.8 %collective-permute-start.6 = (f32[2,96,256]{2,1,0:T(8,128)S(1)}, f32[2,96,256]{2,1,0:T(8,128)S(1)}, u32[]{:S(2)}, u32[]{:S(2)}) collective-permute-start(f32[2,96,256]{2,1,0:T(8,128)S(1)} %copy-done.37), channel_id=1, source_target_pairs={{0,6},{1,7},{2,0},{3,1},{4,2},{5,3},{6,4},{7,5},{8,14},{9,15},{10,... | collective-permute-start | bytes 589832 | tf_op jit(solution)/shard_map/ppermute | solution.py:245
  46.4 6.7 %copy-start.42 = (f32[2,96,256]{2,1,0:T(8,128)S(1)}, f32[2,96,256]{2,1,0:T(8,128)}, u32[]{:S(2)}) copy-start(f32[2,96,256]{2,1,0:T(8,128)} %get-tuple-element.55) | copy-start | bytes 589828
  46.4 11.3 %copy-start.41 = (f32[2,96,256]{2,1,0:T(8,128)S(1)}, f32[2,96,256]{2,1,0:T(8,128)}, u32[]{:S(2)}) copy-start(f32[2,96,256]{2,1,0:T(8,128)} %get-tuple-element.56) | copy-start | bytes 589828
  46.4 13.1 %copy-start.40 = (f32[2,96,256]{2,1,0:T(8,128)S(1)}, f32[2,96,256]{2,1,0:T(8,128)}, u32[]{:S(2)}) copy-start(f32[2,96,256]{2,1,0:T(8,128)} %get-tuple-element.57) | copy-start | bytes 589828
  51.1 19.8 %collective-permute-start.10 = (f32[2,4,96,256]{3,2,1,0:T(8,128)}, f32[2,4,96,256]{3,2,1,0:T(8,128)S(1)}, u32[]{:S(2)}, u32[]{:S(2)}) collective-permute-start(f32[2,4,96,256]{3,2,1,0:T(8,128)} %shard_map.90.refs_1_), channel_id=1, source_target_pairs={{0,8},{1,9},{2,10},{3,11},{4,12},{5,13},{6,14},{7,15},{8,0},{9,1},... | collective-permute-start | bytes 2359304 | tf_op jit(solution)/shard_map/ppermute | solution.py:245
  51.8 19.1 %collective-permute-start.11 = (f32[2,4,96,256]{3,2,1,0:T(8,128)}, f32[2,4,96,256]{3,2,1,0:T(8,128)S(1)}, u32[]{:S(2)}, u32[]{:S(2)}) collective-permute-start(f32[2,4,96,256]{3,2,1,0:T(8,128)} %shard_map.90.refs_1_), channel_id=1, source_target_pairs={{0,16},{1,17},{2,18},{3,19},{4,20},{5,21},{6,22},{7,23},{8,24},{9,... | collective-permute-start | bytes 2359304 | tf_op jit(solution)/shard_map/ppermute | solution.py:245
  53.2 11.7 %collective-permute-start.12 = (f32[2,96,256]{2,1,0:T(8,128)S(1)}, f32[2,96,256]{2,1,0:T(8,128)S(1)}, u32[]{:S(2)}, u32[]{:S(2)}) collective-permute-start(f32[2,96,256]{2,1,0:T(8,128)S(1)} %copy-done.42), channel_id=1, source_target_pairs={{0,2},{1,3},{2,4},{3,5},{4,6},{5,7},{6,0},{7,1},{8,10},{9,11},{10,... | collective-permute-start | bytes 589832 | tf_op jit(solution)/shard_map/ppermute | solution.py:245
  57.7 13.1 %collective-permute-start.13 = (f32[2,96,256]{2,1,0:T(8,128)S(1)}, f32[2,96,256]{2,1,0:T(8,128)S(1)}, u32[]{:S(2)}, u32[]{:S(2)}) collective-permute-start(f32[2,96,256]{2,1,0:T(8,128)S(1)} %copy-done.41), channel_id=1, source_target_pairs={{0,4},{1,5},{2,6},{3,7},{4,0},{5,1},{6,2},{7,3},{8,12},{9,13},{10,... | collective-permute-start | bytes 589832 | tf_op jit(solution)/shard_map/ppermute | solution.py:245
  59.5 11.3 %collective-permute-start.14 = (f32[2,96,256]{2,1,0:T(8,128)S(1)}, f32[2,96,256]{2,1,0:T(8,128)S(1)}, u32[]{:S(2)}, u32[]{:S(2)}) collective-permute-start(f32[2,96,256]{2,1,0:T(8,128)S(1)} %copy-done.40), channel_id=1, source_target_pairs={{0,6},{1,7},{2,0},{3,1},{4,2},{5,3},{6,4},{7,5},{8,14},{9,15},{10,... | collective-permute-start | bytes 589832 | tf_op jit(solution)/shard_map/ppermute | solution.py:245
  64.8 6.1 %copy-start.14 = (f32[2,96,256]{2,1,0:T(8,128)}, f32[2,96,256]{2,1,0:T(8,128)S(1)}, u32[]{:S(2)}) copy-start(f32[2,96,256]{2,1,0:T(8,128)S(1)} %collective-permute-done.12.refs_2_) | copy-start | bytes 589828
  75.0 4.2 %copy-start.17 = (f32[1,4,96,256]{3,2,1,0:T(8,128)S(1)}, f32[1,4,96,256]{3,2,1,0:T(8,128)}, u32[]{:S(2)}) copy-start(f32[1,4,96,256]{3,2,1,0:T(8,128)} %get-tuple-element.58.refs_5_) | copy-start | bytes 1179652
  75.0 5.2 %copy-start.36 = (f32[1,4,96,256]{3,2,1,0:T(8,128)S(1)}, f32[1,4,96,256]{3,2,1,0:T(8,128)}, u32[]{:S(2)}) copy-start(f32[1,4,96,256]{3,2,1,0:T(8,128)} %get-tuple-element.59) | copy-start | bytes 1179652
  77.2 26.8 %copy-start.31 = (s32[48]{0:T(128)S(1)}, s32[48]{0:T(128)}, u32[]{:S(2)}) copy-start(s32[48]{0:T(128)} %reshape.31.refs_1_) | copy-start | bytes 580
  77.2 20.6 %collective-permute-start.17 = (f32[2,4,96,256]{3,2,1,0:T(8,128)}, f32[2,4,96,256]{3,2,1,0:T(8,128)S(1)}, u32[]{:S(2)}, u32[]{:S(2)}) collective-permute-start(f32[2,4,96,256]{3,2,1,0:T(8,128)} %shard_map.92.refs_1_), channel_id=1, source_target_pairs={{0,8},{1,9},{2,10},{3,11},{4,12},{5,13},{6,14},{7,15},{8,0},{9,1},... | collective-permute-start | bytes 2359304 | tf_op jit(solution)/shard_map/ppermute | solution.py:245
  78.1 20.7 %collective-permute-start.18 = (f32[2,4,96,256]{3,2,1,0:T(8,128)}, f32[2,4,96,256]{3,2,1,0:T(8,128)S(1)}, u32[]{:S(2)}, u32[]{:S(2)}) collective-permute-start(f32[2,4,96,256]{3,2,1,0:T(8,128)} %shard_map.92.refs_1_), channel_id=1, source_target_pairs={{0,16},{1,17},{2,18},{3,19},{4,20},{5,21},{6,22},{7,23},{8,24},{9,... | collective-permute-start | bytes 2359304 | tf_op jit(solution)/shard_map/ppermute | solution.py:245
  79.2 28.0 %collective-permute-start.15 = (f32[1,4,96,256]{3,2,1,0:T(8,128)S(1)}, f32[1,4,96,256]{3,2,1,0:T(8,128)S(1)}, u32[]{:S(2)}, u32[]{:S(2)}) collective-permute-start(f32[1,4,96,256]{3,2,1,0:T(8,128)S(1)} %copy-done.17), channel_id=1, source_target_pairs={{0,16},{1,17},{2,18},{3,19},{4,20},{5,21},{6,22},{7,23},{8,24},{9,... | collective-permute-start | bytes 1179656 | tf_op jit(solution)/shard_map/ppermute | solution.py:245
  80.1 27.1 %collective-permute-start.16 = (f32[1,4,96,256]{3,2,1,0:T(8,128)S(1)}, f32[1,4,96,256]{3,2,1,0:T(8,128)S(1)}, u32[]{:S(2)}, u32[]{:S(2)}) collective-permute-start(f32[1,4,96,256]{3,2,1,0:T(8,128)S(1)} %copy-done.36), channel_id=1, source_target_pairs={{0,8},{1,9},{2,10},{3,11},{4,12},{5,13},{6,14},{7,15},{8,0},{9,1},... | collective-permute-start | bytes 1179656 | tf_op jit(solution)/shard_map/ppermute | solution.py:245
  102.0 12.2 %collective-permute-start.19 = (f32[1,4,96,256]{3,2,1,0:T(8,128)}, f32[1,4,96,256]{3,2,1,0:T(8,128)S(1)}, u32[]{:S(2)}, u32[]{:S(2)}) collective-permute-start(f32[1,4,96,256]{3,2,1,0:T(8,128)} %get-tuple-element.60.refs_6_), channel_id=1, source_target_pairs={{0,16},{1,17},{2,18},{3,19},{4,20},{5,21},{6,22},{7,23},{8,24},{9,... | collective-permute-start | bytes 1179656 | tf_op jit(solution)/shard_map/ppermute | solution.py:245
  103.1 11.1 %collective-permute-start.20 = (f32[1,4,96,256]{3,2,1,0:T(8,128)}, f32[1,4,96,256]{3,2,1,0:T(8,128)S(1)}, u32[]{:S(2)}, u32[]{:S(2)}) collective-permute-start(f32[1,4,96,256]{3,2,1,0:T(8,128)} %get-tuple-element.62), channel_id=1, source_target_pairs={{0,8},{1,9},{2,10},{3,11},{4,12},{5,13},{6,14},{7,15},{8,0},{9,1},... | collective-permute-start | bytes 1179656 | tf_op jit(solution)/shard_map/ppermute | solution.py:245
  133.6 3.8 %collective-permute-start.22 = (f32[18,64,256]{2,1,0:T(8,128)}, f32[18,64,256]{2,1,0:T(8,128)S(1)}, u32[]{:S(2)}, u32[]{:S(2)}) collective-permute-start(f32[18,64,256]{2,1,0:T(8,128)} %get-tuple-element.67), channel_id=1, source_target_pairs={{0,1},{1,0},{2,3},{3,2},{4,5},{5,4},{6,7},{7,6},{8,9},{9,8},{10,11... | collective-permute-start | bytes 3538952 | tf_op jit(solution)/shard_map/ppermute | solution.py:245
  133.7 23.5 %collective-permute-start.21 = (f32[18,64,256]{2,1,0:T(8,128)}, f32[18,64,256]{2,1,0:T(8,128)}, u32[]{:S(2)}, u32[]{:S(2)}) collective-permute-start(f32[18,64,256]{2,1,0:T(8,128)} %get-tuple-element.66), channel_id=1, source_target_pairs={{0,1},{1,0},{2,3},{3,2},{4,5},{5,4},{6,7},{7,6},{8,9},{9,8},{10,11... | collective-permute-start | bytes 3538952 | tf_op jit(solution)/shard_map/ppermute | solution.py:245
  138.8 4.7 %copy-start = (f32[18,64,256]{2,1,0:T(8,128)}, f32[18,64,256]{2,1,0:T(8,128)S(1)}, u32[]{:S(2)}) copy-start(f32[18,64,256]{2,1,0:T(8,128)S(1)} %add.189.refs_8_) | copy-start | bytes 3538948
  138.8 21.1 %collective-permute-start.26 = (f32[18,64,256]{2,1,0:T(8,128)S(1)}, f32[18,64,256]{2,1,0:T(8,128)}, u32[]{:S(2)}, u32[]{:S(2)}) collective-permute-start(f32[18,64,256]{2,1,0:T(8,128)S(1)} %add.189.refs_8_), channel_id=1, source_target_pairs={{0,2},{1,0},{2,4},{3,1},{4,6},{5,3},{6,7},{7,5},{8,10},{9,8},{10,1... | collective-permute-start | bytes 3538952 | tf_op jit(solution)/shard_map/ppermute | solution.py:245
  143.5 13.7 %copy-start.8 = (f32[18,64,256]{2,1,0:T(8,128)S(1)}, f32[18,64,256]{2,1,0:T(8,128)}, u32[]{:S(2)}) copy-start(f32[18,64,256]{2,1,0:T(8,128)} %get-tuple-element.66) | copy-start | bytes 3538948
  157.0 3.3 %collective-permute-start.25 = (f32[18,64,256]{2,1,0:T(8,128)}, f32[18,64,256]{2,1,0:T(8,128)}, u32[]{:S(2)}, u32[]{:S(2)}) collective-permute-start(f32[18,64,256]{2,1,0:T(8,128)} %get-tuple-element.70), channel_id=1, source_target_pairs={{0,1},{1,0},{2,3},{3,2},{4,5},{5,4},{6,7},{7,6},{8,9},{9,8},{10,11... | collective-permute-start | bytes 3538952 | tf_op jit(solution)/shard_map/ppermute | solution.py:245
  158.8 19.1 %collective-permute-start.24 = (f32[18,64,256]{2,1,0:T(8,128)S(1)}, f32[18,64,256]{2,1,0:T(8,128)S(1)}, u32[]{:S(2)}, u32[]{:S(2)}) collective-permute-start(f32[18,64,256]{2,1,0:T(8,128)S(1)} %add.185), channel_id=1, source_target_pairs={{0,2},{1,0},{2,4},{3,1},{4,6},{5,3},{6,7},{7,5},{8,10},{9,8},{10,1... | collective-permute-start | bytes 3538952 | tf_op jit(solution)/shard_map/ppermute | solution.py:245
  159.8 18.1 %collective-permute-start.23 = (f32[18,64,256]{2,1,0:T(8,128)S(1)}, f32[18,64,256]{2,1,0:T(8,128)S(1)}, u32[]{:S(2)}, u32[]{:S(2)}) collective-permute-start(f32[18,64,256]{2,1,0:T(8,128)S(1)} %copy-done.2), channel_id=1, source_target_pairs={{0,1},{1,0},{2,3},{3,2},{4,5},{5,4},{6,7},{7,6},{8,9},{9,8},{10,11... | collective-permute-start | bytes 3538952 | tf_op jit(solution)/shard_map/ppermute | solution.py:245
  163.4 22.9 %collective-permute-start.28 = (f32[18,64,256]{2,1,0:T(8,128)}, f32[18,64,256]{2,1,0:T(8,128)}, u32[]{:S(2)}, u32[]{:S(2)}) collective-permute-start(f32[18,64,256]{2,1,0:T(8,128)} %get-tuple-element.80.refs_8_), channel_id=1, source_target_pairs={{0,2},{1,0},{2,4},{3,1},{4,6},{5,3},{6,7},{7,5},{8,10},{9,8},{10,1... | collective-permute-start | bytes 3538952 | tf_op jit(solution)/shard_map/ppermute | solution.py:245
  177.8 8.5 %collective-permute-start.27 = (f32[18,64,256]{2,1,0:T(8,128)}, f32[18,64,256]{2,1,0:T(8,128)}, u32[]{:S(2)}, u32[]{:S(2)}) collective-permute-start(f32[18,64,256]{2,1,0:T(8,128)} %get-tuple-element.71), channel_id=1, source_target_pairs={{0,1},{1,0},{2,3},{3,2},{4,5},{5,4},{6,7},{7,6},{8,9},{9,8},{10,11... | collective-permute-start | bytes 3538952 | tf_op jit(solution)/shard_map/ppermute | solution.py:245
  179.3 19.6 %collective-permute-start.31 = (f32[18,64,256]{2,1,0:T(8,128)}, f32[18,64,256]{2,1,0:T(8,128)}, u32[]{:S(2)}, u32[]{:S(2)}) collective-permute-start(f32[18,64,256]{2,1,0:T(8,128)} %add_select_fusion.3.refs_8_), channel_id=1, source_target_pairs={{0,2},{1,0},{2,4},{3,1},{4,6},{5,3},{6,7},{7,5},{8,10},{9,8},{10,1... | collective-permute-start | bytes 3538952 | tf_op jit(solution)/shard_map/ppermute | solution.py:245
  180.2 18.8 %collective-permute-start.30 = (f32[18,64,256]{2,1,0:T(8,128)}, f32[18,64,256]{2,1,0:T(8,128)}, u32[]{:S(2)}, u32[]{:S(2)}) collective-permute-start(f32[18,64,256]{2,1,0:T(8,128)} %get-tuple-element.73), channel_id=1, source_target_pairs={{0,1},{1,0},{2,3},{3,2},{4,5},{5,4},{6,7},{7,6},{8,9},{9,8},{10,11... | collective-permute-start | bytes 3538952 | tf_op jit(solution)/shard_map/ppermute | solution.py:245
  188.7 28.7 %collective-permute-start.29 = (f32[18,64,256]{2,1,0:T(8,128)S(1)}, f32[18,64,256]{2,1,0:T(8,128)S(1)}, u32[]{:S(2)}, u32[]{:S(2)}) collective-permute-start(f32[18,64,256]{2,1,0:T(8,128)S(1)} %add_select_fusion.1), channel_id=1, source_target_pairs={{0,2},{1,0},{2,4},{3,1},{4,6},{5,3},{6,7},{7,5},{8,10},{9,8},{10,1... | collective-permute-start | bytes 3538952 | tf_op jit(solution)/shard_map/ppermute | solution.py:245
  201.5 22.7 %collective-permute-start.32 = (f32[18,64,256]{2,1,0:T(8,128)S(1)}, f32[18,64,256]{2,1,0:T(8,128)S(1)}, u32[]{:S(2)}, u32[]{:S(2)}) collective-permute-start(f32[18,64,256]{2,1,0:T(8,128)S(1)} %add_select_fusion), channel_id=1, source_target_pairs={{0,2},{1,0},{2,4},{3,1},{4,6},{5,3},{6,7},{7,5},{8,10},{9,8},{10,1... | collective-permute-start | bytes 3538952 | tf_op jit(solution)/shard_map/ppermute | solution.py:245
  217.4 6.8 %copy-start.9 = (f32[18,64,256]{2,1,0:T(8,128)}, f32[18,64,256]{2,1,0:T(8,128)S(1)}, u32[]{:S(2)}) copy-start(f32[18,64,256]{2,1,0:T(8,128)S(1)} %collective-permute-done.29.refs_2_) | copy-start | bytes 3538948
  229.4 3.4 %collective-permute-start.33 = (f32[36,32,256]{2,1,0:T(8,128)}, f32[36,32,256]{2,1,0:T(8,128)S(1)}, u32[]{:S(2)}, u32[]{:S(2)}) collective-permute-start(f32[36,32,256]{2,1,0:T(8,128)} %get-tuple-element.75), channel_id=1, source_target_pairs={{0,1},{1,0},{2,3},{3,2},{4,5},{5,4},{6,7},{7,6},{8,9},{9,8},{10,11... | collective-permute-start | bytes 3538952 | tf_op jit(solution)/shard_map/ppermute | solution.py:245
  240.2 2.0 collective-permute-start.34
  242.3 7.3 %collective-permute-start.37 = (f32[128,256]{1,0:T(8,128)S(1)}, f32[128,256]{1,0:T(8,128)S(1)}, u32[]{:S(2)}, u32[]{:S(2)}) collective-permute-start(f32[128,256]{1,0:T(8,128)S(1)} %get-tuple-element.85), channel_id=1, source_target_pairs={{0,24},{1,25},{2,26},{3,27},{4,28},{5,29},{6,30},{7,31},{8,16},{9,... | collective-permute-start | bytes 393224 | tf_op jit(solution)/shard_map/ppermute | solution.py:245
  243.8 8.1 %collective-permute-start.36 = (f32[128,256]{1,0:T(8,128)S(1)}, f32[128,256]{1,0:T(8,128)S(1)}, u32[]{:S(2)}, u32[]{:S(2)}) collective-permute-start(f32[128,256]{1,0:T(8,128)S(1)} %get-tuple-element.86), channel_id=1, source_target_pairs={{0,16},{1,17},{2,18},{3,19},{4,20},{5,21},{6,22},{7,23},{8,24},{9,... | collective-permute-start | bytes 393224 | tf_op jit(solution)/shard_map/ppermute | solution.py:245
  244.9 6.9 %collective-permute-start.35 = (f32[128,256]{1,0:T(8,128)S(1)}, f32[128,256]{1,0:T(8,128)S(1)}, u32[]{:S(2)}, u32[]{:S(2)}) collective-permute-start(f32[128,256]{1,0:T(8,128)S(1)} %get-tuple-element.84), channel_id=1, source_target_pairs={{0,8},{1,9},{2,10},{3,11},{4,12},{5,13},{6,14},{7,15},{8,0},{9,1},... | collective-permute-start | bytes 393224 | tf_op jit(solution)/shard_map/ppermute | solution.py:245
  251.9 4.2 %collective-permute-start.40 = (f32[32,256]{1,0:T(8,128)S(1)}, f32[32,256]{1,0:T(8,128)S(1)}, u32[]{:S(2)}, u32[]{:S(2)}) collective-permute-start(f32[32,256]{1,0:T(8,128)S(1)} %get-tuple-element.88), channel_id=1, source_target_pairs={{0,6},{1,7},{2,0},{3,1},{4,2},{5,3},{6,4},{7,5},{8,14},{9,15},{10,... | collective-permute-start | bytes 98312 | tf_op jit(solution)/shard_map/ppermute | solution.py:245
  254.4 4.8 %collective-permute-start.39 = (f32[32,256]{1,0:T(8,128)S(1)}, f32[32,256]{1,0:T(8,128)S(1)}, u32[]{:S(2)}, u32[]{:S(2)}) collective-permute-start(f32[32,256]{1,0:T(8,128)S(1)} %get-tuple-element.89), channel_id=1, source_target_pairs={{0,4},{1,5},{2,6},{3,7},{4,0},{5,1},{6,2},{7,3},{8,12},{9,13},{10,... | collective-permute-start | bytes 98312 | tf_op jit(solution)/shard_map/ppermute | solution.py:245
  255.3 5.7 %collective-permute-start.38 = (f32[32,256]{1,0:T(8,128)S(1)}, f32[32,256]{1,0:T(8,128)S(1)}, u32[]{:S(2)}, u32[]{:S(2)}) collective-permute-start(f32[32,256]{1,0:T(8,128)S(1)} %get-tuple-element.87), channel_id=1, source_target_pairs={{0,2},{1,3},{2,4},{3,5},{4,6},{5,7},{6,0},{7,1},{8,10},{9,11},{10,... | collective-permute-start | bytes 98312 | tf_op jit(solution)/shard_map/ppermute | solution.py:245
  261.1 5.8 %collective-permute-start.41 = (f32[32,256]{1,0:T(8,128)S(1)}, f32[32,256]{1,0:T(8,128)S(1)}, u32[]{:S(2)}, u32[]{:S(2)}) collective-permute-start(f32[32,256]{1,0:T(8,128)S(1)} %get-tuple-element.79), channel_id=1, source_target_pairs={{0,2},{1,3},{2,4},{3,5},{4,6},{5,7},{6,0},{7,1},{8,10},{9,11},{10,... | collective-permute-start | bytes 98312 | tf_op jit(solution)/shard_map/ppermute | solution.py:245
  261.2 5.6 %collective-permute-start.42 = (f32[32,256]{1,0:T(8,128)S(1)}, f32[32,256]{1,0:T(8,128)S(1)}, u32[]{:S(2)}, u32[]{:S(2)}) collective-permute-start(f32[32,256]{1,0:T(8,128)S(1)} %get-tuple-element.79), channel_id=1, source_target_pairs={{0,4},{1,5},{2,6},{3,7},{4,0},{5,1},{6,2},{7,3},{8,12},{9,13},{10,... | collective-permute-start | bytes 98312 | tf_op jit(solution)/shard_map/ppermute | solution.py:245
  261.8 5.7 %collective-permute-start.43 = (f32[32,256]{1,0:T(8,128)S(1)}, f32[32,256]{1,0:T(8,128)S(1)}, u32[]{:S(2)}, u32[]{:S(2)}) collective-permute-start(f32[32,256]{1,0:T(8,128)S(1)} %get-tuple-element.79), channel_id=1, source_target_pairs={{0,6},{1,7},{2,0},{3,1},{4,2},{5,3},{6,4},{7,5},{8,14},{9,15},{10,... | collective-permute-start | bytes 98312 | tf_op jit(solution)/shard_map/ppermute | solution.py:245
  267.4 5.0 %collective-permute-start.44 = (f32[128,256]{1,0:T(8,128)S(1)}, f32[128,256]{1,0:T(8,128)S(1)}, u32[]{:S(2)}, u32[]{:S(2)}) collective-permute-start(f32[128,256]{1,0:T(8,128)S(1)} %bitcast.68), channel_id=1, source_target_pairs={{0,8},{1,9},{2,10},{3,11},{4,12},{5,13},{6,14},{7,15},{8,0},{9,1},... | collective-permute-start | bytes 393224 | tf_op jit(solution)/shard_map/ppermute | solution.py:245
  268.5 5.0 %collective-permute-start.45 = (f32[128,256]{1,0:T(8,128)S(1)}, f32[128,256]{1,0:T(8,128)S(1)}, u32[]{:S(2)}, u32[]{:S(2)}) collective-permute-start(f32[128,256]{1,0:T(8,128)S(1)} %bitcast.69), channel_id=1, source_target_pairs={{0,16},{1,17},{2,18},{3,19},{4,20},{5,21},{6,22},{7,23},{8,24},{9,... | collective-permute-start | bytes 393224 | tf_op jit(solution)/shard_map/ppermute | solution.py:245
  269.4 5.9 %collective-permute-start.46 = (f32[128,256]{1,0:T(8,128)S(1)}, f32[128,256]{1,0:T(8,128)S(1)}, u32[]{:S(2)}, u32[]{:S(2)}) collective-permute-start(f32[128,256]{1,0:T(8,128)S(1)} %bitcast.70), channel_id=1, source_target_pairs={{0,24},{1,25},{2,26},{3,27},{4,28},{5,29},{6,30},{7,31},{8,16},{9,... | collective-permute-start | bytes 393224 | tf_op jit(solution)/shard_map/ppermute | solution.py:245
  273.5 3.8 %copy-start.12 = (f32[4,256,256]{2,1,0:T(8,128)S(1)}, f32[4,256,256]{2,1,0:T(8,128)}, u32[]{:S(2)}) copy-start(f32[4,256,256]{2,1,0:T(8,128)} %param.10) | copy-start | bytes 3145732
  275.3 2.0 collective-permute-start.47
  (27 other events, 34.7 us)

commit v4 on v3

--- a/solution.py
+++ b/solution.py
@@ -16,17 +16,20 @@
     return pl.BlockSpec(memory_space=memory_space)
 
 
-def call(kernel, outs, scratch=(), n_scalar=1, n_in=1, n_after=0, flops=0, moved=0):
+def call(kernel, outs, scratch=(), n_scalar=1, n_in=1, n_after=0, n_gated=0, flops=0, moved=0):
     used = n_scalar + n_in
+    made = len(outs) - n_gated
 
     def body(*refs):
-        kernel(*refs[:used], *refs[used + n_after :])
+        rest = refs[used + n_after :]
+        kernel(*refs[:used], *rest[:made], *rest[made + n_gated :])
 
     return pl.pallas_call(
         body,
         out_shape=outs,
         in_specs=[whole(pltpu.SMEM)] * n_scalar + [whole()] * n_in + [whole(pl.ANY)] * n_after,
-        out_specs=jax.tree.map(lambda _: whole(), outs),
+        out_specs=[whole()] * made + [whole(pl.ANY)] * n_gated,
+        input_output_aliases={used + k: made + k for k in range(n_gated)},
         scratch_shapes=list(scratch),
         compiler_params=pltpu.CompilerParams(vmem_limit_bytes=VMEM_LIMIT),
         cost_estimate=pl.CostEstimate(flops=flops, bytes_accessed=moved, transcendentals=0),
@@ -84,11 +87,6 @@
 def stack_kernel(place, *refs):
     for m in range(len(refs) - 1):
         refs[-1][:, m] = refs[m][...]
-
-
-def halves_kernel(first_ref, second_ref, first_half, second_half):
-    first_half[...] = first_ref[:1]
-    second_half[...] = second_ref[1:]
 
 
 def assemble_kernel(lines, rb, place, *refs):
@@ -185,27 +183,24 @@
     )(info, where, g3, *[x[0] for x in xs], *[x[1] for x in xs], *after)
 
 
-def merge_kernel(bounds, lines, place, *refs):
-    mine, other = refs[-2:]
+def merge_kernel(lines, place, own_ref, arrived_ref, mine, other):
     rb = mine.shape[1]
     from_others = place[1] != jnp.where(place[2] == 0, 0, lines - 1)
     for core in range(2):
         rows = slice(core * rb, (core + 1) * rb)
 
         def fill(out, rows=rows):
-            for k in range(len(bounds) - 1):
-                arrived = jnp.where(from_others, refs[2 * k + 1][:, rows, :], 0.0)
-                value = refs[2 * k][:, rows, :] + arrived
-                out[bounds[k] : bounds[k + 1]] = value
+            out[...] = own_ref[:, rows, :] + jnp.where(from_others, arrived_ref[:, rows, :], 0.0)
 
         pl.when(place[2] == core)(functools.partial(fill, mine))
         pl.when(place[2] != core)(functools.partial(fill, other))
 
 
-def finish_kernel(groups, where, *refs):
+def finish_kernel(groups, bounds, where, *refs):
     n_refs, refs = refs[: len(groups)], refs[len(groups) :]
-    mine, swapped, panel_ref, diag_ref, total = refs
-    total[...] = mine[...] + swapped[...]
+    panel_ref, diag_ref, total = refs[-3:]
+    for k in range(len(bounds) - 1):
+        total[bounds[k] : bounds[k + 1]] = refs[2 * k][...] + refs[2 * k + 1][...]
     panels, slots, rb, width = panel_ref.shape
     n_of = {p: n_refs[g][at] for g, group in enumerate(groups) for at, p in enumerate(group)}
     for p in range(panels):
@@ -280,18 +275,22 @@
         parts_of.append(made[1:])
 
     partner = swap(lax.dynamic_slice_in_dim(factor_blocks, (1 - h) * halves, halves, 1))
-    spread = []
     for g, group in enumerate(groups):
-        normalize(group, spread)
+        normalize(group, normalized[-1:])
+    for g, group in enumerate(groups):
         parts = parts_of[g]
-        moved = 8 * lines * math.prod(parts[0].shape)
+        part = jax.ShapeDtypeStruct(parts[0].shape, f32)
         held = [parts[0]] + [across(parts[d], d) for d in range(1, lines)]
+        gated = parts_of[g + 1] if g + 1 < len(groups) else []
         outgoing = call(
             functools.partial(to_planes_kernel, lines),
-            [jax.ShapeDtypeStruct(parts[0].shape, f32)] * lines, n_in=lines, moved=moved,
-        )(place, *held)
-        spread = [outgoing[0]]
-        planes.append(outgoing)
+            [part] * lines + [jax.ShapeDtypeStruct(v.shape, f32) for v in gated],
+            n_in=lines, n_after=len(gated), n_gated=len(gated), moved=8 * lines * parts[0].size,
+        )(place, *held, *gated)
+        planes.append(outgoing[:lines])
+        if gated:
+            parts_of[g + 1] = outgoing[lines:]
+
     along_planes = [
         [outgoing[0]] + [along(outgoing[m], m) for m in range(1, lines)] for outgoing in planes
     ]
@@ -305,14 +304,8 @@
         )(place, *held, *after)
         pieces = [both] + [across(both, d) for d in range(1, lines)]
         if lines == 4:
-            half_shape = jax.ShapeDtypeStruct((1,) + both.shape[1:], f32)
-            before = along_planes[g + 1][1:] if g + 1 < len(groups) else []
-            split_pair = call(
-                halves_kernel, [half_shape, half_shape], n_scalar=0, n_in=2,
-                n_after=len(before), moved=8 * both.size // 2,
-            )(pieces[1], pieces[2], *before)
-            pieces[3:] = [across(split_pair[0], 2), across(split_pair[1], 1)]
-            halved.append(split_pair[0])
+            pieces[3:] = [across(pieces[1][:1], 2), across(pieces[2][1:], 1)]
+        halved.append(pieces[1])
         stacked.append(both)
         gathered.append(pieces)
 
@@ -389,22 +382,22 @@
         after = move(1, step)
         if step == lines - 3:
             compute(after)
-    made_0, made_1 = made
-    moving_0, moving_1 = moving
-
-    half_rows = jax.ShapeDtypeStruct((keep, rb, width), f32)
-    mine, other = call(
-        functools.partial(merge_kernel, bounds, lines), [half_rows, half_rows], n_in=4, moved=24 * keep * rb * width
-    )(place, made_0[-1][0], moving_0[-1], made_1[-1][0], moving_1[-1])
+    finals = []
+    for k in range(2):
+        half_rows = jax.ShapeDtypeStruct((bounds[k + 1] - bounds[k], rb, width), f32)
+        mine, other = call(
+            functools.partial(merge_kernel, lines), [half_rows, half_rows], n_in=2, moved=12 * keep * rb * width
+        )(place, made[k][-1][0], moving[k][-1])
+        finals += [mine, swap(other)]
     panel_inverse, terms = call(
-        functools.partial(finish_kernel, groups),
+        functools.partial(finish_kernel, groups, bounds),
         [
             jax.ShapeDtypeStruct(factor_blocks.shape, f32),
             jax.ShapeDtypeStruct(factor_inverse.shape, f32),
         ],
         [pltpu.VMEM((keep, rb, width), f32)],
-        n_in=len(groups) + 2, flops=12 * factor_blocks.size * width, moved=20 * factor_blocks.size,
-    )(where, *normalized, mine, swap(other))
+        n_in=len(groups) + len(finals), flops=12 * factor_blocks.size * width, moved=20 * factor_blocks.size,
+    )(where, *normalized, *finals)
 
     pick = lambda value, at: lax.dynamic_index_in_dim(value, at, 0, False)
     two = terms.reshape(2, half * width, width)

time: 279 us -> 268 us (0.961)
  waiting for transfers between devices: 92.6 us -> 83.7 us
  Pallas kernels: 94.1 us -> 90.8 us
    ppermute x48 -> x49, waiting for transfers between devices: 92.6 us -> 83.7 us  [send(): return lax.ppermute(value, AXES, pairs)]
    pallas_call x6 -> x5, Pallas kernels: 18.6 us -> 15.5 us  [the longest x2 5.83 us: on_device(): call(functools.partial(merge_kernel, lines), [half_rows, half_rows], n_in...]
    unnamed x86 -> x74, local copies, waits for them, and re-layouts: 10.9 us -> 8.42 us
    ppermute x48 -> x49, starting transfers between devices: 61.1 us -> 62.7 us  [send(): return lax.ppermute(value, AXES, pairs)]
  transfers between devices with their start and end apart: 48 -> 49, of which waited for: 31 -> 29; matrix products, arithmetic and copies ran while one was open for 5% -> 6% of each run, Pallas kernels for 18% -> 22%
where the time goes in v4:
time: 268 us; the launch traced here: 267 us
  Pallas kernels  90.8 us (34%)
  waiting for transfers between devices  83.7 us (31%)
  starting transfers between devices  62.7 us (23%)
  other arithmetic  15.4 us (6%)
  local copies, waits for them, and re-layouts  13.6 us (5%)
    ppermute x49, waiting for transfers between devices, send(): return lax.ppermute(value, AXES, pairs)  83.7 us
    ppermute x49, starting transfers between devices, send(): return lax.ppermute(value, AXES, pairs)  62.7 us
    pallas_call x4, Pallas kernels, product(): pl.pallas_call(functools.partial(product_kernel, len(xs), slots, bounds,...  53.5 us
    select_n x4, other arithmetic, add_arrived(): jnp.where((behind > 0) & (behind <= step + 1), value + arrived, value)  9.37 us
    pallas_call x2, Pallas kernels, assemble(): call(functools.partial(assemble_kernel, lines, rb), [block, block], [pltp...  9.07 us
    pallas_call x2, Pallas kernels, normalize(): call(functools.partial(normalize_kernel, group, lines), [rows_made] + [ja...  8.5 us
    unnamed x74, local copies, waits for them, and re-layouts  8.42 us
    pallas_call x2, Pallas kernels, on_device(): call(functools.partial(merge_kernel, lines), [half_rows, half_rows], n_in...  5.83 us
  transfers between devices with their start and end apart: 49, of which 29 were waited for; matrix products, arithmetic and copies ran while one was open for 6% of the time, Pallas kernels for 22%

profile of v4, /device:TPU:0, one launch (start us, length us, event | category | flops | bytes accessed | tf_op | source)
XLA Modules:
  0.0 267.4 jit_solution(12871371000731475835)
XLA Ops:
  0.7 1.2 constant_dynamic-slice_fusion
  5.2 4.2 %shard_map.86 = (f32[2,12,32,256]{3,2,1,0:T(8,128)}, f32[2,96,256]{2,1,0:T(8,128)}, f32[2,96,256]{2,1,0:T(8,128)}, f32[2,96,256]{2,1,0:T(8,128)}, f32[2,96,256]{2,1,0:T(8,128)}) custom-call(s32[3]{0:T(128)} %pad_add_fusion.refs_0_, s32[48]{0:T(128)} %reshape.31.refs_1_, f32[4,12,32,256]{3,2,1,0:T(8,128)} %refs_2_.3, f32[4,6,32,256]{3,2,1,0:T(8,128)} %copy-done.5, ...), custom_call_target="tpu_custom_call" | custom-call | flops 301989888 | bytes 1572864 | tf_op jit(solution)/shard_map/pallas_call | solution.py:267
  9.4 2.9 %collective-permute-start.1 = (f32[2,96,256]{2,1,0:T(8,128)}, f32[2,96,256]{2,1,0:T(8,128)S(1)}, u32[]{:S(2)}, u32[]{:S(2)}) collective-permute-start(f32[2,96,256]{2,1,0:T(8,128)} %get-tuple-element.45), channel_id=1, source_target_pairs={{0,8},{1,9},{2,10},{3,11},{4,12},{5,13},{6,14},{7,15},{8,0},{9,1},... | collective-permute-start | bytes 589832 | tf_op jit(solution)/shard_map/ppermute | solution.py:240
  12.3 1.5 collective-permute-start.2
  13.8 4.3 %shard_map.87 = (f32[2,12,32,256]{3,2,1,0:T(8,128)}, f32[2,96,256]{2,1,0:T(8,128)}, f32[2,96,256]{2,1,0:T(8,128)}, f32[2,96,256]{2,1,0:T(8,128)}, f32[2,96,256]{2,1,0:T(8,128)}) custom-call(s32[3]{0:T(128)} %pad_add_fusion.refs_0_, s32[48]{0:T(128)} %reshape.31.refs_1_, f32[4,12,32,256]{3,2,1,0:T(8,128)} %refs_2_.3, f32[4,6,32,256]{3,2,1,0:T(8,128)} %copy-done.5, ...), custom_call_target="tpu_custom_call" | custom-call | flops 301989888 | bytes 1572864 | tf_op jit(solution)/shard_map/pallas_call | solution.py:267
  18.2 5.2 %collective-permute-done.2.refs_3_ = f32[2,96,256]{2,1,0:T(8,128)S(1)} collective-permute-done((f32[2,96,256]{2,1,0:T(8,128)}, f32[2,96,256]{2,1,0:T(8,128)S(1)}, u32[]{:S(2)}, u32[]{:S(2)}) %collective-permute-start.2) | collective-permute-done | bytes 196640 | tf_op jit(solution)/shard_map/ppermute | solution.py:240
  24.1 2.2 shard_map.88
  26.4 1.2 collective-permute-start.7
  27.5 1.6 collective-permute-start.4
  30.0 1.4 collective-permute-start.9
  31.4 2.6 collective-permute-start.5
  34.0 3.9 %collective-permute-start.6 = (f32[2,96,256]{2,1,0:T(8,128)}, f32[2,96,256]{2,1,0:T(8,128)S(1)}, u32[]{:S(2)}, u32[]{:S(2)}) collective-permute-start(f32[2,96,256]{2,1,0:T(8,128)} %get-tuple-element.55), channel_id=1, source_target_pairs={{0,6},{1,7},{2,0},{3,1},{4,2},{5,3},{6,4},{7,5},{8,14},{9,15},{10,... | collective-permute-start | bytes 589832 | tf_op jit(solution)/shard_map/ppermute | solution.py:240
  37.9 1.2 collective-permute-done.8.refs_3_
  39.8 2.2 shard_map.89
  42.1 1.9 collective-permute-done.5.refs_3_
  44.7 2.2 shard_map.90.refs_1_
  47.7 4.4 %collective-permute-start.14 = (f32[2,96,256]{2,1,0:T(8,128)S(1)}, f32[2,96,256]{2,1,0:T(8,128)S(1)}, u32[]{:S(2)}, u32[]{:S(2)}) collective-permute-start(f32[2,96,256]{2,1,0:T(8,128)S(1)} %copy-done.36), channel_id=1, source_target_pairs={{0,2},{1,3},{2,4},{3,5},{4,6},{5,7},{6,0},{7,1},{8,10},{9,11},{10,... | collective-permute-start | bytes 589832 | tf_op jit(solution)/shard_map/ppermute | solution.py:240
  52.1 1.8 collective-permute-start.15
  54.5 1.5 collective-permute-start.11
  56.0 3.2 %collective-permute-done.14.refs_2_ = f32[2,96,256]{2,1,0:T(8,128)S(1)} collective-permute-done((f32[2,96,256]{2,1,0:T(8,128)S(1)}, f32[2,96,256]{2,1,0:T(8,128)S(1)}, u32[]{:S(2)}, u32[]{:S(2)}) %collective-permute-start.14) | collective-permute-done | bytes 196640 | tf_op jit(solution)/shard_map/ppermute | solution.py:240
  59.2 6.6 %collective-permute-done.15.refs_3_ = f32[2,96,256]{2,1,0:T(8,128)S(1)} collective-permute-done((f32[2,96,256]{2,1,0:T(8,128)S(1)}, f32[2,96,256]{2,1,0:T(8,128)S(1)}, u32[]{:S(2)}, u32[]{:S(2)}) %collective-permute-start.15) | collective-permute-done | bytes 196640 | tf_op jit(solution)/shard_map/ppermute | solution.py:240
  67.4 2.2 shard_map.91.refs_1_
  73.8 1.9 collective-permute-start.13
  75.6 14.6 %collective-permute-done.17.refs_6_.refs_2_ = f32[2,4,96,256]{3,2,1,0:T(8,128)S(1)} collective-permute-done((f32[2,4,96,256]{3,2,1,0:T(8,128)}, f32[2,4,96,256]{3,2,1,0:T(8,128)S(1)}, u32[]{:S(2)}, u32[]{:S(2)}) %collective-permute-start.17) | collective-permute-done | bytes 786464 | tf_op jit(solution)/shard_map/ppermute | solution.py:240
  90.2 1.2 collective-permute-start.19
  93.9 5.8 %collective-permute-done.12.refs_4_ = f32[1,4,96,256]{3,2,1,0:T(8,128)S(1)} collective-permute-done((f32[1,4,96,256]{3,2,1,0:T(8,128)S(1)}, f32[1,4,96,256]{3,2,1,0:T(8,128)S(1)}, u32[]{:S(2)}, u32[]{:S(2)}) %collective-permute-start.12) | collective-permute-done | bytes 393248 | tf_op jit(solution)/shard_map/ppermute | solution.py:240
  101.2 4.6 %shard_map.92 = (bf16[2,1536,256]{2,1,0:T(8,128)(2,1)}, bf16[2,1536,256]{2,1,0:T(8,128)(2,1)}) custom-call(s32[3]{0:T(128)} %pad_add_fusion.refs_0_, f32[2,4,96,256]{3,2,1,0:T(8,128)} %shard_map.90.refs_1_, f32[2,4,96,256]{3,2,1,0:T(8,128)} %copy-done, f32[2,4,96,256]{3,2,1,0:T(8,128)} %copy-done.6, f32[1,4,96,256]{3,2,1,0:T(8,128)} %copy-done.14, ...), custom_call_target="tpu_custom_call" | custom-call | bytes 6291456 | tf_op jit(solution)/shard_map/pallas_call | solution.py:315
  105.8 1.4 collective-permute-done.19.refs_4_
  107.2 4.5 %shard_map.93 = (bf16[2,1536,256]{2,1,0:T(8,128)(2,1)}, bf16[2,1536,256]{2,1,0:T(8,128)(2,1)}) custom-call(s32[3]{0:T(128)} %pad_add_fusion.refs_0_, f32[2,4,96,256]{3,2,1,0:T(8,128)} %shard_map.91.refs_1_, f32[2,4,96,256]{3,2,1,0:T(8,128)} %copy-done.1, f32[2,4,96,256]{3,2,1,0:T(8,128)} %copy-done.7, f32[1,4,96,256]{3,2,1,0:T(8,128)} %collective-permute-done.19.refs_4_, ...), custom_call_target="tpu_custom_call" | custom-call | bytes 6291456 | tf_op jit(solution)/shard_map/pallas_call | solution.py:315
  111.7 13.3 %shard_map.94 = (f32[18,64,256]{2,1,0:T(8,128)}, f32[18,64,256]{2,1,0:T(8,128)}) custom-call(s32[1]{0:T(128)} %bitcast.5.info, s32[48]{0:T(128)} %compare_select_fusion.where.refs_0_, f32[12,256,1536]{2,1,0:T(8,128)} %bitcast.74, bf16[2,1536,256]{2,1,0:T(8,128)(2,1)} %get-tuple-element.64.refs_0_.refs_1_, ...), custom_call_target="tpu_custom_call" | custom-call | flops 14495514624 | bytes 4718592 | tf_op jit(solution)/shard_map/pallas_call | solution.py:162
  125.6 3.2 %collective-permute-done.22 = f32[18,64,256]{2,1,0:T(8,128)S(1)} collective-permute-done((f32[18,64,256]{2,1,0:T(8,128)}, f32[18,64,256]{2,1,0:T(8,128)S(1)}, u32[]{:S(2)}, u32[]{:S(2)}) %collective-permute-start.22) | collective-permute-done | bytes 1179680 | tf_op jit(solution)/shard_map/ppermute | solution.py:240
  128.7 1.4 add.189.refs_8_
  130.2 4.4 %collective-permute-start.26 = (f32[18,64,256]{2,1,0:T(8,128)S(1)}, f32[18,64,256]{2,1,0:T(8,128)}, u32[]{:S(2)}, u32[]{:S(2)}) collective-permute-start(f32[18,64,256]{2,1,0:T(8,128)S(1)} %add.189.refs_8_), channel_id=1, source_target_pairs={{0,2},{1,0},{2,4},{3,1},{4,6},{5,3},{6,7},{7,5},{8,10},{9,8},{10,1... | collective-permute-start | bytes 3538952 | tf_op jit(solution)/shard_map/ppermute | solution.py:240
  134.6 13.5 %shard_map.95 = (f32[18,64,256]{2,1,0:T(8,128)}, f32[18,64,256]{2,1,0:T(8,128)}) custom-call(s32[1]{0:T(128)} %bitcast.6.info, s32[48]{0:T(128)} %compare_select_fusion.where.refs_0_, f32[12,256,1536]{2,1,0:T(8,128)} %bitcast.75, bf16[2,1536,256]{2,1,0:T(8,128)(2,1)} %get-tuple-element.64.refs_0_.refs_1_, ...), custom_call_target="tpu_custom_call" | custom-call | flops 14495514624 | bytes 4718592 | tf_op jit(solution)/shard_map/pallas_call | solution.py:162
  148.3 1.6 add.185
  151.3 3.1 %add_select_fusion.2 = (f32[18,64,256]{2,1,0:T(8,128)}, f32[18,64,256]{2,1,0:T(8,128)S(1)}) fusion(f32[18,64,256]{2,1,0:T(8,128)} %collective-permute-done.26, f32[18,64,256]{2,1,0:T(8,128)S(1)} %copy-done.3, pred[]{:T(512)S(6)} %or.8, pred[]{:T(512)S(6)} %and.64, f32[18,64,256]{2,1,0:T(8,128)S(1)} %copy-done.11, f32[18,64,256]{2,1,0:T(8,128)} %collective-permute-done.25), kind=kLoop, calls=%fused_computation.2 | loop fusion | flops 1179648 | bytes 7077890 | tf_op jit(solution)/shard_map/jit(_where)/select_n | solution.py:347
  155.5 13.4 %shard_map.97 = (f32[18,64,256]{2,1,0:T(8,128)}, f32[18,64,256]{2,1,0:T(8,128)}) custom-call(s32[1]{0:T(128)} %bitcast.7.info, s32[48]{0:T(128)} %compare_select_fusion.where.refs_0_, f32[12,256,1536]{2,1,0:T(8,128)} %bitcast.76, bf16[2,1536,256]{2,1,0:T(8,128)(2,1)} %get-tuple-element.64.refs_0_.refs_1_, ...), custom_call_target="tpu_custom_call" | custom-call | flops 14495514624 | bytes 4718592 | tf_op jit(solution)/shard_map/pallas_call | solution.py:162
  169.0 1.4 add_select_fusion.3.refs_8_
  170.4 1.2 collective-permute-start.32
  171.6 5.8 %collective-permute-done.28 = f32[18,64,256]{2,1,0:T(8,128)} collective-permute-done((f32[18,64,256]{2,1,0:T(8,128)}, f32[18,64,256]{2,1,0:T(8,128)}, u32[]{:S(2)}, u32[]{:S(2)}) %collective-permute-start.28) | collective-permute-done | bytes 1179680 | tf_op jit(solution)/shard_map/ppermute | solution.py:240
  177.4 2.3 add_select_fusion.1
  179.7 2.5 collective-permute-start.29
  182.2 7.8 %collective-permute-done.32 = f32[18,64,256]{2,1,0:T(8,128)} collective-permute-done((f32[18,64,256]{2,1,0:T(8,128)}, f32[18,64,256]{2,1,0:T(8,128)}, u32[]{:S(2)}, u32[]{:S(2)}) %collective-permute-start.32) | collective-permute-done | bytes 1179680 | tf_op jit(solution)/shard_map/ppermute | solution.py:240
  190.0 2.5 add_select_fusion
  192.5 2.5 collective-permute-start.33
  195.0 13.3 %shard_map.96 = (f32[18,64,256]{2,1,0:T(8,128)}, f32[18,64,256]{2,1,0:T(8,128)}) custom-call(s32[1]{0:T(128)} %bitcast.3.info, s32[48]{0:T(128)} %compare_select_fusion.where.refs_0_, f32[12,256,1536]{2,1,0:T(8,128)} %bitcast.77, bf16[2,1536,256]{2,1,0:T(8,128)(2,1)} %get-tuple-element.64.refs_0_.refs_1_, ...), custom_call_target="tpu_custom_call" | custom-call | flops 14495514624 | bytes 4718592 | tf_op jit(solution)/shard_map/pallas_call | solution.py:162
  209.4 2.8 %shard_map.98 = (f32[18,32,256]{2,1,0:T(8,128)}, f32[18,32,256]{2,1,0:T(8,128)}) custom-call(s32[3]{0:T(128)} %pad_add_fusion.refs_0_, f32[18,64,256]{2,1,0:T(8,128)} %get-tuple-element.71.refs_1_, f32[18,64,256]{2,1,0:T(8,128)} %copy-done.9), custom_call_target="tpu_custom_call" | custom-call | bytes 3538944 | tf_op jit(solution)/shard_map/pallas_call | solution.py:388
  212.2 3.0 %collective-permute-done.33.refs_2_ = f32[18,64,256]{2,1,0:T(8,128)S(1)} collective-permute-done((f32[18,64,256]{2,1,0:T(8,128)S(1)}, f32[18,64,256]{2,1,0:T(8,128)S(1)}, u32[]{:S(2)}, u32[]{:S(2)}) %collective-permute-start.33) | collective-permute-done | bytes 1179680 | tf_op jit(solution)/shard_map/ppermute | solution.py:240
  216.2 3.0 %shard_map.99 = (f32[18,32,256]{2,1,0:T(8,128)}, f32[18,32,256]{2,1,0:T(8,128)}) custom-call(s32[3]{0:T(128)} %pad_add_fusion.refs_0_, f32[18,64,256]{2,1,0:T(8,128)} %get-tuple-element.76.refs_1_, f32[18,64,256]{2,1,0:T(8,128)} %copy-done.10), custom_call_target="tpu_custom_call" | custom-call | bytes 3538944 | tf_op jit(solution)/shard_map/pallas_call | solution.py:388
  219.9 1.8 collective-permute-done.34.refs_6_
  222.6 5.2 %shard_map.100 = (f32[4,12,32,256]{3,2,1,0:T(8,128)}, f32[4,256,256]{2,1,0:T(8,128)}) custom-call(s32[48]{0:T(128)} %compare_select_fusion.where.refs_0_, f32[2,12,32,256]{3,2,1,0:T(8,128)} %get-tuple-element.42.refs_5_.refs_1_, f32[2,12,32,256]{3,2,1,0:T(8,128)} %get-tuple-element.43.refs_2_, f32[18,32,256]{2,1,0:T(8,128)} %get-tuple-element.74.refs_3_, ...), custom_call_target="tpu_custom_call" | custom-call | flops 1207959552 | bytes 7864320 | tf_op jit(solution)/shard_map/pallas_call | solution.py:392
  229.4 1.5 collective-permute-done.35
  231.0 1.7 collective-permute-start.38
  234.6 3.8 %collective-permute-done.38 = f32[128,256]{1,0:T(8,128)S(1)} collective-permute-done((f32[128,256]{1,0:T(8,128)S(1)}, f32[128,256]{1,0:T(8,128)S(1)}, u32[]{:S(2)}, u32[]{:S(2)}) %collective-permute-start.38) | collective-permute-done | bytes 131104 | tf_op jit(solution)/shard_map/ppermute | solution.py:240
  238.4 2.2 collective-permute-done.37
  240.7 3.1 %collective-permute-start.41 = (f32[32,256]{1,0:T(8,128)S(1)}, f32[32,256]{1,0:T(8,128)S(1)}, u32[]{:S(2)}, u32[]{:S(2)}) collective-permute-start(f32[32,256]{1,0:T(8,128)S(1)} %get-tuple-element.92), channel_id=1, source_target_pairs={{0,6},{1,7},{2,0},{3,1},{4,2},{5,3},{6,4},{7,5},{8,14},{9,15},{10,... | collective-permute-start | bytes 98312 | tf_op jit(solution)/shard_map/ppermute | solution.py:240
  245.5 3.1 %collective-permute-done.40 = f32[32,256]{1,0:T(8,128)S(1)} collective-permute-done((f32[32,256]{1,0:T(8,128)S(1)}, f32[32,256]{1,0:T(8,128)S(1)}, u32[]{:S(2)}, u32[]{:S(2)}) %collective-permute-start.40) | collective-permute-done | bytes 32800 | tf_op jit(solution)/shard_map/ppermute | solution.py:240
  251.0 2.8 %collective-permute-start.44 = (f32[32,256]{1,0:T(8,128)S(1)}, f32[32,256]{1,0:T(8,128)S(1)}, u32[]{:S(2)}, u32[]{:S(2)}) collective-permute-start(f32[32,256]{1,0:T(8,128)S(1)} %get-tuple-element.83), channel_id=1, source_target_pairs={{0,6},{1,7},{2,0},{3,1},{4,2},{5,3},{6,4},{7,5},{8,14},{9,15},{10,... | collective-permute-start | bytes 98312 | tf_op jit(solution)/shard_map/ppermute | solution.py:240
  253.8 1.9 collective-permute-done.42
  257.2 1.2 collective-permute-start.46
  258.4 1.3 collective-permute-start.47
  259.8 1.4 collective-permute-done.45
  262.2 2.0 collective-permute-done.47
  264.3 1.9 collective-permute-done.48
  (158 shorter events, 36.1 us)
Async XLA Ops:
  1.9 2.4 collective-permute-start
  9.4 8.8 %collective-permute-start.1 = (f32[2,96,256]{2,1,0:T(8,128)}, f32[2,96,256]{2,1,0:T(8,128)S(1)}, u32[]{:S(2)}, u32[]{:S(2)}) collective-permute-start(f32[2,96,256]{2,1,0:T(8,128)} %get-tuple-element.45), channel_id=1, source_target_pairs={{0,8},{1,9},{2,10},{3,11},{4,12},{5,13},{6,14},{7,15},{8,0},{9,1},... | collective-permute-start | bytes 589832 | tf_op jit(solution)/shard_map/ppermute | solution.py:240
  12.3 11.1 %collective-permute-start.2 = (f32[2,96,256]{2,1,0:T(8,128)}, f32[2,96,256]{2,1,0:T(8,128)S(1)}, u32[]{:S(2)}, u32[]{:S(2)}) collective-permute-start(f32[2,96,256]{2,1,0:T(8,128)} %get-tuple-element.46), channel_id=1, source_target_pairs={{0,16},{1,17},{2,18},{3,19},{4,20},{5,21},{6,22},{7,23},{8,24},{9,... | collective-permute-start | bytes 589832 | tf_op jit(solution)/shard_map/ppermute | solution.py:240
  13.8 9.6 %collective-permute-start.3 = (f32[2,96,256]{2,1,0:T(8,128)}, f32[2,96,256]{2,1,0:T(8,128)S(1)}, u32[]{:S(2)}, u32[]{:S(2)}) collective-permute-start(f32[2,96,256]{2,1,0:T(8,128)} %get-tuple-element.47), channel_id=1, source_target_pairs={{0,24},{1,25},{2,26},{3,27},{4,28},{5,29},{6,30},{7,31},{8,16},{9,... | collective-permute-start | bytes 589832 | tf_op jit(solution)/shard_map/ppermute | solution.py:240
  18.2 5.2 %copy-start.24 = (f32[2,96,256]{2,1,0:T(8,128)}, f32[2,96,256]{2,1,0:T(8,128)S(1)}, u32[]{:S(2)}) copy-start(f32[2,96,256]{2,1,0:T(8,128)S(1)} %collective-permute-done.1.refs_2_) | copy-start | bytes 589828
  26.4 7.7 %collective-permute-start.7 = (f32[2,96,256]{2,1,0:T(8,128)}, f32[2,96,256]{2,1,0:T(8,128)S(1)}, u32[]{:S(2)}, u32[]{:S(2)}) collective-permute-start(f32[2,96,256]{2,1,0:T(8,128)} %get-tuple-element.57), channel_id=1, source_target_pairs={{0,8},{1,9},{2,10},{3,11},{4,12},{5,13},{6,14},{7,15},{8,0},{9,1},... | collective-permute-start | bytes 589832 | tf_op jit(solution)/shard_map/ppermute | solution.py:240
  27.5 14.5 %collective-permute-start.4 = (f32[2,96,256]{2,1,0:T(8,128)}, f32[2,96,256]{2,1,0:T(8,128)S(1)}, u32[]{:S(2)}, u32[]{:S(2)}) collective-permute-start(f32[2,96,256]{2,1,0:T(8,128)} %get-tuple-element.53), channel_id=1, source_target_pairs={{0,2},{1,3},{2,4},{3,5},{4,6},{5,7},{6,0},{7,1},{8,10},{9,11},{10,... | collective-permute-start | bytes 589832 | tf_op jit(solution)/shard_map/ppermute | solution.py:240
  29.1 10.0 %collective-permute-start.8 = (f32[2,96,256]{2,1,0:T(8,128)}, f32[2,96,256]{2,1,0:T(8,128)S(1)}, u32[]{:S(2)}, u32[]{:S(2)}) collective-permute-start(f32[2,96,256]{2,1,0:T(8,128)} %get-tuple-element.58), channel_id=1, source_target_pairs={{0,16},{1,17},{2,18},{3,19},{4,20},{5,21},{6,22},{7,23},{8,24},{9,... | collective-permute-start | bytes 589832 | tf_op jit(solution)/shard_map/ppermute | solution.py:240
  30.0 9.1 %collective-permute-start.9 = (f32[2,96,256]{2,1,0:T(8,128)}, f32[2,96,256]{2,1,0:T(8,128)S(1)}, u32[]{:S(2)}, u32[]{:S(2)}) collective-permute-start(f32[2,96,256]{2,1,0:T(8,128)} %get-tuple-element.59), channel_id=1, source_target_pairs={{0,24},{1,25},{2,26},{3,27},{4,28},{5,29},{6,30},{7,31},{8,16},{9,... | collective-permute-start | bytes 589832 | tf_op jit(solution)/shard_map/ppermute | solution.py:240
  31.4 12.6 %collective-permute-start.5 = (f32[2,96,256]{2,1,0:T(8,128)}, f32[2,96,256]{2,1,0:T(8,128)S(1)}, u32[]{:S(2)}, u32[]{:S(2)}) collective-permute-start(f32[2,96,256]{2,1,0:T(8,128)} %get-tuple-element.54), channel_id=1, source_target_pairs={{0,4},{1,5},{2,6},{3,7},{4,0},{5,1},{6,2},{7,3},{8,12},{9,13},{10,... | collective-permute-start | bytes 589832 | tf_op jit(solution)/shard_map/ppermute | solution.py:240
  34.0 5.1 %copy-start.19 = (f32[2,96,256]{2,1,0:T(8,128)}, f32[2,96,256]{2,1,0:T(8,128)S(1)}, u32[]{:S(2)}) copy-start(f32[2,96,256]{2,1,0:T(8,128)S(1)} %collective-permute-done.7.refs_2_) | copy-start | bytes 589828
  34.0 10.0 %collective-permute-start.6 = (f32[2,96,256]{2,1,0:T(8,128)}, f32[2,96,256]{2,1,0:T(8,128)S(1)}, u32[]{:S(2)}, u32[]{:S(2)}) collective-permute-start(f32[2,96,256]{2,1,0:T(8,128)} %get-tuple-element.55), channel_id=1, source_target_pairs={{0,6},{1,7},{2,0},{3,1},{4,2},{5,3},{6,4},{7,5},{8,14},{9,15},{10,... | collective-permute-start | bytes 589832 | tf_op jit(solution)/shard_map/ppermute | solution.py:240
  42.1 5.6 %copy-start.36 = (f32[2,96,256]{2,1,0:T(8,128)S(1)}, f32[2,96,256]{2,1,0:T(8,128)}, u32[]{:S(2)}) copy-start(f32[2,96,256]{2,1,0:T(8,128)} %get-tuple-element.61) | copy-start | bytes 589828
  42.1 10.0 %copy-start.35 = (f32[2,96,256]{2,1,0:T(8,128)S(1)}, f32[2,96,256]{2,1,0:T(8,128)}, u32[]{:S(2)}) copy-start(f32[2,96,256]{2,1,0:T(8,128)} %get-tuple-element.62) | copy-start | bytes 589828
  42.1 11.8 %copy-start.34 = (f32[2,96,256]{2,1,0:T(8,128)S(1)}, f32[2,96,256]{2,1,0:T(8,128)}, u32[]{:S(2)}) copy-start(f32[2,96,256]{2,1,0:T(8,128)} %get-tuple-element.63) | copy-start | bytes 589828
  46.9 19.6 %collective-permute-start.10 = (f32[2,4,96,256]{3,2,1,0:T(8,128)}, f32[2,4,96,256]{3,2,1,0:T(8,128)S(1)}, u32[]{:S(2)}, u32[]{:S(2)}) collective-permute-start(f32[2,4,96,256]{3,2,1,0:T(8,128)} %shard_map.90.refs_1_), channel_id=1, source_target_pairs={{0,8},{1,9},{2,10},{3,11},{4,12},{5,13},{6,14},{7,15},{8,0},{9,1},... | collective-permute-start | bytes 2359304 | tf_op jit(solution)/shard_map/ppermute | solution.py:240
  47.7 11.5 %collective-permute-start.14 = (f32[2,96,256]{2,1,0:T(8,128)S(1)}, f32[2,96,256]{2,1,0:T(8,128)S(1)}, u32[]{:S(2)}, u32[]{:S(2)}) collective-permute-start(f32[2,96,256]{2,1,0:T(8,128)S(1)} %copy-done.36), channel_id=1, source_target_pairs={{0,2},{1,3},{2,4},{3,5},{4,6},{5,7},{6,0},{7,1},{8,10},{9,11},{10,... | collective-permute-start | bytes 589832 | tf_op jit(solution)/shard_map/ppermute | solution.py:240
  52.1 13.7 %collective-permute-start.15 = (f32[2,96,256]{2,1,0:T(8,128)S(1)}, f32[2,96,256]{2,1,0:T(8,128)S(1)}, u32[]{:S(2)}, u32[]{:S(2)}) collective-permute-start(f32[2,96,256]{2,1,0:T(8,128)S(1)} %copy-done.35), channel_id=1, source_target_pairs={{0,4},{1,5},{2,6},{3,7},{4,0},{5,1},{6,2},{7,3},{8,12},{9,13},{10,... | collective-permute-start | bytes 589832 | tf_op jit(solution)/shard_map/ppermute | solution.py:240
  53.9 11.9 %collective-permute-start.16 = (f32[2,96,256]{2,1,0:T(8,128)S(1)}, f32[2,96,256]{2,1,0:T(8,128)S(1)}, u32[]{:S(2)}, u32[]{:S(2)}) collective-permute-start(f32[2,96,256]{2,1,0:T(8,128)S(1)} %copy-done.34), channel_id=1, source_target_pairs={{0,6},{1,7},{2,0},{3,1},{4,2},{5,3},{6,4},{7,5},{8,14},{9,15},{10,... | collective-permute-start | bytes 589832 | tf_op jit(solution)/shard_map/ppermute | solution.py:240
  54.5 19.2 %collective-permute-start.11 = (f32[2,4,96,256]{3,2,1,0:T(8,128)}, f32[2,4,96,256]{3,2,1,0:T(8,128)S(1)}, u32[]{:S(2)}, u32[]{:S(2)}) collective-permute-start(f32[2,4,96,256]{3,2,1,0:T(8,128)} %shard_map.90.refs_1_), channel_id=1, source_target_pairs={{0,16},{1,17},{2,18},{3,19},{4,20},{5,21},{6,22},{7,23},{8,24},{9,... | collective-permute-start | bytes 2359304 | tf_op jit(solution)/shard_map/ppermute | solution.py:240
  59.2 7.3 %copy-start.16 = (f32[2,96,256]{2,1,0:T(8,128)}, f32[2,96,256]{2,1,0:T(8,128)S(1)}, u32[]{:S(2)}) copy-start(f32[2,96,256]{2,1,0:T(8,128)S(1)} %collective-permute-done.14.refs_2_) | copy-start | bytes 589828
  69.6 20.6 %collective-permute-start.17 = (f32[2,4,96,256]{3,2,1,0:T(8,128)}, f32[2,4,96,256]{3,2,1,0:T(8,128)S(1)}, u32[]{:S(2)}, u32[]{:S(2)}) collective-permute-start(f32[2,4,96,256]{3,2,1,0:T(8,128)} %shard_map.91.refs_1_), channel_id=1, source_target_pairs={{0,8},{1,9},{2,10},{3,11},{4,12},{5,13},{6,14},{7,15},{8,0},{9,1},... | collective-permute-start | bytes 2359304 | tf_op jit(solution)/shard_map/ppermute | solution.py:240
  70.6 20.9 %collective-permute-start.18 = (f32[2,4,96,256]{3,2,1,0:T(8,128)}, f32[2,4,96,256]{3,2,1,0:T(8,128)S(1)}, u32[]{:S(2)}, u32[]{:S(2)}) collective-permute-start(f32[2,4,96,256]{3,2,1,0:T(8,128)} %shard_map.91.refs_1_), channel_id=1, source_target_pairs={{0,16},{1,17},{2,18},{3,19},{4,20},{5,21},{6,22},{7,23},{8,24},{9,... | collective-permute-start | bytes 2359304 | tf_op jit(solution)/shard_map/ppermute | solution.py:240
  72.7 20.6 %copy-start.28 = (s32[48]{0:T(128)S(1)}, s32[48]{0:T(128)}, u32[]{:S(2)}) copy-start(s32[48]{0:T(128)} %reshape.31.refs_1_) | copy-start | bytes 580
  72.7 27.0 %collective-permute-start.12 = (f32[1,4,96,256]{3,2,1,0:T(8,128)S(1)}, f32[1,4,96,256]{3,2,1,0:T(8,128)S(1)}, u32[]{:S(2)}, u32[]{:S(2)}) collective-permute-start(f32[1,4,96,256]{3,2,1,0:T(8,128)S(1)} %slice.16), channel_id=1, source_target_pairs={{0,16},{1,17},{2,18},{3,19},{4,20},{5,21},{6,22},{7,23},{8,24},{9,... | collective-permute-start | bytes 1179656 | tf_op jit(solution)/shard_map/ppermute | solution.py:240
  73.7 18.6 %copy-start.6 = (f32[2,4,96,256]{3,2,1,0:T(8,128)}, f32[2,4,96,256]{3,2,1,0:T(8,128)S(1)}, u32[]{:S(2)}) copy-start(f32[2,4,96,256]{3,2,1,0:T(8,128)S(1)} %collective-permute-done.11.refs_3_) | copy-start | bytes 2359300
  73.8 25.9 %collective-permute-start.13 = (f32[1,4,96,256]{3,2,1,0:T(8,128)S(1)}, f32[1,4,96,256]{3,2,1,0:T(8,128)S(1)}, u32[]{:S(2)}, u32[]{:S(2)}) collective-permute-start(f32[1,4,96,256]{3,2,1,0:T(8,128)S(1)} %slice.17), channel_id=1, source_target_pairs={{0,8},{1,9},{2,10},{3,11},{4,12},{5,13},{6,14},{7,15},{8,0},{9,1},... | collective-permute-start | bytes 1179656 | tf_op jit(solution)/shard_map/ppermute | solution.py:240
  90.2 9.5 %copy-start.1 = (f32[2,4,96,256]{3,2,1,0:T(8,128)}, f32[2,4,96,256]{3,2,1,0:T(8,128)S(1)}, u32[]{:S(2)}) copy-start(f32[2,4,96,256]{3,2,1,0:T(8,128)S(1)} %collective-permute-done.17.refs_6_.refs_2_) | copy-start | bytes 2359300
  90.2 17.0 %collective-permute-start.19 = (f32[1,4,96,256]{3,2,1,0:T(8,128)S(1)}, f32[1,4,96,256]{3,2,1,0:T(8,128)}, u32[]{:S(2)}, u32[]{:S(2)}) collective-permute-start(f32[1,4,96,256]{3,2,1,0:T(8,128)S(1)} %slice.18), channel_id=1, source_target_pairs={{0,16},{1,17},{2,18},{3,19},{4,20},{5,21},{6,22},{7,23},{8,24},{9,... | collective-permute-start | bytes 1179656 | tf_op jit(solution)/shard_map/ppermute | solution.py:240
  91.5 14.4 %copy-start.7 = (f32[2,4,96,256]{3,2,1,0:T(8,128)}, f32[2,4,96,256]{3,2,1,0:T(8,128)S(1)}, u32[]{:S(2)}) copy-start(f32[2,4,96,256]{3,2,1,0:T(8,128)S(1)} %collective-permute-done.18.refs_3_) | copy-start | bytes 2359300
  92.3 14.9 %collective-permute-start.20 = (f32[1,4,96,256]{3,2,1,0:T(8,128)}, f32[1,4,96,256]{3,2,1,0:T(8,128)}, u32[]{:S(2)}, u32[]{:S(2)}) collective-permute-start(f32[1,4,96,256]{3,2,1,0:T(8,128)} %slice.19), channel_id=1, source_target_pairs={{0,8},{1,9},{2,10},{3,11},{4,12},{5,13},{6,14},{7,15},{8,0},{9,1},... | collective-permute-start | bytes 1179656 | tf_op jit(solution)/shard_map/ppermute | solution.py:240
  125.0 3.8 %collective-permute-start.22 = (f32[18,64,256]{2,1,0:T(8,128)}, f32[18,64,256]{2,1,0:T(8,128)S(1)}, u32[]{:S(2)}, u32[]{:S(2)}) collective-permute-start(f32[18,64,256]{2,1,0:T(8,128)} %get-tuple-element.69), channel_id=1, source_target_pairs={{0,1},{1,0},{2,3},{3,2},{4,5},{5,4},{6,7},{7,6},{8,9},{9,8},{10,11... | collective-permute-start | bytes 3538952 | tf_op jit(solution)/shard_map/ppermute | solution.py:240
  125.1 23.2 %collective-permute-start.21 = (f32[18,64,256]{2,1,0:T(8,128)}, f32[18,64,256]{2,1,0:T(8,128)}, u32[]{:S(2)}, u32[]{:S(2)}) collective-permute-start(f32[18,64,256]{2,1,0:T(8,128)} %get-tuple-element.68), channel_id=1, source_target_pairs={{0,1},{1,0},{2,3},{3,2},{4,5},{5,4},{6,7},{7,6},{8,9},{9,8},{10,11... | collective-permute-start | bytes 3538952 | tf_op jit(solution)/shard_map/ppermute | solution.py:240
  130.2 4.4 %copy-start.2 = (f32[18,64,256]{2,1,0:T(8,128)}, f32[18,64,256]{2,1,0:T(8,128)S(1)}, u32[]{:S(2)}) copy-start(f32[18,64,256]{2,1,0:T(8,128)S(1)} %add.189.refs_8_) | copy-start | bytes 3538948
  130.2 20.8 %collective-permute-start.26 = (f32[18,64,256]{2,1,0:T(8,128)S(1)}, f32[18,64,256]{2,1,0:T(8,128)}, u32[]{:S(2)}, u32[]{:S(2)}) collective-permute-start(f32[18,64,256]{2,1,0:T(8,128)S(1)} %add.189.refs_8_), channel_id=1, source_target_pairs={{0,2},{1,0},{2,4},{3,1},{4,6},{5,3},{6,7},{7,5},{8,10},{9,8},{10,1... | collective-permute-start | bytes 3538952 | tf_op jit(solution)/shard_map/ppermute | solution.py:240
  134.6 13.7 %copy-start.8 = (f32[18,64,256]{2,1,0:T(8,128)S(1)}, f32[18,64,256]{2,1,0:T(8,128)}, u32[]{:S(2)}) copy-start(f32[18,64,256]{2,1,0:T(8,128)} %get-tuple-element.68) | copy-start | bytes 3538948
  148.1 3.3 %collective-permute-start.25 = (f32[18,64,256]{2,1,0:T(8,128)}, f32[18,64,256]{2,1,0:T(8,128)}, u32[]{:S(2)}, u32[]{:S(2)}) collective-permute-start(f32[18,64,256]{2,1,0:T(8,128)} %get-tuple-element.72), channel_id=1, source_target_pairs={{0,1},{1,0},{2,3},{3,2},{4,5},{5,4},{6,7},{7,6},{8,9},{9,8},{10,11... | collective-permute-start | bytes 3538952 | tf_op jit(solution)/shard_map/ppermute | solution.py:240
  148.2 3.1 %copy-start.3 = (f32[18,64,256]{2,1,0:T(8,128)S(1)}, f32[18,64,256]{2,1,0:T(8,128)}, u32[]{:S(2)}) copy-start(f32[18,64,256]{2,1,0:T(8,128)} %copy-done.2) | copy-start | bytes 3538948
  149.8 19.1 %collective-permute-start.24 = (f32[18,64,256]{2,1,0:T(8,128)S(1)}, f32[18,64,256]{2,1,0:T(8,128)S(1)}, u32[]{:S(2)}, u32[]{:S(2)}) collective-permute-start(f32[18,64,256]{2,1,0:T(8,128)S(1)} %add.185), channel_id=1, source_target_pairs={{0,2},{1,0},{2,4},{3,1},{4,6},{5,3},{6,7},{7,5},{8,10},{9,8},{10,1... | collective-permute-start | bytes 3538952 | tf_op jit(solution)/shard_map/ppermute | solution.py:240
  150.9 18.0 %collective-permute-start.23 = (f32[18,64,256]{2,1,0:T(8,128)S(1)}, f32[18,64,256]{2,1,0:T(8,128)S(1)}, u32[]{:S(2)}, u32[]{:S(2)}) collective-permute-start(f32[18,64,256]{2,1,0:T(8,128)S(1)} %copy-done.4), channel_id=1, source_target_pairs={{0,1},{1,0},{2,3},{3,2},{4,5},{5,4},{6,7},{7,6},{8,9},{9,8},{10,11... | collective-permute-start | bytes 3538952 | tf_op jit(solution)/shard_map/ppermute | solution.py:240
  154.5 22.9 %collective-permute-start.28 = (f32[18,64,256]{2,1,0:T(8,128)}, f32[18,64,256]{2,1,0:T(8,128)}, u32[]{:S(2)}, u32[]{:S(2)}) collective-permute-start(f32[18,64,256]{2,1,0:T(8,128)} %get-tuple-element.84.refs_8_), channel_id=1, source_target_pairs={{0,2},{1,0},{2,4},{3,1},{4,6},{5,3},{6,7},{7,5},{8,10},{9,8},{10,1... | collective-permute-start | bytes 3538952 | tf_op jit(solution)/shard_map/ppermute | solution.py:240
  168.9 8.5 %collective-permute-start.27 = (f32[18,64,256]{2,1,0:T(8,128)}, f32[18,64,256]{2,1,0:T(8,128)}, u32[]{:S(2)}, u32[]{:S(2)}) collective-permute-start(f32[18,64,256]{2,1,0:T(8,128)} %get-tuple-element.73), channel_id=1, source_target_pairs={{0,1},{1,0},{2,3},{3,2},{4,5},{5,4},{6,7},{7,6},{8,9},{9,8},{10,11... | collective-permute-start | bytes 3538952 | tf_op jit(solution)/shard_map/ppermute | solution.py:240
  170.4 19.7 %collective-permute-start.32 = (f32[18,64,256]{2,1,0:T(8,128)}, f32[18,64,256]{2,1,0:T(8,128)}, u32[]{:S(2)}, u32[]{:S(2)}) collective-permute-start(f32[18,64,256]{2,1,0:T(8,128)} %add_select_fusion.3.refs_8_), channel_id=1, source_target_pairs={{0,2},{1,0},{2,4},{3,1},{4,6},{5,3},{6,7},{7,5},{8,10},{9,8},{10,1... | collective-permute-start | bytes 3538952 | tf_op jit(solution)/shard_map/ppermute | solution.py:240
  171.6 18.5 %collective-permute-start.31 = (f32[18,64,256]{2,1,0:T(8,128)}, f32[18,64,256]{2,1,0:T(8,128)}, u32[]{:S(2)}, u32[]{:S(2)}) collective-permute-start(f32[18,64,256]{2,1,0:T(8,128)} %get-tuple-element.77), channel_id=1, source_target_pairs={{0,1},{1,0},{2,3},{3,2},{4,5},{5,4},{6,7},{7,6},{8,9},{9,8},{10,11... | collective-permute-start | bytes 3538952 | tf_op jit(solution)/shard_map/ppermute | solution.py:240
  179.7 28.6 %collective-permute-start.29 = (f32[18,64,256]{2,1,0:T(8,128)S(1)}, f32[18,64,256]{2,1,0:T(8,128)S(1)}, u32[]{:S(2)}, u32[]{:S(2)}) collective-permute-start(f32[18,64,256]{2,1,0:T(8,128)S(1)} %add_select_fusion.1), channel_id=1, source_target_pairs={{0,2},{1,0},{2,4},{3,1},{4,6},{5,3},{6,7},{7,5},{8,10},{9,8},{10,1... | collective-permute-start | bytes 3538952 | tf_op jit(solution)/shard_map/ppermute | solution.py:240
  192.5 22.7 %collective-permute-start.33 = (f32[18,64,256]{2,1,0:T(8,128)S(1)}, f32[18,64,256]{2,1,0:T(8,128)S(1)}, u32[]{:S(2)}, u32[]{:S(2)}) collective-permute-start(f32[18,64,256]{2,1,0:T(8,128)S(1)} %add_select_fusion), channel_id=1, source_target_pairs={{0,2},{1,0},{2,4},{3,1},{4,6},{5,3},{6,7},{7,5},{8,10},{9,8},{10,1... | collective-permute-start | bytes 3538952 | tf_op jit(solution)/shard_map/ppermute | solution.py:240
  212.2 7.8 %collective-permute-start.30 = (f32[18,32,256]{2,1,0:T(8,128)}, f32[18,32,256]{2,1,0:T(8,128)S(1)}, u32[]{:S(2)}, u32[]{:S(2)}) collective-permute-start(f32[18,32,256]{2,1,0:T(8,128)} %get-tuple-element.75), channel_id=1, source_target_pairs={{0,1},{1,0},{2,3},{3,2},{4,5},{5,4},{6,7},{7,6},{8,9},{9,8},{10,11... | collective-permute-start | bytes 1769480 | tf_op jit(solution)/shard_map/ppermute | solution.py:240
  219.3 2.5 collective-permute-start.34
  227.8 3.1 %copy-start.13 = (f32[4,256,256]{2,1,0:T(8,128)S(1)}, f32[4,256,256]{2,1,0:T(8,128)}, u32[]{:S(2)}) copy-start(f32[4,256,256]{2,1,0:T(8,128)} %get-tuple-element.81) | copy-start | bytes 3145732
  229.0 2.0 collective-permute-start.35
  231.0 7.3 %collective-permute-start.38 = (f32[128,256]{1,0:T(8,128)S(1)}, f32[128,256]{1,0:T(8,128)S(1)}, u32[]{:S(2)}, u32[]{:S(2)}) collective-permute-start(f32[128,256]{1,0:T(8,128)S(1)} %get-tuple-element.89), channel_id=1, source_target_pairs={{0,24},{1,25},{2,26},{3,27},{4,28},{5,29},{6,30},{7,31},{8,16},{9,... | collective-permute-start | bytes 393224 | tf_op jit(solution)/shard_map/ppermute | solution.py:240
  232.7 7.9 %collective-permute-start.37 = (f32[128,256]{1,0:T(8,128)S(1)}, f32[128,256]{1,0:T(8,128)S(1)}, u32[]{:S(2)}, u32[]{:S(2)}) collective-permute-start(f32[128,256]{1,0:T(8,128)S(1)} %get-tuple-element.90), channel_id=1, source_target_pairs={{0,16},{1,17},{2,18},{3,19},{4,20},{5,21},{6,22},{7,23},{8,24},{9,... | collective-permute-start | bytes 393224 | tf_op jit(solution)/shard_map/ppermute | solution.py:240
  233.6 7.0 %collective-permute-start.36 = (f32[128,256]{1,0:T(8,128)S(1)}, f32[128,256]{1,0:T(8,128)S(1)}, u32[]{:S(2)}, u32[]{:S(2)}) collective-permute-start(f32[128,256]{1,0:T(8,128)S(1)} %get-tuple-element.88), channel_id=1, source_target_pairs={{0,8},{1,9},{2,10},{3,11},{4,12},{5,13},{6,14},{7,15},{8,0},{9,1},... | collective-permute-start | bytes 393224 | tf_op jit(solution)/shard_map/ppermute | solution.py:240
  240.7 4.9 %collective-permute-start.41 = (f32[32,256]{1,0:T(8,128)S(1)}, f32[32,256]{1,0:T(8,128)S(1)}, u32[]{:S(2)}, u32[]{:S(2)}) collective-permute-start(f32[32,256]{1,0:T(8,128)S(1)} %get-tuple-element.92), channel_id=1, source_target_pairs={{0,6},{1,7},{2,0},{3,1},{4,2},{5,3},{6,4},{7,5},{8,14},{9,15},{10,... | collective-permute-start | bytes 98312 | tf_op jit(solution)/shard_map/ppermute | solution.py:240
  243.7 4.9 %collective-permute-start.40 = (f32[32,256]{1,0:T(8,128)S(1)}, f32[32,256]{1,0:T(8,128)S(1)}, u32[]{:S(2)}, u32[]{:S(2)}) collective-permute-start(f32[32,256]{1,0:T(8,128)S(1)} %get-tuple-element.93), channel_id=1, source_target_pairs={{0,4},{1,5},{2,6},{3,7},{4,0},{5,1},{6,2},{7,3},{8,12},{9,13},{10,... | collective-permute-start | bytes 98312 | tf_op jit(solution)/shard_map/ppermute | solution.py:240
  244.1 5.7 %collective-permute-start.39 = (f32[32,256]{1,0:T(8,128)S(1)}, f32[32,256]{1,0:T(8,128)S(1)}, u32[]{:S(2)}, u32[]{:S(2)}) collective-permute-start(f32[32,256]{1,0:T(8,128)S(1)} %get-tuple-element.91), channel_id=1, source_target_pairs={{0,2},{1,3},{2,4},{3,5},{4,6},{5,7},{6,0},{7,1},{8,10},{9,11},{10,... | collective-permute-start | bytes 98312 | tf_op jit(solution)/shard_map/ppermute | solution.py:240
  249.9 5.8 %collective-permute-start.42 = (f32[32,256]{1,0:T(8,128)S(1)}, f32[32,256]{1,0:T(8,128)S(1)}, u32[]{:S(2)}, u32[]{:S(2)}) collective-permute-start(f32[32,256]{1,0:T(8,128)S(1)} %get-tuple-element.83), channel_id=1, source_target_pairs={{0,2},{1,3},{2,4},{3,5},{4,6},{5,7},{6,0},{7,1},{8,10},{9,11},{10,... | collective-permute-start | bytes 98312 | tf_op jit(solution)/shard_map/ppermute | solution.py:240
  250.0 5.6 %collective-permute-start.43 = (f32[32,256]{1,0:T(8,128)S(1)}, f32[32,256]{1,0:T(8,128)S(1)}, u32[]{:S(2)}, u32[]{:S(2)}) collective-permute-start(f32[32,256]{1,0:T(8,128)S(1)} %get-tuple-element.83), channel_id=1, source_target_pairs={{0,4},{1,5},{2,6},{3,7},{4,0},{5,1},{6,2},{7,3},{8,12},{9,13},{10,... | collective-permute-start | bytes 98312 | tf_op jit(solution)/shard_map/ppermute | solution.py:240
  251.0 5.2 %collective-permute-start.44 = (f32[32,256]{1,0:T(8,128)S(1)}, f32[32,256]{1,0:T(8,128)S(1)}, u32[]{:S(2)}, u32[]{:S(2)}) collective-permute-start(f32[32,256]{1,0:T(8,128)S(1)} %get-tuple-element.83), channel_id=1, source_target_pairs={{0,6},{1,7},{2,0},{3,1},{4,2},{5,3},{6,4},{7,5},{8,14},{9,15},{10,... | collective-permute-start | bytes 98312 | tf_op jit(solution)/shard_map/ppermute | solution.py:240
  256.2 5.0 %collective-permute-start.45 = (f32[128,256]{1,0:T(8,128)S(1)}, f32[128,256]{1,0:T(8,128)S(1)}, u32[]{:S(2)}, u32[]{:S(2)}) collective-permute-start(f32[128,256]{1,0:T(8,128)S(1)} %bitcast.68), channel_id=1, source_target_pairs={{0,8},{1,9},{2,10},{3,11},{4,12},{5,13},{6,14},{7,15},{8,0},{9,1},... | collective-permute-start | bytes 393224 | tf_op jit(solution)/shard_map/ppermute | solution.py:240
  257.2 5.0 %collective-permute-start.46 = (f32[128,256]{1,0:T(8,128)S(1)}, f32[128,256]{1,0:T(8,128)S(1)}, u32[]{:S(2)}, u32[]{:S(2)}) collective-permute-start(f32[128,256]{1,0:T(8,128)S(1)} %bitcast.69), channel_id=1, source_target_pairs={{0,16},{1,17},{2,18},{3,19},{4,20},{5,21},{6,22},{7,23},{8,24},{9,... | collective-permute-start | bytes 393224 | tf_op jit(solution)/shard_map/ppermute | solution.py:240
  258.4 5.9 %collective-permute-start.47 = (f32[128,256]{1,0:T(8,128)S(1)}, f32[128,256]{1,0:T(8,128)S(1)}, u32[]{:S(2)}, u32[]{:S(2)}) collective-permute-start(f32[128,256]{1,0:T(8,128)S(1)} %bitcast.70), channel_id=1, source_target_pairs={{0,24},{1,25},{2,26},{3,27},{4,28},{5,29},{6,30},{7,31},{8,16},{9,... | collective-permute-start | bytes 393224 | tf_op jit(solution)/shard_map/ppermute | solution.py:240
  262.2 4.1 %copy-start.12 = (f32[4,256,256]{2,1,0:T(8,128)S(1)}, f32[4,256,256]{2,1,0:T(8,128)}, u32[]{:S(2)}) copy-start(f32[4,256,256]{2,1,0:T(8,128)} %param.10) | copy-start | bytes 3145732
  264.3 2.0 collective-permute-start.48
  (22 other events, 27.0 us)

commit v5 on v4

--- a/solution.py
+++ b/solution.py
@@ -183,24 +183,12 @@
     )(info, where, g3, *[x[0] for x in xs], *[x[1] for x in xs], *after)
 
 
-def merge_kernel(lines, place, own_ref, arrived_ref, mine, other):
-    rb = mine.shape[1]
-    from_others = place[1] != jnp.where(place[2] == 0, 0, lines - 1)
-    for core in range(2):
-        rows = slice(core * rb, (core + 1) * rb)
-
-        def fill(out, rows=rows):
-            out[...] = own_ref[:, rows, :] + jnp.where(from_others, arrived_ref[:, rows, :], 0.0)
-
-        pl.when(place[2] == core)(functools.partial(fill, mine))
-        pl.when(place[2] != core)(functools.partial(fill, other))
-
-
-def finish_kernel(groups, bounds, where, *refs):
+def finish_kernel(groups, bounds, lines, place, where, *refs):
+    from_others = place[1] != jnp.where(place[2] == 0, lines - 1, 0)
     n_refs, refs = refs[: len(groups)], refs[len(groups) :]
-    panel_ref, diag_ref, total = refs[-3:]
+    panel_ref, diag_mine, diag_other, total, diag_ref = refs[-5:]
     for k in range(len(bounds) - 1):
-        total[bounds[k] : bounds[k + 1]] = refs[2 * k][...] + refs[2 * k + 1][...]
+        total[bounds[k] : bounds[k + 1]] = refs[2 * k][...] + jnp.where(from_others, refs[2 * k + 1][...], 0.0)
     panels, slots, rb, width = panel_ref.shape
     n_of = {p: n_refs[g][at] for g, group in enumerate(groups) for at, p in enumerate(group)}
     for p in range(panels):
@@ -215,6 +203,9 @@
             precision=HIGHEST,
             preferred_element_type=jnp.float32,
         )
+    half = diag_mine.shape[0]
+    diag_mine[...] = diag_ref[pl.ds(place[2] * half, half)]
+    diag_other[...] = diag_ref[pl.ds((1 - place[2]) * half, half)]
 
 
 def on_device(
@@ -383,25 +374,26 @@
         if step == lines - 3:
             compute(after)
     finals = []
+    from_others = z != jnp.where(h == 0, 0, lines - 1)
+    rows_of = lambda value, core: lax.dynamic_slice_in_dim(value, core * rb, rb, 1)
     for k in range(2):
-        half_rows = jax.ShapeDtypeStruct((bounds[k + 1] - bounds[k], rb, width), f32)
-        mine, other = call(
-            functools.partial(merge_kernel, lines), [half_rows, half_rows], n_in=2, moved=12 * keep * rb * width
-        )(place, made[k][-1][0], moving[k][-1])
-        finals += [mine, swap(other)]
-    panel_inverse, terms = call(
-        functools.partial(finish_kernel, groups, bounds),
+        own, arrived = made[k][-1][0], moving[k][-1]
+        own = rows_of(own, h) + swap(rows_of(own, 1 - h))
+        swapped = swap(rows_of(arrived, 1 - h))
+        finals += [own + jnp.where(from_others, rows_of(arrived, h), 0.0), swapped]
+    diag_half = jax.ShapeDtypeStruct((half, width, width), f32)
+    panel_inverse, mine, other = call(
+        functools.partial(finish_kernel, groups, bounds, lines),
         [
             jax.ShapeDtypeStruct(factor_blocks.shape, f32),
-            jax.ShapeDtypeStruct(factor_inverse.shape, f32),
+            diag_half, diag_half,
         ],
-        [pltpu.VMEM((keep, rb, width), f32)],
-        n_in=len(groups) + len(finals), flops=12 * factor_blocks.size * width, moved=20 * factor_blocks.size,
-    )(where, *normalized, *finals)
+        [pltpu.VMEM((keep, rb, width), f32), pltpu.VMEM(factor_inverse.shape, f32)],
+        n_scalar=2, n_in=len(groups) + len(finals), flops=12 * factor_blocks.size * width, moved=20 * factor_blocks.size,
+    )(place, where, *normalized, *finals)
 
     pick = lambda value, at: lax.dynamic_index_in_dim(value, at, 0, False)
-    two = terms.reshape(2, half * width, width)
-    total = pick(two, h) + swap(pick(two, 1 - h))
+    total = (mine + swap(other)).reshape(half * width, width)
     parts = total.reshape(lines, -1, width)
     total = pick(parts, r)
     for piece in [across(pick(parts, r ^ d), d) for d in range(1, lines)]:

time: 268 us -> 266 us (level)
  other arithmetic: 15.4 us -> 23.1 us
  Pallas kernels: 90.8 us -> 85.2 us
  waiting for transfers between devices: 83.7 us -> 80.5 us
    pallas_call x3 -> x1, Pallas kernels: 11 us -> 5.23 us  [on_device(): call(functools.partial(finish_kernel, groups, bounds, lines), [jax.ShapeD...]
    dynamic_slice x0 -> x2, other arithmetic: none -> 4.47 us  [on_device(): lax.dynamic_slice_in_dim(value, core * rb, rb, 1)]
    ppermute x49 -> x51, waiting for transfers between devices: 83.7 us -> 80.5 us  [send(): return lax.ppermute(value, AXES, pairs)]
    dynamic_slice x0 -> x2, local copies, waits for them, and re-layouts: none -> 2.95 us  [on_device(): lax.dynamic_slice_in_dim(value, core * rb, rb, 1)]
    unnamed x74 -> x72, local copies, waits for them, and re-layouts: 8.42 us -> 6.49 us
    ppermute x49 -> x51, starting transfers between devices: 62.7 us -> 62.1 us  [send(): return lax.ppermute(value, AXES, pairs)]
  transfers between devices with their start and end apart: 49 -> 51, of which waited for: 29 -> 29; matrix products, arithmetic and copies ran while one was open for 6% -> 10% of each run, Pallas kernels for 22% -> 20%
where the time goes in v5:
time: 266 us; the launch traced here: 265 us
  Pallas kernels  85.2 us (32%)
  waiting for transfers between devices  80.5 us (30%)
  starting transfers between devices  62.1 us (23%)
  other arithmetic  23.1 us (9%)
  local copies, waits for them, and re-layouts  13.5 us (5%)
    ppermute x51, waiting for transfers between devices, send(): return lax.ppermute(value, AXES, pairs)  80.5 us
    ppermute x51, starting transfers between devices, send(): return lax.ppermute(value, AXES, pairs)  62.1 us
    pallas_call x4, Pallas kernels, product(): pl.pallas_call(functools.partial(product_kernel, len(xs), slots, bounds,...  53.5 us
    select_n x4, other arithmetic, add_arrived(): jnp.where((behind > 0) & (behind <= step + 1), value + arrived, value)  11.6 us
    pallas_call x2, Pallas kernels, assemble(): call(functools.partial(assemble_kernel, lines, rb), [block, block], [pltp...  9.08 us
    pallas_call x2, Pallas kernels, normalize(): call(functools.partial(normalize_kernel, group, lines), [rows_made] + [ja...  8.53 us
    unnamed x72, local copies, waits for them, and re-layouts  6.49 us
  transfers between devices with their start and end apart: 51, of which 29 were waited for; matrix products, arithmetic and copies ran while one was open for 10% of the time, Pallas kernels for 20%

profile of v5, /device:TPU:0, one launch (start us, length us, event | category | flops | bytes accessed | tf_op | source)
XLA Modules:
  0.0 265.5 jit_solution(1030543141751957705)
XLA Ops:
  0.7 1.2 constant_dynamic-slice_fusion.4
  5.2 4.3 %shard_map.86 = (f32[2,12,32,256]{3,2,1,0:T(8,128)}, f32[2,96,256]{2,1,0:T(8,128)}, f32[2,96,256]{2,1,0:T(8,128)}, f32[2,96,256]{2,1,0:T(8,128)}, f32[2,96,256]{2,1,0:T(8,128)}) custom-call(s32[3]{0:T(128)} %pad_add_fusion.refs_0_, s32[48]{0:T(128)} %reshape.25.refs_1_, f32[4,12,32,256]{3,2,1,0:T(8,128)} %refs_2_.3, f32[4,6,32,256]{3,2,1,0:T(8,128)} %copy-done.5, ...), custom_call_target="tpu_custom_call" | custom-call | flops 301989888 | bytes 1572864 | tf_op jit(solution)/shard_map/pallas_call | solution.py:258
  9.4 2.9 %collective-permute-start.1 = (f32[2,96,256]{2,1,0:T(8,128)}, f32[2,96,256]{2,1,0:T(8,128)S(1)}, u32[]{:S(2)}, u32[]{:S(2)}) collective-permute-start(f32[2,96,256]{2,1,0:T(8,128)} %get-tuple-element.42), channel_id=1, source_target_pairs={{0,8},{1,9},{2,10},{3,11},{4,12},{5,13},{6,14},{7,15},{8,0},{9,1},... | collective-permute-start | bytes 589832 | tf_op jit(solution)/shard_map/ppermute | solution.py:231
  12.3 1.5 collective-permute-start.2
  13.8 4.3 %shard_map.87 = (f32[2,12,32,256]{3,2,1,0:T(8,128)}, f32[2,96,256]{2,1,0:T(8,128)}, f32[2,96,256]{2,1,0:T(8,128)}, f32[2,96,256]{2,1,0:T(8,128)}, f32[2,96,256]{2,1,0:T(8,128)}) custom-call(s32[3]{0:T(128)} %pad_add_fusion.refs_0_, s32[48]{0:T(128)} %reshape.25.refs_1_, f32[4,12,32,256]{3,2,1,0:T(8,128)} %refs_2_.3, f32[4,6,32,256]{3,2,1,0:T(8,128)} %copy-done.5, ...), custom_call_target="tpu_custom_call" | custom-call | flops 301989888 | bytes 1572864 | tf_op jit(solution)/shard_map/pallas_call | solution.py:258
  18.2 5.2 %collective-permute-done.2.refs_3_ = f32[2,96,256]{2,1,0:T(8,128)S(1)} collective-permute-done((f32[2,96,256]{2,1,0:T(8,128)}, f32[2,96,256]{2,1,0:T(8,128)S(1)}, u32[]{:S(2)}, u32[]{:S(2)}) %collective-permute-start.2) | collective-permute-done | bytes 196640 | tf_op jit(solution)/shard_map/ppermute | solution.py:231
  24.1 2.2 shard_map.88
  26.4 1.2 collective-permute-start.7
  27.6 1.6 collective-permute-start.4
  30.0 1.4 collective-permute-start.9
  31.5 2.6 collective-permute-start.5
  34.1 3.9 %collective-permute-start.6 = (f32[2,96,256]{2,1,0:T(8,128)}, f32[2,96,256]{2,1,0:T(8,128)S(1)}, u32[]{:S(2)}, u32[]{:S(2)}) collective-permute-start(f32[2,96,256]{2,1,0:T(8,128)} %get-tuple-element.52), channel_id=1, source_target_pairs={{0,6},{1,7},{2,0},{3,1},{4,2},{5,3},{6,4},{7,5},{8,14},{9,15},{10,... | collective-permute-start | bytes 589832 | tf_op jit(solution)/shard_map/ppermute | solution.py:231
  37.9 1.2 collective-permute-done.8.refs_3_
  39.9 2.3 shard_map.89
  42.2 1.9 collective-permute-done.5.refs_3_
  44.8 2.2 shard_map.90.refs_1_
  47.7 4.4 %collective-permute-start.14 = (f32[2,96,256]{2,1,0:T(8,128)S(1)}, f32[2,96,256]{2,1,0:T(8,128)S(1)}, u32[]{:S(2)}, u32[]{:S(2)}) collective-permute-start(f32[2,96,256]{2,1,0:T(8,128)S(1)} %copy-done.35), channel_id=1, source_target_pairs={{0,2},{1,3},{2,4},{3,5},{4,6},{5,7},{6,0},{7,1},{8,10},{9,11},{10,... | collective-permute-start | bytes 589832 | tf_op jit(solution)/shard_map/ppermute | solution.py:231
  52.1 1.7 collective-permute-start.15
  54.6 1.5 collective-permute-start.11
  56.0 3.2 %collective-permute-done.14.refs_2_ = f32[2,96,256]{2,1,0:T(8,128)S(1)} collective-permute-done((f32[2,96,256]{2,1,0:T(8,128)S(1)}, f32[2,96,256]{2,1,0:T(8,128)S(1)}, u32[]{:S(2)}, u32[]{:S(2)}) %collective-permute-start.14) | collective-permute-done | bytes 196640 | tf_op jit(solution)/shard_map/ppermute | solution.py:231
  59.2 6.6 %collective-permute-done.15.refs_3_ = f32[2,96,256]{2,1,0:T(8,128)S(1)} collective-permute-done((f32[2,96,256]{2,1,0:T(8,128)S(1)}, f32[2,96,256]{2,1,0:T(8,128)S(1)}, u32[]{:S(2)}, u32[]{:S(2)}) %collective-permute-start.15) | collective-permute-done | bytes 196640 | tf_op jit(solution)/shard_map/ppermute | solution.py:231
  67.4 2.2 shard_map.91.refs_1_
  73.8 1.8 collective-permute-start.13
  75.6 14.6 %collective-permute-done.17.refs_6_.refs_2_ = f32[2,4,96,256]{3,2,1,0:T(8,128)S(1)} collective-permute-done((f32[2,4,96,256]{3,2,1,0:T(8,128)}, f32[2,4,96,256]{3,2,1,0:T(8,128)S(1)}, u32[]{:S(2)}, u32[]{:S(2)}) %collective-permute-start.17) | collective-permute-done | bytes 786464 | tf_op jit(solution)/shard_map/ppermute | solution.py:231
  90.3 1.2 collective-permute-start.19
  93.9 5.8 %collective-permute-done.12.refs_4_ = f32[1,4,96,256]{3,2,1,0:T(8,128)S(1)} collective-permute-done((f32[1,4,96,256]{3,2,1,0:T(8,128)S(1)}, f32[1,4,96,256]{3,2,1,0:T(8,128)S(1)}, u32[]{:S(2)}, u32[]{:S(2)}) %collective-permute-start.12) | collective-permute-done | bytes 393248 | tf_op jit(solution)/shard_map/ppermute | solution.py:231
  101.3 4.6 %shard_map.92 = (bf16[2,1536,256]{2,1,0:T(8,128)(2,1)}, bf16[2,1536,256]{2,1,0:T(8,128)(2,1)}) custom-call(s32[3]{0:T(128)} %pad_add_fusion.refs_0_, f32[2,4,96,256]{3,2,1,0:T(8,128)} %shard_map.90.refs_1_, f32[2,4,96,256]{3,2,1,0:T(8,128)} %copy-done, f32[2,4,96,256]{3,2,1,0:T(8,128)} %copy-done.6, f32[1,4,96,256]{3,2,1,0:T(8,128)} %copy-done.13, ...), custom_call_target="tpu_custom_call" | custom-call | bytes 6291456 | tf_op jit(solution)/shard_map/pallas_call | solution.py:306
  105.9 1.3 collective-permute-done.19.refs_4_
  107.2 4.5 %shard_map.93 = (bf16[2,1536,256]{2,1,0:T(8,128)(2,1)}, bf16[2,1536,256]{2,1,0:T(8,128)(2,1)}) custom-call(s32[3]{0:T(128)} %pad_add_fusion.refs_0_, f32[2,4,96,256]{3,2,1,0:T(8,128)} %shard_map.91.refs_1_, f32[2,4,96,256]{3,2,1,0:T(8,128)} %copy-done.1, f32[2,4,96,256]{3,2,1,0:T(8,128)} %copy-done.7, f32[1,4,96,256]{3,2,1,0:T(8,128)} %collective-permute-done.19.refs_4_, ...), custom_call_target="tpu_custom_call" | custom-call | bytes 6291456 | tf_op jit(solution)/shard_map/pallas_call | solution.py:306
  111.7 13.3 %shard_map.94 = (f32[18,64,256]{2,1,0:T(8,128)}, f32[18,64,256]{2,1,0:T(8,128)}) custom-call(s32[1]{0:T(128)} %bitcast.5.info, s32[48]{0:T(128)} %compare_select_fusion.where.refs_1_, f32[12,256,1536]{2,1,0:T(8,128)} %bitcast.67, bf16[2,1536,256]{2,1,0:T(8,128)(2,1)} %get-tuple-element.61.refs_0_.refs_1_, ...), custom_call_target="tpu_custom_call" | custom-call | flops 14495514624 | bytes 4718592 | tf_op jit(solution)/shard_map/pallas_call | solution.py:162
  125.6 3.2 %collective-permute-done.22 = f32[18,64,256]{2,1,0:T(8,128)S(1)} collective-permute-done((f32[18,64,256]{2,1,0:T(8,128)}, f32[18,64,256]{2,1,0:T(8,128)S(1)}, u32[]{:S(2)}, u32[]{:S(2)}) %collective-permute-start.22) | collective-permute-done | bytes 1179680 | tf_op jit(solution)/shard_map/ppermute | solution.py:231
  128.8 1.4 add.205.refs_8_
  130.2 4.4 %collective-permute-start.27 = (f32[18,64,256]{2,1,0:T(8,128)S(1)}, f32[18,64,256]{2,1,0:T(8,128)}, u32[]{:S(2)}, u32[]{:S(2)}) collective-permute-start(f32[18,64,256]{2,1,0:T(8,128)S(1)} %add.205.refs_8_), channel_id=1, source_target_pairs={{0,2},{1,0},{2,4},{3,1},{4,6},{5,3},{6,7},{7,5},{8,10},{9,8},{10,1... | collective-permute-start | bytes 3538952 | tf_op jit(solution)/shard_map/ppermute | solution.py:231
  134.7 13.5 %shard_map.95 = (f32[18,64,256]{2,1,0:T(8,128)}, f32[18,64,256]{2,1,0:T(8,128)}) custom-call(s32[1]{0:T(128)} %bitcast.6.info, s32[48]{0:T(128)} %compare_select_fusion.where.refs_1_, f32[12,256,1536]{2,1,0:T(8,128)} %bitcast.68, bf16[2,1536,256]{2,1,0:T(8,128)(2,1)} %get-tuple-element.61.refs_0_.refs_1_, ...), custom_call_target="tpu_custom_call" | custom-call | flops 14495514624 | bytes 4718592 | tf_op jit(solution)/shard_map/pallas_call | solution.py:162
  148.3 1.6 add.201
  151.4 3.2 %add_select_fusion.2 = (f32[18,64,256]{2,1,0:T(8,128)}, f32[18,64,256]{2,1,0:T(8,128)S(1)}) fusion(f32[18,64,256]{2,1,0:T(8,128)} %collective-permute-done.27, f32[18,64,256]{2,1,0:T(8,128)S(1)} %copy-done.3, pred[]{:T(512)S(6)} %or.8, pred[]{:T(512)S(6)} %and.64, f32[18,64,256]{2,1,0:T(8,128)S(1)} %copy-done.11, f32[18,64,256]{2,1,0:T(8,128)} %collective-permute-done.26), kind=kLoop, calls=%fused_computation.2 | loop fusion | flops 1179648 | bytes 7077890 | tf_op jit(solution)/shard_map/jit(_where)/select_n | solution.py:338
  155.6 13.3 %shard_map.97 = (f32[18,64,256]{2,1,0:T(8,128)}, f32[18,64,256]{2,1,0:T(8,128)}) custom-call(s32[1]{0:T(128)} %bitcast.7.info, s32[48]{0:T(128)} %compare_select_fusion.where.refs_1_, f32[12,256,1536]{2,1,0:T(8,128)} %bitcast.69, bf16[2,1536,256]{2,1,0:T(8,128)(2,1)} %get-tuple-element.61.refs_0_.refs_1_, ...), custom_call_target="tpu_custom_call" | custom-call | flops 14495514624 | bytes 4718592 | tf_op jit(solution)/shard_map/pallas_call | solution.py:162
  169.0 1.4 add_select_fusion.3.refs_8_
  171.6 5.9 %collective-permute-done.29 = f32[18,64,256]{2,1,0:T(8,128)} collective-permute-done((f32[18,64,256]{2,1,0:T(8,128)}, f32[18,64,256]{2,1,0:T(8,128)}, u32[]{:S(2)}, u32[]{:S(2)}) %collective-permute-start.29) | collective-permute-done | bytes 1179680 | tf_op jit(solution)/shard_map/ppermute | solution.py:231
  177.5 3.4 %add_select_fusion.1 = f32[18,64,256]{2,1,0:T(8,128)} fusion(f32[18,64,256]{2,1,0:T(8,128)} %collective-permute-done.29, f32[18,64,256]{2,1,0:T(8,128)S(1)} %get-tuple-element.79, f32[18,64,256]{2,1,0:T(8,128)} %get-tuple-element.70, f32[18,64,256]{2,1,0:T(8,128)} %collective-permute-done.28, pred[]{:T(512)S(6)} %or.9, pred[]{:T(512)S(6)} %and.67), kind=kLoop, calls=%fused_computation.1 | loop fusion | flops 1179648 | bytes 5898242 | tf_op jit(solution)/shard_map/jit(_where)/select_n | solution.py:338
  180.9 2.5 collective-permute-start.30
  183.4 6.8 %collective-permute-done.34 = f32[18,64,256]{2,1,0:T(8,128)} collective-permute-done((f32[18,64,256]{2,1,0:T(8,128)}, f32[18,64,256]{2,1,0:T(8,128)}, u32[]{:S(2)}, u32[]{:S(2)}) %collective-permute-start.34) | collective-permute-done | bytes 1179680 | tf_op jit(solution)/shard_map/ppermute | solution.py:231
  190.1 3.6 %add_select_fusion = f32[18,64,256]{2,1,0:T(8,128)} fusion(f32[18,64,256]{2,1,0:T(8,128)} %collective-permute-done.34, f32[18,64,256]{2,1,0:T(8,128)} %get-tuple-element.72, f32[18,64,256]{2,1,0:T(8,128)} %collective-permute-done.33, pred[]{:T(512)S(6)} %or.9, pred[]{:T(512)S(6)} %and.67, f32[18,64,256]{2,1,0:T(8,128)S(1)} %copy-done.4, ...), kind=kLoop, calls=%fused_computation | loop fusion | flops 1474560 | bytes 7077890 | tf_op jit(solution)/shard_map/jit(_where)/select_n | solution.py:338
  193.7 2.5 collective-permute-start.35
  196.2 13.4 %shard_map.96 = (f32[18,64,256]{2,1,0:T(8,128)}, f32[18,64,256]{2,1,0:T(8,128)}) custom-call(s32[1]{0:T(128)} %bitcast.3.info, s32[48]{0:T(128)} %compare_select_fusion.where.refs_1_, f32[12,256,1536]{2,1,0:T(8,128)} %bitcast.70, bf16[2,1536,256]{2,1,0:T(8,128)(2,1)} %get-tuple-element.61.refs_0_.refs_1_, ...), custom_call_target="tpu_custom_call" | custom-call | flops 14495514624 | bytes 4718592 | tf_op jit(solution)/shard_map/pallas_call | solution.py:162
  209.6 2.1 constant_dynamic-slice_fusion.3
  214.1 2.4 constant_dynamic-slice_fusion.2
  216.6 2.1 constant_dynamic-slice_fusion
  219.1 1.6 collective-permute-done.36.refs_7_
  221.5 5.2 %shard_map.98 = (f32[4,12,32,256]{3,2,1,0:T(8,128)}, f32[2,256,256]{2,1,0:T(8,128)}, f32[2,256,256]{2,1,0:T(8,128)}) custom-call(s32[3]{0:T(128)} %pad_add_fusion.refs_0_, s32[48]{0:T(128)} %compare_select_fusion.where.refs_1_, f32[2,12,32,256]{3,2,1,0:T(8,128)} %get-tuple-element.39.refs_5_.refs_2_, f32[2,12,32,256]{3,2,1,0:T(8,128)} %get-tuple-element.40.refs_3_, ...), custom_call_target="tpu_custom_call" | custom-call | flops 1207959552 | bytes 7864320 | tf_op jit(solution)/shard_map/pallas_call | solution.py:385
  227.1 1.7 collective-permute-done.37
  230.0 1.7 collective-permute-start.40
  233.6 3.8 %collective-permute-done.40 = f32[128,256]{1,0:T(8,128)S(1)} collective-permute-done((f32[128,256]{1,0:T(8,128)S(1)}, f32[128,256]{1,0:T(8,128)S(1)}, u32[]{:S(2)}, u32[]{:S(2)}) %collective-permute-start.40) | collective-permute-done | bytes 131104 | tf_op jit(solution)/shard_map/ppermute | solution.py:231
  237.4 2.2 collective-permute-done.39
  239.7 2.1 collective-permute-start.43
  243.6 3.2 %collective-permute-done.42 = f32[32,256]{1,0:T(8,128)S(1)} collective-permute-done((f32[32,256]{1,0:T(8,128)S(1)}, f32[32,256]{1,0:T(8,128)S(1)}, u32[]{:S(2)}, u32[]{:S(2)}) %collective-permute-start.42) | collective-permute-done | bytes 32800 | tf_op jit(solution)/shard_map/ppermute | solution.py:231
  246.8 1.2 collective-permute-done.41
  249.0 2.9 %collective-permute-start.46 = (f32[32,256]{1,0:T(8,128)S(1)}, f32[32,256]{1,0:T(8,128)S(1)}, u32[]{:S(2)}, u32[]{:S(2)}) collective-permute-start(f32[32,256]{1,0:T(8,128)S(1)} %get-tuple-element.77), channel_id=1, source_target_pairs={{0,6},{1,7},{2,0},{3,1},{4,2},{5,3},{6,4},{7,5},{8,14},{9,15},{10,... | collective-permute-start | bytes 98312 | tf_op jit(solution)/shard_map/ppermute | solution.py:231
  251.9 1.9 collective-permute-done.44
  255.2 1.3 collective-permute-start.48
  256.4 1.4 collective-permute-start.49
  257.9 1.4 collective-permute-done.47
  260.2 2.1 collective-permute-done.49
  262.4 1.9 collective-permute-done.50
  (161 shorter events, 35.8 us)
Async XLA Ops:
  1.9 2.4 collective-permute-start
  9.4 8.8 %collective-permute-start.1 = (f32[2,96,256]{2,1,0:T(8,128)}, f32[2,96,256]{2,1,0:T(8,128)S(1)}, u32[]{:S(2)}, u32[]{:S(2)}) collective-permute-start(f32[2,96,256]{2,1,0:T(8,128)} %get-tuple-element.42), channel_id=1, source_target_pairs={{0,8},{1,9},{2,10},{3,11},{4,12},{5,13},{6,14},{7,15},{8,0},{9,1},... | collective-permute-start | bytes 589832 | tf_op jit(solution)/shard_map/ppermute | solution.py:231
  12.3 11.1 %collective-permute-start.2 = (f32[2,96,256]{2,1,0:T(8,128)}, f32[2,96,256]{2,1,0:T(8,128)S(1)}, u32[]{:S(2)}, u32[]{:S(2)}) collective-permute-start(f32[2,96,256]{2,1,0:T(8,128)} %get-tuple-element.43), channel_id=1, source_target_pairs={{0,16},{1,17},{2,18},{3,19},{4,20},{5,21},{6,22},{7,23},{8,24},{9,... | collective-permute-start | bytes 589832 | tf_op jit(solution)/shard_map/ppermute | solution.py:231
  13.8 9.6 %collective-permute-start.3 = (f32[2,96,256]{2,1,0:T(8,128)}, f32[2,96,256]{2,1,0:T(8,128)S(1)}, u32[]{:S(2)}, u32[]{:S(2)}) collective-permute-start(f32[2,96,256]{2,1,0:T(8,128)} %get-tuple-element.44), channel_id=1, source_target_pairs={{0,24},{1,25},{2,26},{3,27},{4,28},{5,29},{6,30},{7,31},{8,16},{9,... | collective-permute-start | bytes 589832 | tf_op jit(solution)/shard_map/ppermute | solution.py:231
  18.2 5.2 %copy-start.23 = (f32[2,96,256]{2,1,0:T(8,128)}, f32[2,96,256]{2,1,0:T(8,128)S(1)}, u32[]{:S(2)}) copy-start(f32[2,96,256]{2,1,0:T(8,128)S(1)} %collective-permute-done.1.refs_2_) | copy-start | bytes 589828
  26.4 7.7 %collective-permute-start.7 = (f32[2,96,256]{2,1,0:T(8,128)}, f32[2,96,256]{2,1,0:T(8,128)S(1)}, u32[]{:S(2)}, u32[]{:S(2)}) collective-permute-start(f32[2,96,256]{2,1,0:T(8,128)} %get-tuple-element.54), channel_id=1, source_target_pairs={{0,8},{1,9},{2,10},{3,11},{4,12},{5,13},{6,14},{7,15},{8,0},{9,1},... | collective-permute-start | bytes 589832 | tf_op jit(solution)/shard_map/ppermute | solution.py:231
  27.6 14.6 %collective-permute-start.4 = (f32[2,96,256]{2,1,0:T(8,128)}, f32[2,96,256]{2,1,0:T(8,128)S(1)}, u32[]{:S(2)}, u32[]{:S(2)}) collective-permute-start(f32[2,96,256]{2,1,0:T(8,128)} %get-tuple-element.50), channel_id=1, source_target_pairs={{0,2},{1,3},{2,4},{3,5},{4,6},{5,7},{6,0},{7,1},{8,10},{9,11},{10,... | collective-permute-start | bytes 589832 | tf_op jit(solution)/shard_map/ppermute | solution.py:231
  29.1 10.0 %collective-permute-start.8 = (f32[2,96,256]{2,1,0:T(8,128)}, f32[2,96,256]{2,1,0:T(8,128)S(1)}, u32[]{:S(2)}, u32[]{:S(2)}) collective-permute-start(f32[2,96,256]{2,1,0:T(8,128)} %get-tuple-element.55), channel_id=1, source_target_pairs={{0,16},{1,17},{2,18},{3,19},{4,20},{5,21},{6,22},{7,23},{8,24},{9,... | collective-permute-start | bytes 589832 | tf_op jit(solution)/shard_map/ppermute | solution.py:231
  30.0 9.1 %collective-permute-start.9 = (f32[2,96,256]{2,1,0:T(8,128)}, f32[2,96,256]{2,1,0:T(8,128)S(1)}, u32[]{:S(2)}, u32[]{:S(2)}) collective-permute-start(f32[2,96,256]{2,1,0:T(8,128)} %get-tuple-element.56), channel_id=1, source_target_pairs={{0,24},{1,25},{2,26},{3,27},{4,28},{5,29},{6,30},{7,31},{8,16},{9,... | collective-permute-start | bytes 589832 | tf_op jit(solution)/shard_map/ppermute | solution.py:231
  31.5 12.6 %collective-permute-start.5 = (f32[2,96,256]{2,1,0:T(8,128)}, f32[2,96,256]{2,1,0:T(8,128)S(1)}, u32[]{:S(2)}, u32[]{:S(2)}) collective-permute-start(f32[2,96,256]{2,1,0:T(8,128)} %get-tuple-element.51), channel_id=1, source_target_pairs={{0,4},{1,5},{2,6},{3,7},{4,0},{5,1},{6,2},{7,3},{8,12},{9,13},{10,... | collective-permute-start | bytes 589832 | tf_op jit(solution)/shard_map/ppermute | solution.py:231
  34.0 5.1 %copy-start.18 = (f32[2,96,256]{2,1,0:T(8,128)}, f32[2,96,256]{2,1,0:T(8,128)S(1)}, u32[]{:S(2)}) copy-start(f32[2,96,256]{2,1,0:T(8,128)S(1)} %collective-permute-done.7.refs_2_) | copy-start | bytes 589828
  34.1 10.0 %collective-permute-start.6 = (f32[2,96,256]{2,1,0:T(8,128)}, f32[2,96,256]{2,1,0:T(8,128)S(1)}, u32[]{:S(2)}, u32[]{:S(2)}) collective-permute-start(f32[2,96,256]{2,1,0:T(8,128)} %get-tuple-element.52), channel_id=1, source_target_pairs={{0,6},{1,7},{2,0},{3,1},{4,2},{5,3},{6,4},{7,5},{8,14},{9,15},{10,... | collective-permute-start | bytes 589832 | tf_op jit(solution)/shard_map/ppermute | solution.py:231
  42.1 5.6 %copy-start.35 = (f32[2,96,256]{2,1,0:T(8,128)S(1)}, f32[2,96,256]{2,1,0:T(8,128)}, u32[]{:S(2)}) copy-start(f32[2,96,256]{2,1,0:T(8,128)} %get-tuple-element.58) | copy-start | bytes 589828
  42.1 10.0 %copy-start.34 = (f32[2,96,256]{2,1,0:T(8,128)S(1)}, f32[2,96,256]{2,1,0:T(8,128)}, u32[]{:S(2)}) copy-start(f32[2,96,256]{2,1,0:T(8,128)} %get-tuple-element.59) | copy-start | bytes 589828
  42.1 11.8 %copy-start.33 = (f32[2,96,256]{2,1,0:T(8,128)S(1)}, f32[2,96,256]{2,1,0:T(8,128)}, u32[]{:S(2)}) copy-start(f32[2,96,256]{2,1,0:T(8,128)} %get-tuple-element.60) | copy-start | bytes 589828
  46.9 19.6 %collective-permute-start.10 = (f32[2,4,96,256]{3,2,1,0:T(8,128)}, f32[2,4,96,256]{3,2,1,0:T(8,128)S(1)}, u32[]{:S(2)}, u32[]{:S(2)}) collective-permute-start(f32[2,4,96,256]{3,2,1,0:T(8,128)} %shard_map.90.refs_1_), channel_id=1, source_target_pairs={{0,8},{1,9},{2,10},{3,11},{4,12},{5,13},{6,14},{7,15},{8,0},{9,1},... | collective-permute-start | bytes 2359304 | tf_op jit(solution)/shard_map/ppermute | solution.py:231
  47.7 11.5 %collective-permute-start.14 = (f32[2,96,256]{2,1,0:T(8,128)S(1)}, f32[2,96,256]{2,1,0:T(8,128)S(1)}, u32[]{:S(2)}, u32[]{:S(2)}) collective-permute-start(f32[2,96,256]{2,1,0:T(8,128)S(1)} %copy-done.35), channel_id=1, source_target_pairs={{0,2},{1,3},{2,4},{3,5},{4,6},{5,7},{6,0},{7,1},{8,10},{9,11},{10,... | collective-permute-start | bytes 589832 | tf_op jit(solution)/shard_map/ppermute | solution.py:231
  52.1 13.7 %collective-permute-start.15 = (f32[2,96,256]{2,1,0:T(8,128)S(1)}, f32[2,96,256]{2,1,0:T(8,128)S(1)}, u32[]{:S(2)}, u32[]{:S(2)}) collective-permute-start(f32[2,96,256]{2,1,0:T(8,128)S(1)} %copy-done.34), channel_id=1, source_target_pairs={{0,4},{1,5},{2,6},{3,7},{4,0},{5,1},{6,2},{7,3},{8,12},{9,13},{10,... | collective-permute-start | bytes 589832 | tf_op jit(solution)/shard_map/ppermute | solution.py:231
  53.9 11.9 %collective-permute-start.16 = (f32[2,96,256]{2,1,0:T(8,128)S(1)}, f32[2,96,256]{2,1,0:T(8,128)S(1)}, u32[]{:S(2)}, u32[]{:S(2)}) collective-permute-start(f32[2,96,256]{2,1,0:T(8,128)S(1)} %copy-done.33), channel_id=1, source_target_pairs={{0,6},{1,7},{2,0},{3,1},{4,2},{5,3},{6,4},{7,5},{8,14},{9,15},{10,... | collective-permute-start | bytes 589832 | tf_op jit(solution)/shard_map/ppermute | solution.py:231
  54.6 19.2 %collective-permute-start.11 = (f32[2,4,96,256]{3,2,1,0:T(8,128)}, f32[2,4,96,256]{3,2,1,0:T(8,128)S(1)}, u32[]{:S(2)}, u32[]{:S(2)}) collective-permute-start(f32[2,4,96,256]{3,2,1,0:T(8,128)} %shard_map.90.refs_1_), channel_id=1, source_target_pairs={{0,16},{1,17},{2,18},{3,19},{4,20},{5,21},{6,22},{7,23},{8,24},{9,... | collective-permute-start | bytes 2359304 | tf_op jit(solution)/shard_map/ppermute | solution.py:231
  59.2 7.3 %copy-start.15 = (f32[2,96,256]{2,1,0:T(8,128)}, f32[2,96,256]{2,1,0:T(8,128)S(1)}, u32[]{:S(2)}) copy-start(f32[2,96,256]{2,1,0:T(8,128)S(1)} %collective-permute-done.14.refs_2_) | copy-start | bytes 589828
  69.6 20.6 %collective-permute-start.17 = (f32[2,4,96,256]{3,2,1,0:T(8,128)}, f32[2,4,96,256]{3,2,1,0:T(8,128)S(1)}, u32[]{:S(2)}, u32[]{:S(2)}) collective-permute-start(f32[2,4,96,256]{3,2,1,0:T(8,128)} %shard_map.91.refs_1_), channel_id=1, source_target_pairs={{0,8},{1,9},{2,10},{3,11},{4,12},{5,13},{6,14},{7,15},{8,0},{9,1},... | collective-permute-start | bytes 2359304 | tf_op jit(solution)/shard_map/ppermute | solution.py:231
  70.6 20.9 %collective-permute-start.18 = (f32[2,4,96,256]{3,2,1,0:T(8,128)}, f32[2,4,96,256]{3,2,1,0:T(8,128)S(1)}, u32[]{:S(2)}, u32[]{:S(2)}) collective-permute-start(f32[2,4,96,256]{3,2,1,0:T(8,128)} %shard_map.91.refs_1_), channel_id=1, source_target_pairs={{0,16},{1,17},{2,18},{3,19},{4,20},{5,21},{6,22},{7,23},{8,24},{9,... | collective-permute-start | bytes 2359304 | tf_op jit(solution)/shard_map/ppermute | solution.py:231
  72.7 20.6 %copy-start.27 = (s32[48]{0:T(128)S(1)}, s32[48]{0:T(128)}, u32[]{:S(2)}) copy-start(s32[48]{0:T(128)} %reshape.25.refs_1_) | copy-start | bytes 580
  72.7 27.0 %collective-permute-start.12 = (f32[1,4,96,256]{3,2,1,0:T(8,128)S(1)}, f32[1,4,96,256]{3,2,1,0:T(8,128)S(1)}, u32[]{:S(2)}, u32[]{:S(2)}) collective-permute-start(f32[1,4,96,256]{3,2,1,0:T(8,128)S(1)} %slice.16), channel_id=1, source_target_pairs={{0,16},{1,17},{2,18},{3,19},{4,20},{5,21},{6,22},{7,23},{8,24},{9,... | collective-permute-start | bytes 1179656 | tf_op jit(solution)/shard_map/ppermute | solution.py:231
  73.8 18.6 %copy-start.6 = (f32[2,4,96,256]{3,2,1,0:T(8,128)}, f32[2,4,96,256]{3,2,1,0:T(8,128)S(1)}, u32[]{:S(2)}) copy-start(f32[2,4,96,256]{3,2,1,0:T(8,128)S(1)} %collective-permute-done.11.refs_3_) | copy-start | bytes 2359300
  73.8 25.9 %collective-permute-start.13 = (f32[1,4,96,256]{3,2,1,0:T(8,128)S(1)}, f32[1,4,96,256]{3,2,1,0:T(8,128)S(1)}, u32[]{:S(2)}, u32[]{:S(2)}) collective-permute-start(f32[1,4,96,256]{3,2,1,0:T(8,128)S(1)} %slice.17), channel_id=1, source_target_pairs={{0,8},{1,9},{2,10},{3,11},{4,12},{5,13},{6,14},{7,15},{8,0},{9,1},... | collective-permute-start | bytes 1179656 | tf_op jit(solution)/shard_map/ppermute | solution.py:231
  90.2 9.5 %copy-start.1 = (f32[2,4,96,256]{3,2,1,0:T(8,128)}, f32[2,4,96,256]{3,2,1,0:T(8,128)S(1)}, u32[]{:S(2)}) copy-start(f32[2,4,96,256]{3,2,1,0:T(8,128)S(1)} %collective-permute-done.17.refs_6_.refs_2_) | copy-start | bytes 2359300
  90.3 16.9 %collective-permute-start.19 = (f32[1,4,96,256]{3,2,1,0:T(8,128)S(1)}, f32[1,4,96,256]{3,2,1,0:T(8,128)}, u32[]{:S(2)}, u32[]{:S(2)}) collective-permute-start(f32[1,4,96,256]{3,2,1,0:T(8,128)S(1)} %slice.18), channel_id=1, source_target_pairs={{0,16},{1,17},{2,18},{3,19},{4,20},{5,21},{6,22},{7,23},{8,24},{9,... | collective-permute-start | bytes 1179656 | tf_op jit(solution)/shard_map/ppermute | solution.py:231
  91.5 14.4 %copy-start.7 = (f32[2,4,96,256]{3,2,1,0:T(8,128)}, f32[2,4,96,256]{3,2,1,0:T(8,128)S(1)}, u32[]{:S(2)}) copy-start(f32[2,4,96,256]{3,2,1,0:T(8,128)S(1)} %collective-permute-done.18.refs_3_) | copy-start | bytes 2359300
  92.4 14.8 %collective-permute-start.20 = (f32[1,4,96,256]{3,2,1,0:T(8,128)}, f32[1,4,96,256]{3,2,1,0:T(8,128)}, u32[]{:S(2)}, u32[]{:S(2)}) collective-permute-start(f32[1,4,96,256]{3,2,1,0:T(8,128)} %slice.19), channel_id=1, source_target_pairs={{0,8},{1,9},{2,10},{3,11},{4,12},{5,13},{6,14},{7,15},{8,0},{9,1},... | collective-permute-start | bytes 1179656 | tf_op jit(solution)/shard_map/ppermute | solution.py:231
  125.0 3.8 %collective-permute-start.22 = (f32[18,64,256]{2,1,0:T(8,128)}, f32[18,64,256]{2,1,0:T(8,128)S(1)}, u32[]{:S(2)}, u32[]{:S(2)}) collective-permute-start(f32[18,64,256]{2,1,0:T(8,128)} %get-tuple-element.66), channel_id=1, source_target_pairs={{0,1},{1,0},{2,3},{3,2},{4,5},{5,4},{6,7},{7,6},{8,9},{9,8},{10,11... | collective-permute-start | bytes 3538952 | tf_op jit(solution)/shard_map/ppermute | solution.py:231
  125.1 23.2 %collective-permute-start.21 = (f32[18,64,256]{2,1,0:T(8,128)}, f32[18,64,256]{2,1,0:T(8,128)}, u32[]{:S(2)}, u32[]{:S(2)}) collective-permute-start(f32[18,64,256]{2,1,0:T(8,128)} %get-tuple-element.65), channel_id=1, source_target_pairs={{0,1},{1,0},{2,3},{3,2},{4,5},{5,4},{6,7},{7,6},{8,9},{9,8},{10,11... | collective-permute-start | bytes 3538952 | tf_op jit(solution)/shard_map/ppermute | solution.py:231
  130.2 4.4 %copy-start.2 = (f32[18,64,256]{2,1,0:T(8,128)}, f32[18,64,256]{2,1,0:T(8,128)S(1)}, u32[]{:S(2)}) copy-start(f32[18,64,256]{2,1,0:T(8,128)S(1)} %add.205.refs_8_) | copy-start | bytes 3538948
  130.2 20.8 %collective-permute-start.27 = (f32[18,64,256]{2,1,0:T(8,128)S(1)}, f32[18,64,256]{2,1,0:T(8,128)}, u32[]{:S(2)}, u32[]{:S(2)}) collective-permute-start(f32[18,64,256]{2,1,0:T(8,128)S(1)} %add.205.refs_8_), channel_id=1, source_target_pairs={{0,2},{1,0},{2,4},{3,1},{4,6},{5,3},{6,7},{7,5},{8,10},{9,8},{10,1... | collective-permute-start | bytes 3538952 | tf_op jit(solution)/shard_map/ppermute | solution.py:231
  134.6 13.7 %copy-start.8 = (f32[18,64,256]{2,1,0:T(8,128)S(1)}, f32[18,64,256]{2,1,0:T(8,128)}, u32[]{:S(2)}) copy-start(f32[18,64,256]{2,1,0:T(8,128)} %get-tuple-element.65) | copy-start | bytes 3538948
  148.1 3.3 %collective-permute-start.26 = (f32[18,64,256]{2,1,0:T(8,128)}, f32[18,64,256]{2,1,0:T(8,128)}, u32[]{:S(2)}, u32[]{:S(2)}) collective-permute-start(f32[18,64,256]{2,1,0:T(8,128)} %get-tuple-element.69), channel_id=1, source_target_pairs={{0,1},{1,0},{2,3},{3,2},{4,5},{5,4},{6,7},{7,6},{8,9},{9,8},{10,11... | collective-permute-start | bytes 3538952 | tf_op jit(solution)/shard_map/ppermute | solution.py:231
  149.9 19.1 %collective-permute-start.24 = (f32[18,64,256]{2,1,0:T(8,128)S(1)}, f32[18,64,256]{2,1,0:T(8,128)S(1)}, u32[]{:S(2)}, u32[]{:S(2)}) collective-permute-start(f32[18,64,256]{2,1,0:T(8,128)S(1)} %add.201), channel_id=1, source_target_pairs={{0,2},{1,0},{2,4},{3,1},{4,6},{5,3},{6,7},{7,5},{8,10},{9,8},{10,1... | collective-permute-start | bytes 3538952 | tf_op jit(solution)/shard_map/ppermute | solution.py:231
  151.0 18.0 %collective-permute-start.23 = (f32[18,64,256]{2,1,0:T(8,128)S(1)}, f32[18,64,256]{2,1,0:T(8,128)S(1)}, u32[]{:S(2)}, u32[]{:S(2)}) collective-permute-start(f32[18,64,256]{2,1,0:T(8,128)S(1)} %copy-done.4), channel_id=1, source_target_pairs={{0,1},{1,0},{2,3},{3,2},{4,5},{5,4},{6,7},{7,6},{8,9},{9,8},{10,11... | collective-permute-start | bytes 3538952 | tf_op jit(solution)/shard_map/ppermute | solution.py:231
  154.6 22.9 %collective-permute-start.29 = (f32[18,64,256]{2,1,0:T(8,128)}, f32[18,64,256]{2,1,0:T(8,128)}, u32[]{:S(2)}, u32[]{:S(2)}) collective-permute-start(f32[18,64,256]{2,1,0:T(8,128)} %get-tuple-element.78.refs_8_), channel_id=1, source_target_pairs={{0,2},{1,0},{2,4},{3,1},{4,6},{5,3},{6,7},{7,5},{8,10},{9,8},{10,1... | collective-permute-start | bytes 3538952 | tf_op jit(solution)/shard_map/ppermute | solution.py:231
  168.9 8.6 %collective-permute-start.28 = (f32[18,64,256]{2,1,0:T(8,128)}, f32[18,64,256]{2,1,0:T(8,128)}, u32[]{:S(2)}, u32[]{:S(2)}) collective-permute-start(f32[18,64,256]{2,1,0:T(8,128)} %get-tuple-element.70), channel_id=1, source_target_pairs={{0,1},{1,0},{2,3},{3,2},{4,5},{5,4},{6,7},{7,6},{8,9},{9,8},{10,11... | collective-permute-start | bytes 3538952 | tf_op jit(solution)/shard_map/ppermute | solution.py:231
  170.5 19.7 %collective-permute-start.34 = (f32[18,64,256]{2,1,0:T(8,128)}, f32[18,64,256]{2,1,0:T(8,128)}, u32[]{:S(2)}, u32[]{:S(2)}) collective-permute-start(f32[18,64,256]{2,1,0:T(8,128)} %add_select_fusion.3.refs_8_), channel_id=1, source_target_pairs={{0,2},{1,0},{2,4},{3,1},{4,6},{5,3},{6,7},{7,5},{8,10},{9,8},{10,1... | collective-permute-start | bytes 3538952 | tf_op jit(solution)/shard_map/ppermute | solution.py:231
  171.6 18.5 %collective-permute-start.33 = (f32[18,64,256]{2,1,0:T(8,128)}, f32[18,64,256]{2,1,0:T(8,128)}, u32[]{:S(2)}, u32[]{:S(2)}) collective-permute-start(f32[18,64,256]{2,1,0:T(8,128)} %get-tuple-element.72), channel_id=1, source_target_pairs={{0,1},{1,0},{2,3},{3,2},{4,5},{5,4},{6,7},{7,6},{8,9},{9,8},{10,11... | collective-permute-start | bytes 3538952 | tf_op jit(solution)/shard_map/ppermute | solution.py:231
  180.9 33.2 %collective-permute-start.30 = (f32[18,64,256]{2,1,0:T(8,128)}, f32[18,64,256]{2,1,0:T(8,128)}, u32[]{:S(2)}, u32[]{:S(2)}) collective-permute-start(f32[18,64,256]{2,1,0:T(8,128)} %add_select_fusion.1), channel_id=1, source_target_pairs={{0,2},{1,0},{2,4},{3,1},{4,6},{5,3},{6,7},{7,5},{8,10},{9,8},{10,1... | collective-permute-start | bytes 3538952 | tf_op jit(solution)/shard_map/ppermute | solution.py:231
  193.7 22.9 %collective-permute-start.35 = (f32[18,64,256]{2,1,0:T(8,128)}, f32[18,64,256]{2,1,0:T(8,128)S(1)}, u32[]{:S(2)}, u32[]{:S(2)}) collective-permute-start(f32[18,64,256]{2,1,0:T(8,128)} %add_select_fusion), channel_id=1, source_target_pairs={{0,2},{1,0},{2,4},{3,1},{4,6},{5,3},{6,7},{7,5},{8,10},{9,8},{10,1... | collective-permute-start | bytes 3538952 | tf_op jit(solution)/shard_map/ppermute | solution.py:231
  209.6 4.5 %copy-start.10 = (f32[18,64,256]{2,1,0:T(8,128)S(1)}, f32[18,64,256]{2,1,0:T(8,128)}, u32[]{:S(2)}) copy-start(f32[18,64,256]{2,1,0:T(8,128)} %get-tuple-element.68) | copy-start | bytes 3538948
  211.7 2.3 collective-permute-start.25
  212.6 4.0 %collective-permute-start.32 = (f32[18,32,256]{2,1,0:T(8,128)}, f32[18,32,256]{2,1,0:T(8,128)}, u32[]{:S(2)}, u32[]{:S(2)}) collective-permute-start(f32[18,32,256]{2,1,0:T(8,128)} %constant_dynamic-slice_fusion.1), channel_id=1, source_target_pairs={{0,1},{1,0},{2,3},{3,2},{4,5},{5,4},{6,7},{7,6},{8,9},{9,8},{10,11... | collective-permute-start | bytes 1769480 | tf_op jit(solution)/shard_map/ppermute | solution.py:231
  216.5 2.6 collective-permute-start.31
  218.7 2.0 collective-permute-start.36
  226.8 2.1 collective-permute-start.37
  230.0 7.3 %collective-permute-start.40 = (f32[128,256]{1,0:T(8,128)S(1)}, f32[128,256]{1,0:T(8,128)S(1)}, u32[]{:S(2)}, u32[]{:S(2)}) collective-permute-start(f32[128,256]{1,0:T(8,128)S(1)} %get-tuple-element.87), channel_id=1, source_target_pairs={{0,24},{1,25},{2,26},{3,27},{4,28},{5,29},{6,30},{7,31},{8,16},{9,... | collective-permute-start | bytes 393224 | tf_op jit(solution)/shard_map/ppermute | solution.py:231
  231.7 7.9 %collective-permute-start.39 = (f32[128,256]{1,0:T(8,128)S(1)}, f32[128,256]{1,0:T(8,128)S(1)}, u32[]{:S(2)}, u32[]{:S(2)}) collective-permute-start(f32[128,256]{1,0:T(8,128)S(1)} %get-tuple-element.88), channel_id=1, source_target_pairs={{0,16},{1,17},{2,18},{3,19},{4,20},{5,21},{6,22},{7,23},{8,24},{9,... | collective-permute-start | bytes 393224 | tf_op jit(solution)/shard_map/ppermute | solution.py:231
  232.6 7.0 %collective-permute-start.38 = (f32[128,256]{1,0:T(8,128)S(1)}, f32[128,256]{1,0:T(8,128)S(1)}, u32[]{:S(2)}, u32[]{:S(2)}) collective-permute-start(f32[128,256]{1,0:T(8,128)S(1)} %get-tuple-element.86), channel_id=1, source_target_pairs={{0,8},{1,9},{2,10},{3,11},{4,12},{5,13},{6,14},{7,15},{8,0},{9,1},... | collective-permute-start | bytes 393224 | tf_op jit(solution)/shard_map/ppermute | solution.py:231
  239.7 4.0 %collective-permute-start.43 = (f32[32,256]{1,0:T(8,128)S(1)}, f32[32,256]{1,0:T(8,128)S(1)}, u32[]{:S(2)}, u32[]{:S(2)}) collective-permute-start(f32[32,256]{1,0:T(8,128)S(1)} %get-tuple-element.90), channel_id=1, source_target_pairs={{0,6},{1,7},{2,0},{3,1},{4,2},{5,3},{6,4},{7,5},{8,14},{9,15},{10,... | collective-permute-start | bytes 98312 | tf_op jit(solution)/shard_map/ppermute | solution.py:231
  241.7 5.1 %collective-permute-start.42 = (f32[32,256]{1,0:T(8,128)S(1)}, f32[32,256]{1,0:T(8,128)S(1)}, u32[]{:S(2)}, u32[]{:S(2)}) collective-permute-start(f32[32,256]{1,0:T(8,128)S(1)} %get-tuple-element.91), channel_id=1, source_target_pairs={{0,4},{1,5},{2,6},{3,7},{4,0},{5,1},{6,2},{7,3},{8,12},{9,13},{10,... | collective-permute-start | bytes 98312 | tf_op jit(solution)/shard_map/ppermute | solution.py:231
  242.3 5.7 %collective-permute-start.41 = (f32[32,256]{1,0:T(8,128)S(1)}, f32[32,256]{1,0:T(8,128)S(1)}, u32[]{:S(2)}, u32[]{:S(2)}) collective-permute-start(f32[32,256]{1,0:T(8,128)S(1)} %get-tuple-element.89), channel_id=1, source_target_pairs={{0,2},{1,3},{2,4},{3,5},{4,6},{5,7},{6,0},{7,1},{8,10},{9,11},{10,... | collective-permute-start | bytes 98312 | tf_op jit(solution)/shard_map/ppermute | solution.py:231
  248.0 5.8 %collective-permute-start.44 = (f32[32,256]{1,0:T(8,128)S(1)}, f32[32,256]{1,0:T(8,128)S(1)}, u32[]{:S(2)}, u32[]{:S(2)}) collective-permute-start(f32[32,256]{1,0:T(8,128)S(1)} %get-tuple-element.77), channel_id=1, source_target_pairs={{0,2},{1,3},{2,4},{3,5},{4,6},{5,7},{6,0},{7,1},{8,10},{9,11},{10,... | collective-permute-start | bytes 98312 | tf_op jit(solution)/shard_map/ppermute | solution.py:231
  248.2 5.6 %collective-permute-start.45 = (f32[32,256]{1,0:T(8,128)S(1)}, f32[32,256]{1,0:T(8,128)S(1)}, u32[]{:S(2)}, u32[]{:S(2)}) collective-permute-start(f32[32,256]{1,0:T(8,128)S(1)} %get-tuple-element.77), channel_id=1, source_target_pairs={{0,4},{1,5},{2,6},{3,7},{4,0},{5,1},{6,2},{7,3},{8,12},{9,13},{10,... | collective-permute-start | bytes 98312 | tf_op jit(solution)/shard_map/ppermute | solution.py:231
  249.0 5.3 %collective-permute-start.46 = (f32[32,256]{1,0:T(8,128)S(1)}, f32[32,256]{1,0:T(8,128)S(1)}, u32[]{:S(2)}, u32[]{:S(2)}) collective-permute-start(f32[32,256]{1,0:T(8,128)S(1)} %get-tuple-element.77), channel_id=1, source_target_pairs={{0,6},{1,7},{2,0},{3,1},{4,2},{5,3},{6,4},{7,5},{8,14},{9,15},{10,... | collective-permute-start | bytes 98312 | tf_op jit(solution)/shard_map/ppermute | solution.py:231
  254.4 5.0 %collective-permute-start.47 = (f32[128,256]{1,0:T(8,128)S(1)}, f32[128,256]{1,0:T(8,128)S(1)}, u32[]{:S(2)}, u32[]{:S(2)}) collective-permute-start(f32[128,256]{1,0:T(8,128)S(1)} %bitcast.61), channel_id=1, source_target_pairs={{0,8},{1,9},{2,10},{3,11},{4,12},{5,13},{6,14},{7,15},{8,0},{9,1},... | collective-permute-start | bytes 393224 | tf_op jit(solution)/shard_map/ppermute | solution.py:231
  255.2 5.0 %collective-permute-start.48 = (f32[128,256]{1,0:T(8,128)S(1)}, f32[128,256]{1,0:T(8,128)S(1)}, u32[]{:S(2)}, u32[]{:S(2)}) collective-permute-start(f32[128,256]{1,0:T(8,128)S(1)} %bitcast.62), channel_id=1, source_target_pairs={{0,16},{1,17},{2,18},{3,19},{4,20},{5,21},{6,22},{7,23},{8,24},{9,... | collective-permute-start | bytes 393224 | tf_op jit(solution)/shard_map/ppermute | solution.py:231
  256.4 5.9 %collective-permute-start.49 = (f32[128,256]{1,0:T(8,128)S(1)}, f32[128,256]{1,0:T(8,128)S(1)}, u32[]{:S(2)}, u32[]{:S(2)}) collective-permute-start(f32[128,256]{1,0:T(8,128)S(1)} %bitcast.63), channel_id=1, source_target_pairs={{0,24},{1,25},{2,26},{3,27},{4,28},{5,29},{6,30},{7,31},{8,16},{9,... | collective-permute-start | bytes 393224 | tf_op jit(solution)/shard_map/ppermute | solution.py:231
  262.3 2.0 collective-permute-start.50
  (23 other events, 34.3 us)
